TPU v7x, 1024 devices: a whole 8x8x8 slice. The times are simulated.
1024 devices in a mesh: dp: 4 (over x_hi), expert: 64 (over z, y), tensor: 4 (over x_lo, core).
Axes of the slice: x: 8 (x_hi: 4, x_lo: 2; x = x_hi * 2 + x_lo), y: 8, z: 8, core: 2. Of those that a mesh axis runs over, the one named last changes fastest.
Arguments:
- grad_out: bfloat16 [40960, 5120], P(('dp', 'expert'), 'tensor'), may hold values from -6 to 6
- expert_ids: int32 [40960, 6], P(('dp', 'expert')), may hold values from 0 to 159, all different within a row
- route_probs: float32 [40960, 6], P(('dp', 'expert')), may hold values from 0.05 to 0.6
- saved_gate: bfloat16 [4, 64, 512, 768], P('dp', 'expert'), may hold values from -0.25 to 2
- w_up: bfloat16 [64, 5120, 768], P('expert', 'tensor'), may hold values from -0.078125 to 0.078125
- w_down: bfloat16 [64, 768, 5120], P('expert', None, 'tensor'), may hold values from -0.21875 to 0.21875
- shared_gate: bfloat16 [40960, 768], P(('dp', 'expert')), may hold values from -0.25 to 2
- shared_up: bfloat16 [5120, 768], P('tensor'), may hold values from -0.078125 to 0.078125
- shared_down: bfloat16 [768, 5120], P(None, 'tensor'), may hold values from -0.21875 to 0.21875
Outputs:
- moe_grad: bfloat16 [40960, 5120], P(('dp', 'expert'), 'tensor')
- shared_grad: bfloat16 [40960, 5120], P(('dp', 'expert'), 'tensor')
All inputs are finite; a program needn't handle non-finite values.
Results may differ from a plain program's by a relative error of at most 0.0063.
Values may be sent and summed in bfloat16 or wider, within the bound.
No kernel may reach another device: no remote copies, remote signals or barrier semaphores. Data moves between devices by JAX's collectives and lax.ppermute only.
A program may use at most 32 MiB of HBM per device.

v0:
```python
import jax
import jax.numpy as jnp
from jax import lax
from jax.sharding import PartitionSpec as P

TOP = 6
CAP = 8


def on_device(
    grad_out, expert_ids, route_probs, saved_gate, w_up, w_down, shared_gate, shared_up, shared_down
):
    experts = lax.axis_size("expert")
    tok_rows = grad_out.shape[0]
    quarter = grad_out.shape[1]
    flat = expert_ids.reshape(-1)
    onehot = (flat[:, None] == jnp.arange(experts, dtype=jnp.int32)[None, :]).astype(jnp.int32)
    ranks = jnp.sum((jnp.cumsum(onehot, axis=0) - 1) * onehot, axis=1)
    kept = (flat < experts) & (ranks < CAP)
    dests = jnp.where(kept, flat * CAP + ranks, -1)
    pick_slot = dests[:, None] == jnp.arange(experts * CAP, dtype=jnp.int32)[None, :]
    pick_slot = pick_slot.reshape(tok_rows, TOP, experts * CAP)
    slot_token = jnp.any(pick_slot, axis=1).astype(jnp.bfloat16)
    slot_prob = jnp.sum(jnp.where(pick_slot, route_probs[:, :, None], 0.0), axis=(0, 1))
    picked = lax.dot_general(
        slot_token, grad_out, (((0,), (0,)), ((), ())), preferred_element_type=jnp.float32
    )
    sent = (picked * slot_prob[:, None]).astype(jnp.bfloat16).reshape(experts, CAP, quarter)
    arrived = lax.all_to_all(sent, "expert", split_axis=0, concat_axis=0, tiled=True).reshape(
        experts * CAP, quarter
    )
    dense_part = lax.dot_general(
        grad_out, shared_down, (((1,), (1,)), ((), ())), preferred_element_type=jnp.float32
    )
    dense_hidden = lax.psum(dense_part, "tensor")
    dense_up = (dense_hidden * shared_gate.astype(jnp.float32)).astype(jnp.bfloat16)
    shared_grad = lax.dot_general(
        dense_up, shared_up, (((1,), (1,)), ((), ())), preferred_element_type=jnp.float32
    ).astype(jnp.bfloat16)
    partial_hidden = lax.dot_general(
        arrived, w_down[0], (((1,), (1,)), ((), ())), preferred_element_type=jnp.float32
    )
    gate_rows = saved_gate[0, 0]
    hidden = lax.psum(partial_hidden, "tensor")
    up_grad = (hidden * gate_rows.astype(jnp.float32)).astype(jnp.bfloat16)
    slot_grad = lax.dot_general(
        up_grad, w_up[0], (((1,), (1,)), ((), ())), preferred_element_type=jnp.float32
    )
    slot_grad = slot_grad.astype(jnp.bfloat16).reshape(experts, CAP, quarter)
    back = lax.all_to_all(slot_grad, "expert", split_axis=0, concat_axis=0, tiled=True).reshape(
        experts * CAP, quarter
    )
    moe_grad = jnp.dot(slot_token, back, preferred_element_type=jnp.float32).astype(jnp.bfloat16)
    return (moe_grad, shared_grad)


def solution(mesh):
    placed = (
        P(("dp", "expert"), "tensor"),
        P(("dp", "expert"), None),
        P(("dp", "expert"), None),
        P("dp", "expert", None, None),
        P("expert", "tensor", None),
        P("expert", None, "tensor"),
        P(("dp", "expert"), None),
        P("tensor", None),
        P(None, "tensor"),
    )
    return jax.shard_map(
        on_device,
        mesh=mesh,
        in_specs=placed,
        out_specs=(P(("dp", "expert"), "tensor"), P(("dp", "expert"), "tensor")),
        check_vma=False,
    )
```

profile of v0, /device:TPU:1, one launch (start us, length us, event | category | flops | bytes accessed | tf_op | source)
XLA Modules:
  0.0 220.9 jit_solution(17288739674094682772)
XLA Ops:
  7.2 0.0 copy-start
  7.2 0.9 copy.29
  8.1 0.0 copy-start.2
  8.1 0.1 eq.36
  8.3 0.0 copy-start.3
  8.3 0.0 copy-start.1
  8.4 18.0 %reduce-window.6 = s32[64,8,128]{2,1,0:T(8,128)S(1)} reduce-window(s32[64,8,128]{2,1,0:T(8,128)S(1)} %bitcast.39, s32[]{:T(128)} %constant.5.clone.1), window={size=1x1x128 pad=0_0x0_0x127_0}, to_apply=%region_0.0 | reduce-window | flops 8323072 | bytes 524292 | tf_op jit(solution)/shard_map/reduce-window
  26.4 0.1 slice.12
  26.6 0.1 copy.30
  26.8 0.1 copy.31
  26.8 0.1 broadcast_add_fusion
  27.1 0.1 fusion.13
  27.1 0.1 reduce_sum.21
  27.2 0.1 copy.32
  27.3 0.0 copy-done.2
  27.3 0.3 fusion.6
  27.6 0.0 copy-done.3
  27.7 0.3 select_reduce_fusion
  28.0 1.7 fusion.2
  29.7 24.2 %all-to-all-start = ((bf16[64,8,1280]{2,1,0:T(8,128)(2,1)}), bf16[64,8,1280]{2,1,0:T(8,128)(2,1)}, u32[]{:S(2)}, u32[]{:S(2)}) async-start(bf16[64,8,1280]{2,1,0:T(8,128)(2,1)} %fusion.2), calls=%async_computation | async-start | bytes 2621440 | tf_op jit(solution)/shard_map/all_to_all | solution.py:29
  53.9 0.0 all-reduce.4.cloned.1.call-start
  54.0 3.1 %fusion.14 = f32[160,768]{1,0:T(8,128)} fusion(bf16[160,1280]{1,0:T(8,128)(2,1)S(1)} %copy-done.1, bf16[768,1280]{1,0:T(8,128)(2,1)} %param.17), kind=kOutput, calls=%fused_computation.28 | convolution fusion | flops 314572800 | bytes 2867200 | tf_op jit(solution)/shard_map/dot_general | solution.py:32
  57.1 29.9 %all-to-all-done = bf16[64,8,1280]{2,1,0:T(8,128)(2,1)} async-done(((bf16[64,8,1280]{2,1,0:T(8,128)(2,1)}), bf16[64,8,1280]{2,1,0:T(8,128)(2,1)}, u32[]{:S(2)}, u32[]{:S(2)}) %all-to-all-start) | async-done | bytes 1310752 | tf_op jit(solution)/shard_map/all_to_all | solution.py:29
  87.0 4.3 %fusion.4 = f32[512,768]{1,0:T(8,128)} fusion(bf16[1,768,1280]{2,1,0:T(8,128)(2,1)} %param.14, bf16[64,8,1280]{2,1,0:T(8,128)(2,1)} %all-to-all-done), kind=kOutput, calls=%fused_computation.8 | convolution fusion | flops 1006632960 | bytes 4849664 | tf_op jit(solution)/shard_map/dot_general | solution.py:40
  91.3 0.0 all-reduce.4.cloned.1.call-update
  91.3 70.8 %all-reduce.4.cloned.1.call-done = (f32[512,768]{1,0:T(8,128)}, f32[160,768]{1,0:T(8,128)}) async-done(((f32[512,768]{1,0:T(8,128)}, f32[160,768]{1,0:T(8,128)}), (f32[512,768]{1,0:T(8,128)}, f32[160,768]{1,0:T(8,128)})) %all-reduce.4.cloned.1.call-update) | async-done | bytes 2064400 | tf_op jit(solution)/shard_map/psum | solution.py:44
  162.1 0.0 copy-done.4
  162.1 3.7 %fusion.1 = bf16[64,8,1280]{2,1,0:T(8,128)(2,1)} fusion(bf16[1,1280,768]{2,1,0:T(8,128)(2,1)S(1)} %copy-done, f32[512,768]{1,0:T(8,128)} %get-tuple-element.2, bf16[1,1,512,768]{3,2,1,0:T(8,128)(2,1)S(1)} %copy-done.4), kind=kOutput, calls=%fused_computation.3 | convolution fusion | flops 1008467968 | bytes 5636096 | tf_op jit(solution)/shard_map/dot_general | solution.py:46
  165.8 13.8 %all-to-all-start.1 = ((bf16[64,8,1280]{2,1,0:T(8,128)(2,1)}), bf16[64,8,1280]{2,1,0:T(8,128)(2,1)S(1)}, u32[]{:S(2)}, u32[]{:S(2)}) async-start(bf16[64,8,1280]{2,1,0:T(8,128)(2,1)} %fusion.1), calls=%async_computation.1 | async-start | bytes 2621440 | tf_op jit(solution)/shard_map/all_to_all | solution.py:50
  179.7 3.4 %convolution_convert_fusion.1 = bf16[160,1280]{1,0:T(8,128)(2,1)} fusion(bf16[1280,768]{1,0:T(8,128)(2,1)} %param.16, f32[160,768]{1,0:T(8,128)} %get-tuple-element.3, bf16[160,768]{1,0:T(8,128)(2,1)} %param.15), kind=kOutput, calls=%fused_computation.5 | convolution fusion | flops 315146240 | bytes 3112960 | tf_op jit(solution)/shard_map/dot_general | solution.py:37
  183.1 29.8 %all-to-all-done.1 = bf16[64,8,1280]{2,1,0:T(8,128)(2,1)S(1)} async-done(((bf16[64,8,1280]{2,1,0:T(8,128)(2,1)}), bf16[64,8,1280]{2,1,0:T(8,128)(2,1)S(1)}, u32[]{:S(2)}, u32[]{:S(2)}) %all-to-all-start.1) | async-done | bytes 1310752 | tf_op jit(solution)/shard_map/all_to_all | solution.py:50
  212.9 1.1 convolution_convert_fusion.2
  (10 shorter events, 0.2 us)
Async XLA Ops:
  7.2 155.0 %copy-start = (bf16[1,1280,768]{2,1,0:T(8,128)(2,1)S(1)}, bf16[1,1280,768]{2,1,0:T(8,128)(2,1)}, u32[]{:S(2)}) copy-start(bf16[1,1280,768]{2,1,0:T(8,128)(2,1)} %param.13) | copy-start | bytes 5898244
  8.1 19.2 %copy-start.2 = (s32[160,6]{0,1:T(8,128)S(1)}, s32[160,6]{0,1:T(8,128)}, u32[]{:S(2)}) copy-start(s32[160,6]{0,1:T(8,128)} %param.10) | copy-start | bytes 11524
  8.3 19.4 %copy-start.3 = (f32[160,6]{0,1:T(8,128)S(1)}, f32[160,6]{0,1:T(8,128)}, u32[]{:S(2)}) copy-start(f32[160,6]{0,1:T(8,128)} %param.11) | copy-start | bytes 11524
  8.3 19.7 %copy-start.1 = (bf16[160,1280]{1,0:T(8,128)(2,1)S(1)}, bf16[160,1280]{1,0:T(8,128)(2,1)}, u32[]{:S(2)}) copy-start(bf16[160,1280]{1,0:T(8,128)(2,1)} %param.9) | copy-start | bytes 1228804
  29.7 57.3 %all-to-all-start = ((bf16[64,8,1280]{2,1,0:T(8,128)(2,1)}), bf16[64,8,1280]{2,1,0:T(8,128)(2,1)}, u32[]{:S(2)}, u32[]{:S(2)}) async-start(bf16[64,8,1280]{2,1,0:T(8,128)(2,1)} %fusion.2), calls=%async_computation | async-start | bytes 2621440 | tf_op jit(solution)/shard_map/all_to_all | solution.py:29
  53.9 108.2 %all-reduce.4.cloned.1.call-start = ((), (), s32[]{:S(2)}) async-start(), calls=%async_computation.2 | async-start | bytes 4128768 | tf_op jit(solution)/shard_map/psum | solution.py:44
  91.3 70.8 %copy-start.4 = (bf16[1,1,512,768]{3,2,1,0:T(8,128)(2,1)S(1)}, bf16[1,1,512,768]{3,2,1,0:T(8,128)(2,1)}, u32[]{:S(2)}) copy-start(bf16[1,1,512,768]{3,2,1,0:T(8,128)(2,1)} %param.12) | copy-start | bytes 2359300
  165.8 47.0 %all-to-all-start.1 = ((bf16[64,8,1280]{2,1,0:T(8,128)(2,1)}), bf16[64,8,1280]{2,1,0:T(8,128)(2,1)S(1)}, u32[]{:S(2)}, u32[]{:S(2)}) async-start(bf16[64,8,1280]{2,1,0:T(8,128)(2,1)} %fusion.1), calls=%async_computation.1 | async-start | bytes 2621440 | tf_op jit(solution)/shard_map/all_to_all | solution.py:50
Sparse Core Ops, SparseCore 0:
  91.4 70.6 all-reduce.3
where the time goes:
time: 223 us; the launch traced here: 221 us
  waiting for transfers between devices  130 us (58%)
  starting transfers between devices  38 us (17%)
  other arithmetic  18.9 us (8%)
  matrix products  17.4 us (8%)
  between operations  14.2 us (6%)
    psum x1, waiting for transfers between devices, on_device(): hidden = lax.psum(partial_hidden, 'tensor')  70.8 us
    all_to_all x1, waiting for transfers between devices, on_device(): lax.all_to_all(sent, 'expert', split_axis=0, concat_axis=0, tiled=True)  29.9 us
    all_to_all x1, waiting for transfers between devices, on_device(): lax.all_to_all(slot_grad, 'expert', split_axis=0, concat_axis=0, tiled=True)  29.8 us
    all_to_all x1, starting transfers between devices, on_device(): lax.all_to_all(sent, 'expert', split_axis=0, concat_axis=0, tiled=True)  24.2 us
    another operation x3, other arithmetic  18.2 us
    all_to_all x1, starting transfers between devices, on_device(): lax.all_to_all(slot_grad, 'expert', split_axis=0, concat_axis=0, tiled=True)  13.8 us
  transfers between devices with their start and end apart: 3, of which 3 were waited for; matrix products, arithmetic and copies ran while one was open for 3% of the time, Pallas kernels for 0%

commit v1 on v0

v1 whole, which is shorter than its diff:
```python
import jax
import jax.numpy as jnp
from jax import lax
from jax.sharding import PartitionSpec as P

TOP = 6
CAP = 8
CORE_SWAP = [(0, 1), (1, 0), (2, 3), (3, 2)]
CHIP_SWAP = [(0, 2), (1, 3), (2, 0), (3, 1)]


def dot(a, b, dims):
    return lax.dot_general(a, b, (dims, ((), ())), preferred_element_type=jnp.float32)


def pair_sum(part):
    core = lax.axis_index("tensor") % 2
    half = part.shape[0] // 2
    mine = lax.dynamic_slice_in_dim(part, core * half, half)
    other = lax.dynamic_slice_in_dim(part, (1 - core) * half, half)
    chip = mine + lax.ppermute(other, "tensor", CORE_SWAP)
    away = lax.ppermute(chip.astype(jnp.bfloat16), "tensor", CHIP_SWAP)
    return chip + away.astype(jnp.float32)


def both_halves(rows):
    core = lax.axis_index("tensor") % 2
    other = lax.ppermute(rows, "tensor", CORE_SWAP)
    low = jnp.where(core == 0, rows, other)
    high = jnp.where(core == 0, other, rows)
    return jnp.concatenate([low, high], axis=0)


def gated(part, gate):
    core = lax.axis_index("tensor") % 2
    half = part.shape[0] // 2
    mine = lax.dynamic_slice_in_dim(gate, core * half, half)
    up = (pair_sum(part) * mine.astype(jnp.float32)).astype(jnp.bfloat16)
    return both_halves(up)


def on_device(
    grad_out, expert_ids, route_probs, saved_gate, w_up, w_down, shared_gate, shared_up, shared_down
):
    experts = lax.axis_size("expert")
    tok_rows, quarter = grad_out.shape
    parts = 2
    cap = CAP // parts
    picks = expert_ids[:, :, None] == jnp.arange(experts, dtype=jnp.int32)[None, None, :]
    named = jnp.any(picks, axis=1)
    prob = jnp.sum(jnp.where(picks, route_probs[:, :, None], 0.0), axis=1)
    earlier = jnp.arange(tok_rows)[None, :] < jnp.arange(tok_rows)[:, None]
    rank = dot(earlier.astype(jnp.bfloat16), named.astype(jnp.bfloat16), ((1,), (0,)))
    rank = jnp.where(named, rank.astype(jnp.int32), CAP)

    masks, arrived = [], []
    for part in range(parts):
        slots = part * cap + jnp.arange(cap, dtype=jnp.int32)
        mask = rank[:, :, None] == slots[None, None, :]
        slot_prob = jnp.sum(jnp.where(mask, prob[:, :, None], 0.0), axis=0).reshape(experts * cap)
        mask = mask.reshape(tok_rows, experts * cap).astype(jnp.bfloat16)
        picked = dot(mask, grad_out, ((0,), (0,)))
        sent = (picked * slot_prob[:, None]).astype(jnp.bfloat16)
        masks.append(mask)
        arrived.append(
            lax.all_to_all(
                sent.reshape(experts, cap, quarter), "expert", split_axis=0, concat_axis=0, tiled=True
            )
        )
    dense_up = gated(dot(grad_out, shared_down, ((1,), (1,))), shared_gate)
    shared_grad = dot(dense_up, shared_up, ((1,), (1,))).astype(jnp.bfloat16)

    gate = saved_gate[0, 0].reshape(experts, CAP, -1)
    total = None
    for part in range(parts):
        rows = arrived[part].reshape(experts * cap, quarter)
        hidden = dot(rows, w_down[0], ((1,), (1,)))
        gate_rows = gate[:, part * cap : (part + 1) * cap].reshape(experts * cap, -1)
        up_grad = gated(hidden, gate_rows)
        slot_grad = dot(up_grad, w_up[0], ((1,), (1,))).astype(jnp.bfloat16)
        back = lax.all_to_all(
            slot_grad.reshape(experts, cap, quarter), "expert", split_axis=0, concat_axis=0, tiled=True
        )
        term = dot(masks[part], back.reshape(experts * cap, quarter), ((1,), (0,)))
        total = term if total is None else total + term
    return (total.astype(jnp.bfloat16), shared_grad)


def solution(mesh):
    placed = (
        P(("dp", "expert"), "tensor"),
        P(("dp", "expert"), None),
        P(("dp", "expert"), None),
        P("dp", "expert", None, None),
        P("expert", "tensor", None),
        P("expert", None, "tensor"),
        P(("dp", "expert"), None),
        P("tensor", None),
        P(None, "tensor"),
    )
    return jax.shard_map(
        on_device,
        mesh=mesh,
        in_specs=placed,
        out_specs=(P(("dp", "expert"), "tensor"), P(("dp", "expert"), "tensor")),
        check_vma=False,
    )
```

time: 223 us -> 167 us (0.75)
  the two profiles are of different devices: /device:TPU:1 before, /device:TPU:4 now
where the time goes in v1:
time: 167 us; the launch traced here: 166 us
  starting transfers between devices  62.6 us (37%)
  waiting for transfers between devices  59.6 us (36%)
  local copies, waits for them, and re-layouts  16.5 us (10%)
  matrix products  16.5 us (10%)
  other arithmetic  9.69 us (6%)
    all_to_all x2, waiting for transfers between devices, on_device(): lax.all_to_all(sent.reshape(experts, cap, quarter), 'expert', split_axis=...  33.3 us
    all_to_all x2, starting transfers between devices, on_device(): lax.all_to_all(sent.reshape(experts, cap, quarter), 'expert', split_axis=...  29.1 us
    all_to_all x2, waiting for transfers between devices, on_device(): lax.all_to_all(slot_grad.reshape(experts, cap, quarter), 'expert', split_...  17.6 us
    dot_general x11, matrix products, dot(): lax.dot_general(a, b, (dims, ((), ())), preferred_element_type=jnp.float32)  16.5 us
    all_to_all x2, starting transfers between devices, on_device(): lax.all_to_all(slot_grad.reshape(experts, cap, quarter), 'expert', split_...  12.2 us
    ppermute x3, starting transfers between devices, pair_sum(): away = lax.ppermute(chip.astype(jnp.bfloat16), 'tensor', CHIP_SWAP)  9.36 us
    ppermute x3, waiting for transfers between devices, pair_sum(): away = lax.ppermute(chip.astype(jnp.bfloat16), 'tensor', CHIP_SWAP)  7.46 us
    ppermute x3, starting transfers between devices, pair_sum(): chip = mine + lax.ppermute(other, 'tensor', CORE_SWAP)  6.2 us
  transfers between devices with their start and end apart: 13, of which 7 were waited for; matrix products, arithmetic and copies ran while one was open for 22% of the time, Pallas kernels for 0%

profile of v1, /device:TPU:4, one launch (start us, length us, event | category | flops | bytes accessed | tf_op | source)
XLA Modules:
  0.0 166.0 jit_solution(5174062886716504324)
XLA Ops:
  3.8 1.4 fusion
  6.2 23.4 %all-to-all-start = ((bf16[64,4,1280]{2,1,0:T(4,128)(2,1)}), bf16[64,4,1280]{2,1,0:T(4,128)(2,1)S(1)}, u32[]{:S(2)}, u32[]{:S(2)}) async-start(bf16[64,4,1280]{2,1,0:T(4,128)(2,1)} %reshape.46), calls=%async_computation | async-start | bytes 1310720 | tf_op jit(solution)/shard_map/all_to_all | solution.py:66
  31.1 2.3 %reshape.50 = bf16[64,4,1280]{2,1,0:T(4,128)(2,1)} reshape(bf16[256,1280]{1,0:T(8,128)(2,1)} %fusion.1) | data formatting | bytes 1310720 | tf_op jit(solution)/shard_map/reshape | solution.py:67
  33.4 18.3 %all-to-all-done = bf16[64,4,1280]{2,1,0:T(4,128)(2,1)S(1)} async-done(((bf16[64,4,1280]{2,1,0:T(4,128)(2,1)}), bf16[64,4,1280]{2,1,0:T(4,128)(2,1)S(1)}, u32[]{:S(2)}, u32[]{:S(2)}) %all-to-all-start) | async-done | bytes 655392 | tf_op jit(solution)/shard_map/all_to_all | solution.py:66
  51.8 5.7 %all-to-all-start.2 = ((bf16[64,4,1280]{2,1,0:T(4,128)(2,1)}), bf16[64,4,1280]{2,1,0:T(4,128)(2,1)}, u32[]{:S(2)}, u32[]{:S(2)}) async-start(bf16[64,4,1280]{2,1,0:T(4,128)(2,1)} %reshape.50), calls=%async_computation.2 | async-start | bytes 1310720 | tf_op jit(solution)/shard_map/all_to_all | solution.py:66
  58.5 2.5 %fusion.8 = f32[256,768]{1,0:T(8,128)S(1)} fusion(bf16[256,1280]{1,0:T(8,128)(2,1)} %reshape.47, bf16[1,768,1280]{2,1,0:T(8,128)(2,1)} %param.14), kind=kOutput, calls=%fused_computation.15 | convolution fusion | flops 503316480 | bytes 3407872 | tf_op jit(solution)/shard_map/dot_general | solution.py:13
  61.8 1.9 %collective-permute-start = (f32[128,768]{1,0:T(8,128)}, f32[128,768]{1,0:T(8,128)}, u32[]{:S(2)}, u32[]{:S(2)}) collective-permute-start(f32[128,768]{1,0:T(8,128)} %constant_dynamic-slice_fusion.2), channel_id=1, source_target_pairs={{0,1},{1,0},{2,3},{3,2},{4,5},{5,4},{6,7},{7,6},{8,9},{9,8},{10,11... | collective-permute-start | bytes 1179656 | tf_op jit(solution)/shard_map/ppermute | solution.py:21
  63.7 15.0 %all-to-all-done.2 = bf16[64,4,1280]{2,1,0:T(4,128)(2,1)} async-done(((bf16[64,4,1280]{2,1,0:T(4,128)(2,1)}), bf16[64,4,1280]{2,1,0:T(4,128)(2,1)}, u32[]{:S(2)}, u32[]{:S(2)}) %all-to-all-start.2) | async-done | bytes 655392 | tf_op jit(solution)/shard_map/all_to_all | solution.py:66
  78.7 2.2 %reshape.51 = bf16[256,1280]{1,0:T(8,128)(2,1)} reshape(bf16[64,4,1280]{2,1,0:T(4,128)(2,1)} %all-to-all-done.2) | data formatting | bytes 1310720 | tf_op jit(solution)/shard_map/reshape | solution.py:76
  80.9 2.5 %fusion.6 = f32[256,768]{1,0:T(8,128)S(1)} fusion(bf16[256,1280]{1,0:T(8,128)(2,1)} %reshape.51, bf16[1,768,1280]{2,1,0:T(8,128)(2,1)} %param.14), kind=kOutput, calls=%fused_computation.13 | convolution fusion | flops 503316480 | bytes 3407872 | tf_op jit(solution)/shard_map/dot_general | solution.py:13
  84.2 1.9 %collective-permute-start.3 = (f32[128,768]{1,0:T(8,128)}, f32[128,768]{1,0:T(8,128)}, u32[]{:S(2)}, u32[]{:S(2)}) collective-permute-start(f32[128,768]{1,0:T(8,128)} %constant_dynamic-slice_fusion.1), channel_id=1, source_target_pairs={{0,1},{1,0},{2,3},{3,2},{4,5},{5,4},{6,7},{7,6},{8,9},{9,8},{10,11... | collective-permute-start | bytes 1179656 | tf_op jit(solution)/shard_map/ppermute | solution.py:21
  86.2 1.7 %fusion.27 = bf16[128,768]{1,0:T(8,128)(2,1)} fusion(f32[128,768]{1,0:T(8,128)} %collective-permute-done, f32[256,768]{1,0:T(8,128)S(1)} %fusion.8, s32[]{:T(128)S(6)} %select_n.92), kind=kLoop, calls=%fused_computation.51 | loop fusion | flops 196608 | bytes 983044 | tf_op jit(solution)/shard_map/convert_element_type | solution.py:22
  87.9 3.4 %collective-permute-start.1 = (bf16[128,768]{1,0:T(8,128)(2,1)}, bf16[128,768]{1,0:T(8,128)(2,1)}, u32[]{:S(2)}, u32[]{:S(2)}) collective-permute-start(bf16[128,768]{1,0:T(8,128)(2,1)} %fusion.27), channel_id=1, source_target_pairs={{0,2},{1,3},{2,0},{3,1},{4,6},{5,7},{6,4},{7,5},{8,10},{9,11},{10,... | collective-permute-start | bytes 589832 | tf_op jit(solution)/shard_map/ppermute | solution.py:22
  92.4 1.8 %reshape.48 = bf16[256,768]{1,0:T(8,128)(2,1)} reshape(bf16[64,4,768]{2,1,0:T(4,128)(2,1)} %get-tuple-element.6) | data formatting | bytes 786432 | tf_op jit(solution)/shard_map/reshape | solution.py:78
  94.2 3.1 %collective-permute-done.1 = bf16[128,768]{1,0:T(8,128)(2,1)} collective-permute-done((bf16[128,768]{1,0:T(8,128)(2,1)}, bf16[128,768]{1,0:T(8,128)(2,1)}, u32[]{:S(2)}, u32[]{:S(2)}) %collective-permute-start.1) | collective-permute-done | bytes 196640 | tf_op jit(solution)/shard_map/ppermute | solution.py:22
  98.7 1.9 %collective-permute-start.2 = (bf16[128,768]{1,0:T(8,128)(2,1)S(1)}, bf16[128,768]{1,0:T(8,128)(2,1)S(1)}, u32[]{:S(2)}, u32[]{:S(2)}) collective-permute-start(bf16[128,768]{1,0:T(8,128)(2,1)S(1)} %multiply_convert_fusion.1), channel_id=1, source_target_pairs={{0,1},{1,0},{2,3},{3,2},{4,5},{5,4},{6,7},{7,6},{8,9},{9,8},{10,11... | collective-permute-start | bytes 589832 | tf_op jit(solution)/shard_map/ppermute | solution.py:28
  100.6 1.7 %fusion.28 = bf16[128,768]{1,0:T(8,128)(2,1)} fusion(f32[128,768]{1,0:T(8,128)} %collective-permute-done.3, f32[256,768]{1,0:T(8,128)S(1)} %fusion.6, s32[]{:T(128)S(6)} %select_n.92), kind=kLoop, calls=%fused_computation.52 | loop fusion | flops 196608 | bytes 983044 | tf_op jit(solution)/shard_map/convert_element_type | solution.py:22
  102.3 3.4 %collective-permute-start.4 = (bf16[128,768]{1,0:T(8,128)(2,1)}, bf16[128,768]{1,0:T(8,128)(2,1)}, u32[]{:S(2)}, u32[]{:S(2)}) collective-permute-start(bf16[128,768]{1,0:T(8,128)(2,1)} %fusion.28), channel_id=1, source_target_pairs={{0,2},{1,3},{2,0},{3,1},{4,6},{5,7},{6,4},{7,5},{8,10},{9,11},{10,... | collective-permute-start | bytes 589832 | tf_op jit(solution)/shard_map/ppermute | solution.py:22
  105.8 1.6 convolution_convert_fusion.1
  107.3 2.3 %reshape.49 = bf16[64,4,1280]{2,1,0:T(4,128)(2,1)} reshape(bf16[256,1280]{1,0:T(8,128)(2,1)} %convolution_convert_fusion.1) | data formatting | bytes 1310720 | tf_op jit(solution)/shard_map/reshape | solution.py:82
  109.7 5.8 %all-to-all-start.1 = ((bf16[64,4,1280]{2,1,0:T(4,128)(2,1)}), bf16[64,4,1280]{2,1,0:T(4,128)(2,1)}, u32[]{:S(2)}, u32[]{:S(2)}) async-start(bf16[64,4,1280]{2,1,0:T(4,128)(2,1)} %reshape.49), calls=%async_computation.1 | async-start | bytes 1310720 | tf_op jit(solution)/shard_map/all_to_all | solution.py:81
  117.6 1.9 %collective-permute-start.5 = (bf16[128,768]{1,0:T(8,128)(2,1)S(1)}, bf16[128,768]{1,0:T(8,128)(2,1)S(1)}, u32[]{:S(2)}, u32[]{:S(2)}) collective-permute-start(bf16[128,768]{1,0:T(8,128)(2,1)S(1)} %multiply_convert_fusion), channel_id=1, source_target_pairs={{0,1},{1,0},{2,3},{3,2},{4,5},{5,4},{6,7},{7,6},{8,9},{9,8},{10,11... | collective-permute-start | bytes 589832 | tf_op jit(solution)/shard_map/ppermute | solution.py:28
  119.6 2.3 %fusion.36 = f32[160,768]{1,0:T(8,128)S(1)} fusion(bf16[160,1280]{1,0:T(8,128)(2,1)S(1)} %copy-done.2, bf16[768,1280]{1,0:T(8,128)(2,1)} %param.17), kind=kOutput, calls=%fused_computation.67 | convolution fusion | flops 314572800 | bytes 2867200 | tf_op jit(solution)/shard_map/dot_general | solution.py:13
  122.6 2.4 %collective-permute-start.6 = (f32[80,768]{1,0:T(8,128)}, f32[80,768]{1,0:T(8,128)S(1)}, u32[]{:S(2)}, u32[]{:S(2)}) collective-permute-start(f32[80,768]{1,0:T(8,128)} %constant_dynamic-slice_fusion), channel_id=1, source_target_pairs={{0,1},{1,0},{2,3},{3,2},{4,5},{5,4},{6,7},{7,6},{8,9},{9,8},{10,11... | collective-permute-start | bytes 737288 | tf_op jit(solution)/shard_map/ppermute | solution.py:21
  126.8 10.3 %all-to-all-done.1 = bf16[64,4,1280]{2,1,0:T(4,128)(2,1)} async-done(((bf16[64,4,1280]{2,1,0:T(4,128)(2,1)}), bf16[64,4,1280]{2,1,0:T(4,128)(2,1)}, u32[]{:S(2)}, u32[]{:S(2)}) %all-to-all-start.1) | async-done | bytes 655392 | tf_op jit(solution)/shard_map/all_to_all | solution.py:81
  137.1 6.4 %all-to-all-start.3 = ((bf16[64,4,1280]{2,1,0:T(4,128)(2,1)}), bf16[64,4,1280]{2,1,0:T(4,128)(2,1)S(1)}, u32[]{:S(2)}, u32[]{:S(2)}) async-start(bf16[64,4,1280]{2,1,0:T(4,128)(2,1)} %reshape.53), calls=%async_computation.3 | async-start | bytes 1310720 | tf_op jit(solution)/shard_map/all_to_all | solution.py:81
  143.5 2.6 %collective-permute-start.7 = (bf16[80,768]{1,0:T(8,128)(2,1)S(1)}, bf16[80,768]{1,0:T(8,128)(2,1)S(1)}, u32[]{:S(2)}, u32[]{:S(2)}) collective-permute-start(bf16[80,768]{1,0:T(8,128)(2,1)S(1)} %fusion.31), channel_id=1, source_target_pairs={{0,2},{1,3},{2,0},{3,1},{4,6},{5,7},{6,4},{7,5},{8,10},{9,11},{10,... | collective-permute-start | bytes 368648 | tf_op jit(solution)/shard_map/ppermute | solution.py:22
  146.1 4.3 %collective-permute-done.7 = bf16[80,768]{1,0:T(8,128)(2,1)S(1)} collective-permute-done((bf16[80,768]{1,0:T(8,128)(2,1)S(1)}, bf16[80,768]{1,0:T(8,128)(2,1)S(1)}, u32[]{:S(2)}, u32[]{:S(2)}) %collective-permute-start.7) | collective-permute-done | bytes 122912 | tf_op jit(solution)/shard_map/ppermute | solution.py:22
  151.4 1.9 %collective-permute-start.8 = (bf16[80,768]{1,0:T(8,128)(2,1)S(1)}, bf16[80,768]{1,0:T(8,128)(2,1)S(1)}, u32[]{:S(2)}, u32[]{:S(2)}) collective-permute-start(bf16[80,768]{1,0:T(8,128)(2,1)S(1)} %multiply_convert_fusion.2), channel_id=1, source_target_pairs={{0,1},{1,0},{2,3},{3,2},{4,5},{5,4},{6,7},{7,6},{8,9},{9,8},{10,11... | collective-permute-start | bytes 368648 | tf_op jit(solution)/shard_map/ppermute | solution.py:28
  154.7 1.6 convolution_convert_fusion.2
  156.2 1.4 convolution_bitcast_fusion.1
  157.6 7.3 %all-to-all-done.3 = bf16[64,4,1280]{2,1,0:T(4,128)(2,1)S(1)} async-done(((bf16[64,4,1280]{2,1,0:T(4,128)(2,1)}), bf16[64,4,1280]{2,1,0:T(4,128)(2,1)S(1)}, u32[]{:S(2)}, u32[]{:S(2)}) %all-to-all-start.3) | async-done | bytes 655392 | tf_op jit(solution)/shard_map/all_to_all | solution.py:81
  (57 shorter events, 18.5 us)
Async XLA Ops:
  0.6 105.1 %copy-start = (bf16[1,1280,768]{2,1,0:T(8,128)(2,1)S(1)}, bf16[1,1280,768]{2,1,0:T(8,128)(2,1)}, u32[]{:S(2)}) copy-start(bf16[1,1280,768]{2,1,0:T(8,128)(2,1)} %param.13) | copy-start | bytes 5898244
  2.5 1.2 copy-start.6
  3.8 26.1 %copy-start.1 = (bf16[160,1280]{1,0:T(8,128)(2,1)S(1)}, bf16[160,1280]{1,0:T(8,128)(2,1)}, u32[]{:S(2)}) copy-start(bf16[160,1280]{1,0:T(8,128)(2,1)} %param.9) | copy-start | bytes 1228804
  6.2 45.5 %all-to-all-start = ((bf16[64,4,1280]{2,1,0:T(4,128)(2,1)}), bf16[64,4,1280]{2,1,0:T(4,128)(2,1)S(1)}, u32[]{:S(2)}, u32[]{:S(2)}) async-start(bf16[64,4,1280]{2,1,0:T(4,128)(2,1)} %reshape.46), calls=%async_computation | async-start | bytes 1310720 | tf_op jit(solution)/shard_map/all_to_all | solution.py:66
  51.8 26.9 %all-to-all-start.2 = ((bf16[64,4,1280]{2,1,0:T(4,128)(2,1)}), bf16[64,4,1280]{2,1,0:T(4,128)(2,1)}, u32[]{:S(2)}, u32[]{:S(2)}) async-start(bf16[64,4,1280]{2,1,0:T(4,128)(2,1)} %reshape.50), calls=%async_computation.2 | async-start | bytes 1310720 | tf_op jit(solution)/shard_map/all_to_all | solution.py:66
  61.8 24.4 %collective-permute-start = (f32[128,768]{1,0:T(8,128)}, f32[128,768]{1,0:T(8,128)}, u32[]{:S(2)}, u32[]{:S(2)}) collective-permute-start(f32[128,768]{1,0:T(8,128)} %constant_dynamic-slice_fusion.2), channel_id=1, source_target_pairs={{0,1},{1,0},{2,3},{3,2},{4,5},{5,4},{6,7},{7,6},{8,9},{9,8},{10,11... | collective-permute-start | bytes 1179656 | tf_op jit(solution)/shard_map/ppermute | solution.py:21
  80.9 10.4 %copy-start.5 = (bf16[1,1,512,768]{3,2,1,0:T(8,128)(2,1)S(1)}, bf16[1,1,512,768]{3,2,1,0:T(8,128)(2,1)}, u32[]{:S(2)}) copy-start(bf16[1,1,512,768]{3,2,1,0:T(8,128)(2,1)} %param.12) | copy-start | bytes 2359300
  84.2 16.4 %collective-permute-start.3 = (f32[128,768]{1,0:T(8,128)}, f32[128,768]{1,0:T(8,128)}, u32[]{:S(2)}, u32[]{:S(2)}) collective-permute-start(f32[128,768]{1,0:T(8,128)} %constant_dynamic-slice_fusion.1), channel_id=1, source_target_pairs={{0,1},{1,0},{2,3},{3,2},{4,5},{5,4},{6,7},{7,6},{8,9},{9,8},{10,11... | collective-permute-start | bytes 1179656 | tf_op jit(solution)/shard_map/ppermute | solution.py:21
  87.9 9.5 %collective-permute-start.1 = (bf16[128,768]{1,0:T(8,128)(2,1)}, bf16[128,768]{1,0:T(8,128)(2,1)}, u32[]{:S(2)}, u32[]{:S(2)}) collective-permute-start(bf16[128,768]{1,0:T(8,128)(2,1)} %fusion.27), channel_id=1, source_target_pairs={{0,2},{1,3},{2,0},{3,1},{4,6},{5,7},{6,4},{7,5},{8,10},{9,11},{10,... | collective-permute-start | bytes 589832 | tf_op jit(solution)/shard_map/ppermute | solution.py:22
  98.7 7.1 %collective-permute-start.2 = (bf16[128,768]{1,0:T(8,128)(2,1)S(1)}, bf16[128,768]{1,0:T(8,128)(2,1)S(1)}, u32[]{:S(2)}, u32[]{:S(2)}) collective-permute-start(bf16[128,768]{1,0:T(8,128)(2,1)S(1)} %multiply_convert_fusion.1), channel_id=1, source_target_pairs={{0,1},{1,0},{2,3},{3,2},{4,5},{5,4},{6,7},{7,6},{8,9},{9,8},{10,11... | collective-permute-start | bytes 589832 | tf_op jit(solution)/shard_map/ppermute | solution.py:28
  102.3 14.0 %collective-permute-start.4 = (bf16[128,768]{1,0:T(8,128)(2,1)}, bf16[128,768]{1,0:T(8,128)(2,1)}, u32[]{:S(2)}, u32[]{:S(2)}) collective-permute-start(bf16[128,768]{1,0:T(8,128)(2,1)} %fusion.28), channel_id=1, source_target_pairs={{0,2},{1,3},{2,0},{3,1},{4,6},{5,7},{6,4},{7,5},{8,10},{9,11},{10,... | collective-permute-start | bytes 589832 | tf_op jit(solution)/shard_map/ppermute | solution.py:22
  107.3 8.1 %copy-start.4 = (bf16[64,4,768]{2,1,0:T(4,128)(2,1)S(1)}, bf16[64,4,768]{2,1,0:T(4,128)(2,1)}, u32[]{:S(2)}) copy-start(bf16[64,4,768]{2,1,0:T(4,128)(2,1)} %get-tuple-element.5) | copy-start | bytes 1179652
  109.7 9.9 %copy-start.2 = (bf16[160,1280]{1,0:T(8,128)(2,1)S(1)}, bf16[160,1280]{1,0:T(8,128)(2,1)}, u32[]{:S(2)}) copy-start(bf16[160,1280]{1,0:T(8,128)(2,1)} %param.9) | copy-start | bytes 1228804
  109.7 27.4 %all-to-all-start.1 = ((bf16[64,4,1280]{2,1,0:T(4,128)(2,1)}), bf16[64,4,1280]{2,1,0:T(4,128)(2,1)}, u32[]{:S(2)}, u32[]{:S(2)}) async-start(bf16[64,4,1280]{2,1,0:T(4,128)(2,1)} %reshape.49), calls=%async_computation.1 | async-start | bytes 1310720 | tf_op jit(solution)/shard_map/all_to_all | solution.py:81
  117.6 7.4 %collective-permute-start.5 = (bf16[128,768]{1,0:T(8,128)(2,1)S(1)}, bf16[128,768]{1,0:T(8,128)(2,1)S(1)}, u32[]{:S(2)}, u32[]{:S(2)}) collective-permute-start(bf16[128,768]{1,0:T(8,128)(2,1)S(1)} %multiply_convert_fusion), channel_id=1, source_target_pairs={{0,1},{1,0},{2,3},{3,2},{4,5},{5,4},{6,7},{7,6},{8,9},{9,8},{10,11... | collective-permute-start | bytes 589832 | tf_op jit(solution)/shard_map/ppermute | solution.py:28
  122.6 20.9 %collective-permute-start.6 = (f32[80,768]{1,0:T(8,128)}, f32[80,768]{1,0:T(8,128)S(1)}, u32[]{:S(2)}, u32[]{:S(2)}) collective-permute-start(f32[80,768]{1,0:T(8,128)} %constant_dynamic-slice_fusion), channel_id=1, source_target_pairs={{0,1},{1,0},{2,3},{3,2},{4,5},{5,4},{6,7},{7,6},{8,9},{9,8},{10,11... | collective-permute-start | bytes 737288 | tf_op jit(solution)/shard_map/ppermute | solution.py:21
  125.8 27.5 %copy-start.7 = (s32[160,64]{0,1:T(8,128)S(1)}, s32[160,64]{0,1:T(8,128)}, u32[]{:S(2)}) copy-start(s32[160,64]{0,1:T(8,128)} %copy-done.6) | copy-start | bytes 122884
  137.1 27.9 %all-to-all-start.3 = ((bf16[64,4,1280]{2,1,0:T(4,128)(2,1)}), bf16[64,4,1280]{2,1,0:T(4,128)(2,1)S(1)}, u32[]{:S(2)}, u32[]{:S(2)}) async-start(bf16[64,4,1280]{2,1,0:T(4,128)(2,1)} %reshape.53), calls=%async_computation.3 | async-start | bytes 1310720 | tf_op jit(solution)/shard_map/all_to_all | solution.py:81
  143.5 11.2 %copy-start.3 = (bf16[1280,768]{1,0:T(8,128)(2,1)S(1)}, bf16[1280,768]{1,0:T(8,128)(2,1)}, u32[]{:S(2)}) copy-start(bf16[1280,768]{1,0:T(8,128)(2,1)} %param.16) | copy-start | bytes 5898244
  143.5 6.9 %collective-permute-start.7 = (bf16[80,768]{1,0:T(8,128)(2,1)S(1)}, bf16[80,768]{1,0:T(8,128)(2,1)S(1)}, u32[]{:S(2)}, u32[]{:S(2)}) collective-permute-start(bf16[80,768]{1,0:T(8,128)(2,1)S(1)} %fusion.31), channel_id=1, source_target_pairs={{0,2},{1,3},{2,0},{3,1},{4,6},{5,7},{6,4},{7,5},{8,10},{9,11},{10,... | collective-permute-start | bytes 368648 | tf_op jit(solution)/shard_map/ppermute | solution.py:22
  151.4 3.2 %collective-permute-start.8 = (bf16[80,768]{1,0:T(8,128)(2,1)S(1)}, bf16[80,768]{1,0:T(8,128)(2,1)S(1)}, u32[]{:S(2)}, u32[]{:S(2)}) collective-permute-start(bf16[80,768]{1,0:T(8,128)(2,1)S(1)} %multiply_convert_fusion.2), channel_id=1, source_target_pairs={{0,1},{1,0},{2,3},{3,2},{4,5},{5,4},{6,7},{7,6},{8,9},{9,8},{10,11... | collective-permute-start | bytes 368648 | tf_op jit(solution)/shard_map/ppermute | solution.py:28
  154.7 10.3 %copy-start.8 = (pred[160,64,4]{0,2,1:T(4,128)(4,1)S(1)}, pred[160,64,4]{0,2,1:T(4,128)(4,1)}, u32[]{:S(2)}) copy-start(pred[160,64,4]{0,2,1:T(4,128)(4,1)} %get-tuple-element.4) | copy-start | bytes 122884

commit v2 on v0

v2 whole, which is shorter than its diff:
```python
import functools

import jax
import jax.numpy as jnp
from jax import lax
from jax.experimental import pallas as pl
from jax.experimental.pallas import tpu as pltpu
from jax.sharding import PartitionSpec as P

TOP = 6
CAP = 8
CHUNKS = 2
CORE_SWAP = [(0, 1), (1, 0), (2, 3), (3, 2)]
CHIP_SWAP = [(0, 2), (1, 3), (2, 0), (3, 1)]
F32, BF16 = jnp.float32, jnp.bfloat16
WHOLE = pl.BlockSpec(memory_space=pltpu.VMEM)
SCALAR = pl.BlockSpec(memory_space=pltpu.SMEM)


def dot(a, b, dims=((1,), (1,))):
    return lax.dot_general(a, b, (dims, ((), ())), preferred_element_type=F32)


def call(body, outs, specs, scratch=(), flops=0, moved=0):
    return pl.pallas_call(
        body,
        out_shape=outs,
        in_specs=specs,
        out_specs=jax.tree.map(lambda _: WHOLE, outs),
        scratch_shapes=list(scratch),
        compiler_params=pltpu.CompilerParams(vmem_limit_bytes=24 << 20),
        cost_estimate=pl.CostEstimate(flops=flops, bytes_accessed=moved, transcendentals=0),
    )


def route_body(ids_ref, prob_ref, grad_ref, sent_ref, mask_ref, *, experts):
    tokens = ids_ref.shape[1]
    expert = lax.broadcasted_iota(jnp.int32, (experts, tokens), 0)
    named = jnp.zeros((experts, tokens), F32)
    prob = jnp.zeros((experts, tokens), F32)
    for pick in range(TOP):
        hit = ids_ref[pick : pick + 1, :] == expert
        named = jnp.where(hit, 1.0, named)
        prob = jnp.where(hit, prob_ref[pick : pick + 1, :], prob)
    square = (tokens, tokens)
    earlier = lax.broadcasted_iota(jnp.int32, square, 0) < lax.broadcasted_iota(jnp.int32, square, 1)
    rank = dot(named.astype(BF16), jnp.where(earlier, 1.0, 0.0).astype(BF16), ((1,), (0,)))
    rank = jnp.where(named > 0.0, rank, float(CAP))
    shape = (experts, CAP, tokens)
    slot = lax.broadcasted_iota(jnp.int32, shape, 1).astype(F32)
    hit = jnp.broadcast_to(rank[:, None, :], shape) == slot
    scale = jnp.sum(
        jnp.where(hit, jnp.broadcast_to(prob[:, None, :], shape), 0.0), axis=2, keepdims=True
    )
    mask = jnp.where(hit, 1.0, 0.0).reshape(experts * CAP, tokens).astype(BF16)
    mask_ref[...] = mask
    picked = dot(mask, grad_ref[...], ((1,), (0,)))
    sent_ref[...] = (picked * scale.reshape(experts * CAP, 1)).astype(BF16)


def part_body(core_ref, rows_ref, w_ref, mine_ref, other_ref, full_ref, *, first):
    count = full_ref.shape[0]
    half = count // 2
    full_ref[...] = dot(rows_ref[first : first + count, :], w_ref[...])
    mine = pl.multiple_of(core_ref[0] * half, half)
    other = pl.multiple_of((1 - core_ref[0]) * half, half)
    mine_ref[...] = full_ref[pl.ds(mine, half), :]
    other_ref[...] = full_ref[pl.ds(other, half), :]


def gate_body(core_ref, mine_ref, pair_ref, away_ref, gate_ref, up_ref, *, first):
    half = up_ref.shape[0]
    start = pl.multiple_of(first + core_ref[0] * half, 16)
    gate = gate_ref[pl.ds(start, half), :].astype(F32)
    hidden = mine_ref[...] + pair_ref[...] + away_ref[...].astype(F32)
    up_ref[...] = (hidden * gate).astype(BF16)


def up_body(core_ref, *refs):
    *ups, w_ref, out_ref = refs
    half = ups[0].shape[0]
    chunks = len(ups) // 2
    for side in range(2):
        lane = core_ref[0] if side == 0 else 1 - core_ref[0]
        rows = jnp.concatenate([ups[2 * chunk + side][...] for chunk in range(chunks)], axis=0)
        grad = dot(rows, w_ref[...]).astype(BF16)
        for chunk in range(chunks):
            start = pl.multiple_of((2 * chunk + lane) * half, 16)
            out_ref[pl.ds(start, half), :] = grad[chunk * half : (chunk + 1) * half]


def combine_body(mask_ref, back_ref, out_ref):
    out_ref[...] = dot(mask_ref[...], back_ref[...], ((0,), (0,))).astype(BF16)


def tensor_sum(core, parts, gate, count):
    half = count // 2
    width = gate.shape[1]
    pairs = [lax.ppermute(other, "tensor", CORE_SWAP) for _, other in parts]
    aways = [
        lax.ppermute((mine + pair).astype(BF16), "tensor", CHIP_SWAP)
        for (mine, _), pair in zip(parts, pairs)
    ]
    ups = []
    for chunk, ((mine, _), pair, away) in enumerate(zip(parts, pairs, aways)):
        up = call(
            functools.partial(gate_body, first=chunk * count),
            jax.ShapeDtypeStruct((half, width), BF16),
            [SCALAR] + [WHOLE] * 4,
            flops=3 * half * width,
            moved=14 * half * width,
        )(core, mine, pair, away, gate)
        ups += [up, lax.ppermute(up, "tensor", CORE_SWAP)]
    return ups


def partial_rows(core, rows, weight, chunk, count):
    width, depth = weight.shape
    half = jax.ShapeDtypeStruct((count // 2, width), F32)
    return call(
        functools.partial(part_body, first=chunk * count),
        (half, half),
        [SCALAR, WHOLE, WHOLE],
        [pltpu.VMEM((count, width), F32)],
        flops=2 * count * width * depth,
        moved=2 * width * depth,
    )(core, rows, weight)


def up_project(core, ups, weight):
    width, depth = weight.shape
    rows = ups[0].shape[0] * len(ups)
    return call(
        up_body,
        jax.ShapeDtypeStruct((rows, width), BF16),
        [SCALAR] + [WHOLE] * (len(ups) + 1),
        flops=2 * rows * width * depth,
        moved=2 * width * depth,
    )(core, *ups, weight)


def on_device(
    grad_out, expert_ids, route_probs, saved_gate, w_up, w_down, shared_gate, shared_up, shared_down
):
    experts = lax.axis_size("expert")
    tokens, quarter = grad_out.shape
    slots = experts * CAP
    core = (lax.axis_index("tensor") & 1).reshape(1)
    sent, mask = call(
        functools.partial(route_body, experts=experts),
        (
            jax.ShapeDtypeStruct((slots, quarter), BF16),
            jax.ShapeDtypeStruct((slots, tokens), BF16),
        ),
        [WHOLE] * 3,
        flops=2 * slots * tokens * quarter,
        moved=4 * slots * quarter,
    )(expert_ids.T, route_probs.T, grad_out)
    arrived = lax.all_to_all(
        sent.reshape(experts, CAP, quarter), "expert", split_axis=0, concat_axis=0, tiled=True
    ).reshape(slots, quarter)

    dense = [partial_rows(core, grad_out, shared_down, 0, tokens)]
    dense_up = tensor_sum(core, dense, shared_gate, tokens)
    arrived, dense_up = lax.optimization_barrier((arrived, dense_up))
    shared_grad = up_project(core, dense_up, shared_up)

    count = slots // CHUNKS
    parts = [partial_rows(core, arrived, w_down[0], chunk, count) for chunk in range(CHUNKS)]
    ups = tensor_sum(core, parts, saved_gate[0, 0], count)
    slot_grad = up_project(core, ups, w_up[0])
    back = lax.all_to_all(
        slot_grad.reshape(experts, CAP, quarter), "expert", split_axis=0, concat_axis=0, tiled=True
    ).reshape(slots, quarter)
    moe_grad = call(
        combine_body,
        jax.ShapeDtypeStruct((tokens, quarter), BF16),
        [WHOLE, WHOLE],
        flops=2 * slots * tokens * quarter,
        moved=2 * slots * quarter,
    )(mask, back)
    return (moe_grad, shared_grad)


def solution(mesh):
    placed = (
        P(("dp", "expert"), "tensor"),
        P(("dp", "expert"), None),
        P(("dp", "expert"), None),
        P("dp", "expert", None, None),
        P("expert", "tensor", None),
        P("expert", None, "tensor"),
        P(("dp", "expert"), None),
        P("tensor", None),
        P(None, "tensor"),
    )
    return jax.shard_map(
        on_device,
        mesh=mesh,
        in_specs=placed,
        out_specs=(P(("dp", "expert"), "tensor"), P(("dp", "expert"), "tensor")),
        check_vma=False,
    )
```

time: 223 us -> 135 us (0.61)
  waiting for transfers between devices: 130 us -> 54.3 us
  starting transfers between devices: 38 us -> 59.5 us
  other arithmetic: 18.9 us -> 0.11 us
  matrix products: 17.4 us -> 0 us
  between operations: 14.2 us -> 0.85 us
  Pallas kernels: 0 us -> 9.9 us
  local copies, waits for them, and re-layouts: 1.76 us -> 7.54 us
    psum x1 -> x0, waiting for transfers between devices: 70.8 us -> none  [on_device(): hidden = lax.psum(partial_hidden, 'tensor')]
    ppermute x0 -> x9, starting transfers between devices: none -> 28.9 us  [the longest x3 10.5 us: tensor_sum(): ups += [up, lax.ppermute(up, 'tensor', CORE_SWAP)]]
    another operation x3 -> x0, other arithmetic: 18.2 us -> none
    dot_general x6 -> x0, matrix products: 17.4 us -> none  [the longest x1 4.31 us: on_device(): lax.dot_general(arrived, w_down[0], (((1,), (1,)), ((), ())), preferred_e...]
    all_to_all x2, waiting for transfers between devices: 59.7 us -> 45.4 us  [the longest x1 31.1 us: on_device(): lax.all_to_all(slot_grad.reshape(experts, CAP, quarter), 'expert', split_...]
    pallas_call x0 -> x10, Pallas kernels: none -> 9.9 us  [the longest x2 4.39 us: up_project(): call(up_body, jax.ShapeDtypeStruct((rows, width), BF16), [SCALAR] + [WHOL...]
    ppermute x0 -> x9, waiting for transfers between devices: none -> 8.92 us  [the longest x3 5.81 us: tensor_sum(): lax.ppermute((mine + pair).astype(BF16), 'tensor', CHIP_SWAP)]
    all_to_all x2, starting transfers between devices: 38 us -> 30.6 us  [the longest x1 24 us: on_device(): lax.all_to_all(sent.reshape(experts, CAP, quarter), 'expert', split_axis=...]
  transfers between devices with their start and end apart: 3 -> 11, of which waited for: 3 -> 7; matrix products, arithmetic and copies ran while one was open for 3% -> 0% of each run, Pallas kernels for 0% -> 3%
where the time goes in v2:
time: 135 us; the launch traced here: 132 us
  starting transfers between devices  59.5 us (44%)
  waiting for transfers between devices  54.3 us (40%)
  Pallas kernels  9.9 us (7%)
  local copies, waits for them, and re-layouts  7.54 us (6%)
    all_to_all x1, waiting for transfers between devices, on_device(): lax.all_to_all(slot_grad.reshape(experts, CAP, quarter), 'expert', split_...  31.1 us
    all_to_all x1, starting transfers between devices, on_device(): lax.all_to_all(sent.reshape(experts, CAP, quarter), 'expert', split_axis=...  24 us
    all_to_all x1, waiting for transfers between devices, on_device(): lax.all_to_all(sent.reshape(experts, CAP, quarter), 'expert', split_axis=...  14.3 us
    ppermute x3, starting transfers between devices, tensor_sum(): ups += [up, lax.ppermute(up, 'tensor', CORE_SWAP)]  10.5 us
    ppermute x3, starting transfers between devices, tensor_sum(): pairs = [lax.ppermute(other, 'tensor', CORE_SWAP) for _, other in parts]  10.1 us
    ppermute x3, starting transfers between devices, tensor_sum(): lax.ppermute((mine + pair).astype(BF16), 'tensor', CHIP_SWAP)  8.41 us
    unnamed x24, local copies, waits for them, and re-layouts  7.54 us
    all_to_all x1, starting transfers between devices, on_device(): lax.all_to_all(slot_grad.reshape(experts, CAP, quarter), 'expert', split_...  6.63 us
  transfers between devices with their start and end apart: 11, of which 7 were waited for; matrix products, arithmetic and copies ran while one was open for 0% of the time, Pallas kernels for 3%

profile of v2, /device:TPU:1, one launch (start us, length us, event | category | flops | bytes accessed | tf_op | source)
XLA Modules:
  0.0 132.3 jit_solution(15497159298878454625)
XLA Ops:
  0.6 1.0 copy-done.5
  1.6 0.7 copy-done.10
  3.0 1.8 %shard_map.104 = (bf16[512,1280]{1,0:T(8,128)(2,1)}, bf16[512,160]{1,0:T(8,128)(2,1)S(1)}) custom-call(s32[6,160]{1,0:T(8,128)S(1)} %bitcast.18, f32[6,160]{1,0:T(8,128)S(1)} %bitcast.19, bf16[160,1280]{1,0:T(8,128)(2,1)S(1)} %copy-done.5), custom_call_target="tpu_custom_call" | custom-call | flops 209715200 | bytes 2621440 | tf_op jit(solution)/shard_map/pallas_call | solution.py:149
  4.8 0.7 copy-done.7
  5.5 24.0 %all-to-all-start = ((bf16[64,8,1280]{2,1,0:T(8,128)(2,1)}), bf16[64,8,1280]{2,1,0:T(8,128)(2,1)S(1)}, u32[]{:S(2)}, u32[]{:S(2)}) async-start(bf16[64,8,1280]{2,1,0:T(8,128)(2,1)} %bitcast.3), calls=%async_computation | async-start | bytes 2621440 | tf_op jit(solution)/shard_map/all_to_all | solution.py:159
  29.5 1.5 %copy-done.4 = bf16[768,1280]{1,0:T(8,128)(2,1)S(1)} copy-done((bf16[768,1280]{1,0:T(8,128)(2,1)S(1)}, bf16[768,1280]{1,0:T(8,128)(2,1)}, u32[]{:S(2)}) %copy-start.4) | copy-done | bytes 1966104
  31.0 1.0 copy-done.6
  32.0 0.8 shard_map.105
  32.9 2.9 %collective-permute-start = (f32[80,768]{1,0:T(8,128)S(1)}, f32[80,768]{1,0:T(8,128)S(1)}, u32[]{:S(2)}, u32[]{:S(2)}) collective-permute-start(f32[80,768]{1,0:T(8,128)S(1)} %get-tuple-element.16), channel_id=1, source_target_pairs={{0,1},{1,0},{2,3},{3,2},{4,5},{5,4},{6,7},{7,6},{8,9},{9,8},{10,11... | collective-permute-start | bytes 737288 | tf_op jit(solution)/shard_map/ppermute | solution.py:99
  35.7 1.1 collective-permute-done.pair_ref
  36.9 3.1 %collective-permute-start.1 = (bf16[80,768]{1,0:T(8,128)(2,1)S(1)}, bf16[80,768]{1,0:T(8,128)(2,1)S(1)}, u32[]{:S(2)}, u32[]{:S(2)}) collective-permute-start(bf16[80,768]{1,0:T(8,128)(2,1)S(1)} %add_convert_fusion.2), channel_id=1, source_target_pairs={{0,2},{1,3},{2,0},{3,1},{4,6},{5,7},{6,4},{7,5},{8,10},{9,11},{10,... | collective-permute-start | bytes 368648 | tf_op jit(solution)/shard_map/ppermute | solution.py:101
  40.0 3.3 %collective-permute-done.1.away_ref = bf16[80,768]{1,0:T(8,128)(2,1)S(1)} collective-permute-done((bf16[80,768]{1,0:T(8,128)(2,1)S(1)}, bf16[80,768]{1,0:T(8,128)(2,1)S(1)}, u32[]{:S(2)}, u32[]{:S(2)}) %collective-permute-start.1) | collective-permute-done | bytes 122912 | tf_op jit(solution)/shard_map/ppermute | solution.py:101
  43.3 0.9 copy-done.9
  44.3 3.1 %collective-permute-start.2 = (bf16[80,768]{1,0:T(8,128)(2,1)S(1)}, bf16[80,768]{1,0:T(8,128)(2,1)S(1)}, u32[]{:S(2)}, u32[]{:S(2)}) collective-permute-start(bf16[80,768]{1,0:T(8,128)(2,1)S(1)} %shard_map.106.refs_0_), channel_id=1, source_target_pairs={{0,1},{1,0},{2,3},{3,2},{4,5},{5,4},{6,7},{7,6},{8,9},{9,8},{10,11... | collective-permute-start | bytes 368648 | tf_op jit(solution)/shard_map/ppermute | solution.py:113
  47.4 1.0 collective-permute-done.2.refs_1_
  48.4 14.3 %all-to-all-done = bf16[64,8,1280]{2,1,0:T(8,128)(2,1)S(1)} async-done(((bf16[64,8,1280]{2,1,0:T(8,128)(2,1)}), bf16[64,8,1280]{2,1,0:T(8,128)(2,1)S(1)}, u32[]{:S(2)}, u32[]{:S(2)}) %all-to-all-start) | async-done | bytes 1310752 | tf_op jit(solution)/shard_map/all_to_all | solution.py:159
  62.7 0.8 shard_map.107
  63.5 5.3 %collective-permute-start.3 = (f32[128,768]{1,0:T(8,128)S(1)}, f32[128,768]{1,0:T(8,128)S(1)}, u32[]{:S(2)}, u32[]{:S(2)}) collective-permute-start(f32[128,768]{1,0:T(8,128)S(1)} %get-tuple-element.19), channel_id=1, source_target_pairs={{0,1},{1,0},{2,3},{3,2},{4,5},{5,4},{6,7},{7,6},{8,9},{9,8},{10,11... | collective-permute-start | bytes 1179656 | tf_op jit(solution)/shard_map/ppermute | solution.py:99
  68.7 0.8 shard_map.109
  69.5 1.9 %collective-permute-start.6 = (f32[128,768]{1,0:T(8,128)S(1)}, f32[128,768]{1,0:T(8,128)S(1)}, u32[]{:S(2)}, u32[]{:S(2)}) collective-permute-start(f32[128,768]{1,0:T(8,128)S(1)} %get-tuple-element.21), channel_id=1, source_target_pairs={{0,1},{1,0},{2,3},{3,2},{4,5},{5,4},{6,7},{7,6},{8,9},{9,8},{10,11... | collective-permute-start | bytes 1179656 | tf_op jit(solution)/shard_map/ppermute | solution.py:99
  71.5 3.1 %collective-permute-start.4 = (bf16[128,768]{1,0:T(8,128)(2,1)S(1)}, bf16[128,768]{1,0:T(8,128)(2,1)S(1)}, u32[]{:S(2)}, u32[]{:S(2)}) collective-permute-start(bf16[128,768]{1,0:T(8,128)(2,1)S(1)} %add_convert_fusion.1), channel_id=1, source_target_pairs={{0,2},{1,3},{2,0},{3,1},{4,6},{5,7},{6,4},{7,5},{8,10},{9,11},{10,... | collective-permute-start | bytes 589832 | tf_op jit(solution)/shard_map/ppermute | solution.py:101
  74.7 2.2 %collective-permute-start.7 = (bf16[128,768]{1,0:T(8,128)(2,1)S(1)}, bf16[128,768]{1,0:T(8,128)(2,1)S(1)}, u32[]{:S(2)}, u32[]{:S(2)}) collective-permute-start(bf16[128,768]{1,0:T(8,128)(2,1)S(1)} %add_convert_fusion), channel_id=1, source_target_pairs={{0,2},{1,3},{2,0},{3,1},{4,6},{5,7},{6,4},{7,5},{8,10},{9,11},{10,... | collective-permute-start | bytes 589832 | tf_op jit(solution)/shard_map/ppermute | solution.py:101
  76.8 2.5 %collective-permute-done.4.away_ref = bf16[128,768]{1,0:T(8,128)(2,1)S(1)} collective-permute-done((bf16[128,768]{1,0:T(8,128)(2,1)S(1)}, bf16[128,768]{1,0:T(8,128)(2,1)S(1)}, u32[]{:S(2)}, u32[]{:S(2)}) %collective-permute-start.4) | collective-permute-done | bytes 196640 | tf_op jit(solution)/shard_map/ppermute | solution.py:101
  79.4 4.3 %collective-permute-start.5 = (bf16[128,768]{1,0:T(8,128)(2,1)S(1)}, bf16[128,768]{1,0:T(8,128)(2,1)S(1)}, u32[]{:S(2)}, u32[]{:S(2)}) collective-permute-start(bf16[128,768]{1,0:T(8,128)(2,1)S(1)} %shard_map.108.refs_0_), channel_id=1, source_target_pairs={{0,1},{1,0},{2,3},{3,2},{4,5},{5,4},{6,7},{7,6},{8,9},{9,8},{10,11... | collective-permute-start | bytes 589832 | tf_op jit(solution)/shard_map/ppermute | solution.py:113
  83.9 3.0 %collective-permute-start.8 = (bf16[128,768]{1,0:T(8,128)(2,1)S(1)}, bf16[128,768]{1,0:T(8,128)(2,1)S(1)}, u32[]{:S(2)}, u32[]{:S(2)}) collective-permute-start(bf16[128,768]{1,0:T(8,128)(2,1)S(1)} %shard_map.110.refs_2_), channel_id=1, source_target_pairs={{0,1},{1,0},{2,3},{3,2},{4,5},{5,4},{6,7},{7,6},{8,9},{9,8},{10,11... | collective-permute-start | bytes 589832 | tf_op jit(solution)/shard_map/ppermute | solution.py:113
  86.9 1.0 collective-permute-done.8.refs_3_
  88.0 2.3 %shard_map.111 = bf16[512,1280]{1,0:T(8,128)(2,1)} custom-call(s32[1]{0:T(128)} %bitcast.2.core_ref, bf16[128,768]{1,0:T(8,128)(2,1)S(1)} %shard_map.108.refs_0_, bf16[128,768]{1,0:T(8,128)(2,1)S(1)} %collective-permute-done.5.refs_1_, bf16[128,768]{1,0:T(8,128)(2,1)S(1)} %shard_map.110.refs_2_, bf16[128,768]{1,0:T(8,128)(2,1)S(1)} %collective-permute-done.8.refs_3_, ...), custom_call_target="tpu_custom_call" | custom-call | flops 1006632960 | bytes 1966080 | tf_op jit(solution)/shard_map/pallas_call | solution.py:133
  90.3 6.6 %all-to-all-start.1 = ((bf16[64,8,1280]{2,1,0:T(8,128)(2,1)}), bf16[64,8,1280]{2,1,0:T(8,128)(2,1)S(1)}, u32[]{:S(2)}, u32[]{:S(2)}) async-start(bf16[64,8,1280]{2,1,0:T(8,128)(2,1)} %bitcast.8), calls=%async_computation.1 | async-start | bytes 2621440 | tf_op jit(solution)/shard_map/all_to_all | solution.py:172
  96.9 2.1 %shard_map.113 = bf16[160,1280]{1,0:T(8,128)(2,1)} custom-call(s32[1]{0:T(128)} %bitcast.2.core_ref, bf16[80,768]{1,0:T(8,128)(2,1)S(1)} %shard_map.106.refs_0_, bf16[80,768]{1,0:T(8,128)(2,1)S(1)} %collective-permute-done.2.refs_1_, bf16[1280,768]{1,0:T(8,128)(2,1)S(1)} %copy-done.3), custom_call_target="tpu_custom_call" | custom-call | flops 314572800 | bytes 1966080 | tf_op jit(solution)/shard_map/pallas_call | solution.py:133
  99.0 31.1 %all-to-all-done.1 = bf16[64,8,1280]{2,1,0:T(8,128)(2,1)S(1)} async-done(((bf16[64,8,1280]{2,1,0:T(8,128)(2,1)}), bf16[64,8,1280]{2,1,0:T(8,128)(2,1)S(1)}, u32[]{:S(2)}, u32[]{:S(2)}) %all-to-all-start.1) | async-done | bytes 1310752 | tf_op jit(solution)/shard_map/all_to_all | solution.py:172
  130.1 0.9 copy-done.8
  131.1 1.2 shard_map.112
  (27 shorter events, 1.1 us)
Async XLA Ops:
  0.6 1.0 copy-start.5
  1.6 0.7 copy-start.10
  2.3 0.7 copy-start.11
  4.8 0.7 copy-start.7
  5.5 57.2 %all-to-all-start = ((bf16[64,8,1280]{2,1,0:T(8,128)(2,1)}), bf16[64,8,1280]{2,1,0:T(8,128)(2,1)S(1)}, u32[]{:S(2)}, u32[]{:S(2)}) async-start(bf16[64,8,1280]{2,1,0:T(8,128)(2,1)} %bitcast.3), calls=%async_computation | async-start | bytes 2621440 | tf_op jit(solution)/shard_map/all_to_all | solution.py:159
  29.5 1.5 %copy-start.4 = (bf16[768,1280]{1,0:T(8,128)(2,1)S(1)}, bf16[768,1280]{1,0:T(8,128)(2,1)}, u32[]{:S(2)}) copy-start(bf16[768,1280]{1,0:T(8,128)(2,1)} %w_ref.1) | copy-start | bytes 5898244
  31.0 1.0 copy-start.6
  32.0 30.6 %copy-start = (bf16[1,768,1280]{2,1,0:T(8,128)(2,1)S(1)}, bf16[1,768,1280]{2,1,0:T(8,128)(2,1)}, u32[]{:S(2)}) copy-start(bf16[1,768,1280]{2,1,0:T(8,128)(2,1)} %param.14) | copy-start | bytes 5898244
  32.9 4.0 %collective-permute-start = (f32[80,768]{1,0:T(8,128)S(1)}, f32[80,768]{1,0:T(8,128)S(1)}, u32[]{:S(2)}, u32[]{:S(2)}) collective-permute-start(f32[80,768]{1,0:T(8,128)S(1)} %get-tuple-element.16), channel_id=1, source_target_pairs={{0,1},{1,0},{2,3},{3,2},{4,5},{5,4},{6,7},{7,6},{8,9},{9,8},{10,11... | collective-permute-start | bytes 737288 | tf_op jit(solution)/shard_map/ppermute | solution.py:99
  36.9 6.4 %collective-permute-start.1 = (bf16[80,768]{1,0:T(8,128)(2,1)S(1)}, bf16[80,768]{1,0:T(8,128)(2,1)S(1)}, u32[]{:S(2)}, u32[]{:S(2)}) collective-permute-start(bf16[80,768]{1,0:T(8,128)(2,1)S(1)} %add_convert_fusion.2), channel_id=1, source_target_pairs={{0,2},{1,3},{2,0},{3,1},{4,6},{5,7},{6,4},{7,5},{8,10},{9,11},{10,... | collective-permute-start | bytes 368648 | tf_op jit(solution)/shard_map/ppermute | solution.py:101
  43.3 0.9 copy-start.9
  44.3 4.1 %collective-permute-start.2 = (bf16[80,768]{1,0:T(8,128)(2,1)S(1)}, bf16[80,768]{1,0:T(8,128)(2,1)S(1)}, u32[]{:S(2)}, u32[]{:S(2)}) collective-permute-start(bf16[80,768]{1,0:T(8,128)(2,1)S(1)} %shard_map.106.refs_0_), channel_id=1, source_target_pairs={{0,1},{1,0},{2,3},{3,2},{4,5},{5,4},{6,7},{7,6},{8,9},{9,8},{10,11... | collective-permute-start | bytes 368648 | tf_op jit(solution)/shard_map/ppermute | solution.py:113
  63.4 15.9 %copy-start.1 = (bf16[1,1,512,768]{3,2,1,0:T(8,128)(2,1)S(1)}, bf16[1,1,512,768]{3,2,1,0:T(8,128)(2,1)}, u32[]{:S(2)}) copy-start(bf16[1,1,512,768]{3,2,1,0:T(8,128)(2,1)} %param.12) | copy-start | bytes 2359300
  63.5 8.0 %collective-permute-start.3 = (f32[128,768]{1,0:T(8,128)S(1)}, f32[128,768]{1,0:T(8,128)S(1)}, u32[]{:S(2)}, u32[]{:S(2)}) collective-permute-start(f32[128,768]{1,0:T(8,128)S(1)} %get-tuple-element.19), channel_id=1, source_target_pairs={{0,1},{1,0},{2,3},{3,2},{4,5},{5,4},{6,7},{7,6},{8,9},{9,8},{10,11... | collective-permute-start | bytes 1179656 | tf_op jit(solution)/shard_map/ppermute | solution.py:99
  69.5 5.1 %collective-permute-start.6 = (f32[128,768]{1,0:T(8,128)S(1)}, f32[128,768]{1,0:T(8,128)S(1)}, u32[]{:S(2)}, u32[]{:S(2)}) collective-permute-start(f32[128,768]{1,0:T(8,128)S(1)} %get-tuple-element.21), channel_id=1, source_target_pairs={{0,1},{1,0},{2,3},{3,2},{4,5},{5,4},{6,7},{7,6},{8,9},{9,8},{10,11... | collective-permute-start | bytes 1179656 | tf_op jit(solution)/shard_map/ppermute | solution.py:99
  71.5 7.9 %collective-permute-start.4 = (bf16[128,768]{1,0:T(8,128)(2,1)S(1)}, bf16[128,768]{1,0:T(8,128)(2,1)S(1)}, u32[]{:S(2)}, u32[]{:S(2)}) collective-permute-start(bf16[128,768]{1,0:T(8,128)(2,1)S(1)} %add_convert_fusion.1), channel_id=1, source_target_pairs={{0,2},{1,3},{2,0},{3,1},{4,6},{5,7},{6,4},{7,5},{8,10},{9,11},{10,... | collective-permute-start | bytes 589832 | tf_op jit(solution)/shard_map/ppermute | solution.py:101
  74.7 9.1 %collective-permute-start.7 = (bf16[128,768]{1,0:T(8,128)(2,1)S(1)}, bf16[128,768]{1,0:T(8,128)(2,1)S(1)}, u32[]{:S(2)}, u32[]{:S(2)}) collective-permute-start(bf16[128,768]{1,0:T(8,128)(2,1)S(1)} %add_convert_fusion), channel_id=1, source_target_pairs={{0,2},{1,3},{2,0},{3,1},{4,6},{5,7},{6,4},{7,5},{8,10},{9,11},{10,... | collective-permute-start | bytes 589832 | tf_op jit(solution)/shard_map/ppermute | solution.py:101
  79.4 8.6 %copy-start.2 = (bf16[1,1280,768]{2,1,0:T(8,128)(2,1)S(1)}, bf16[1,1280,768]{2,1,0:T(8,128)(2,1)}, u32[]{:S(2)}) copy-start(bf16[1,1280,768]{2,1,0:T(8,128)(2,1)} %param.13) | copy-start | bytes 5898244
  79.4 7.5 %collective-permute-start.5 = (bf16[128,768]{1,0:T(8,128)(2,1)S(1)}, bf16[128,768]{1,0:T(8,128)(2,1)S(1)}, u32[]{:S(2)}, u32[]{:S(2)}) collective-permute-start(bf16[128,768]{1,0:T(8,128)(2,1)S(1)} %shard_map.108.refs_0_), channel_id=1, source_target_pairs={{0,1},{1,0},{2,3},{3,2},{4,5},{5,4},{6,7},{7,6},{8,9},{9,8},{10,11... | collective-permute-start | bytes 589832 | tf_op jit(solution)/shard_map/ppermute | solution.py:113
  83.9 4.1 %collective-permute-start.8 = (bf16[128,768]{1,0:T(8,128)(2,1)S(1)}, bf16[128,768]{1,0:T(8,128)(2,1)S(1)}, u32[]{:S(2)}, u32[]{:S(2)}) collective-permute-start(bf16[128,768]{1,0:T(8,128)(2,1)S(1)} %shard_map.110.refs_2_), channel_id=1, source_target_pairs={{0,1},{1,0},{2,3},{3,2},{4,5},{5,4},{6,7},{7,6},{8,9},{9,8},{10,11... | collective-permute-start | bytes 589832 | tf_op jit(solution)/shard_map/ppermute | solution.py:113
  90.3 6.6 %copy-start.3 = (bf16[1280,768]{1,0:T(8,128)(2,1)S(1)}, bf16[1280,768]{1,0:T(8,128)(2,1)}, u32[]{:S(2)}) copy-start(bf16[1280,768]{1,0:T(8,128)(2,1)} %refs_2_.1) | copy-start | bytes 5898244
  90.3 39.8 %all-to-all-start.1 = ((bf16[64,8,1280]{2,1,0:T(8,128)(2,1)}), bf16[64,8,1280]{2,1,0:T(8,128)(2,1)S(1)}, u32[]{:S(2)}, u32[]{:S(2)}) async-start(bf16[64,8,1280]{2,1,0:T(8,128)(2,1)} %bitcast.8), calls=%async_computation.1 | async-start | bytes 2621440 | tf_op jit(solution)/shard_map/all_to_all | solution.py:172
  130.1 1.0 copy-start.8

commit v3 on v0

v3 whole, which is shorter than its diff:
```python
import functools

import jax
import jax.numpy as jnp
from jax import lax
from jax.experimental import pallas as pl
from jax.experimental.pallas import tpu as pltpu
from jax.sharding import PartitionSpec as P

TOP = 6
CAP = 8
CORES = 2
HELD = CAP // CORES
CORE_SWAP = [(0, 1), (1, 0), (2, 3), (3, 2)]
CHIP_SWAP = [(0, 2), (1, 3), (2, 0), (3, 1)]
F32, BF16 = jnp.float32, jnp.bfloat16
WHOLE = pl.BlockSpec(memory_space=pltpu.VMEM)
FAR = pl.BlockSpec(memory_space=pltpu.HBM)
SCALAR = pl.BlockSpec(memory_space=pltpu.SMEM)


def dot(a, b, dims=((1,), (1,))):
    return lax.dot_general(a, b, (dims, ((), ())), preferred_element_type=F32)


def call(body, outs, specs, scratch=(), flops=0, moved=0):
    return pl.pallas_call(
        body,
        out_shape=outs,
        in_specs=specs,
        out_specs=jax.tree.map(lambda _: WHOLE, outs),
        scratch_shapes=list(scratch),
        compiler_params=pltpu.CompilerParams(vmem_limit_bytes=12 << 20),
        cost_estimate=pl.CostEstimate(flops=flops, bytes_accessed=moved, transcendentals=0),
    )


def low_rows(shape):
    return lax.broadcasted_iota(jnp.int32, shape, len(shape) - 2) < HELD


def route_body(ids_in, prob_in, grad_in, sent_ref, ids_ref, prob_ref, grad_ref, sems, *, experts):
    tokens, quarter = grad_ref.shape
    loads = [
        pltpu.make_async_copy(source, target, sems.at[index])
        for index, (source, target) in enumerate(
            ((ids_in, ids_ref), (prob_in, prob_ref), (grad_in, grad_ref))
        )
    ]
    for load in loads:
        load.start()
    loads[0].wait()
    loads[1].wait()
    expert = lax.broadcasted_iota(jnp.int32, (experts, tokens), 0)
    named = jnp.zeros((experts, tokens), F32)
    prob = jnp.zeros((experts, tokens), F32)
    for pick in range(TOP):
        hit = ids_ref[pick : pick + 1, :] == expert
        named = jnp.where(hit, 1.0, named)
        prob = jnp.where(hit, prob_ref[pick : pick + 1, :], prob)
    square = (tokens, tokens)
    earlier = lax.broadcasted_iota(jnp.int32, square, 0) < lax.broadcasted_iota(jnp.int32, square, 1)
    rank = dot(named.astype(BF16), jnp.where(earlier, 1.0, 0.0).astype(BF16), ((1,), (0,)))
    rank = jnp.where(named > 0.0, rank, float(CAP))
    shape = (experts, CAP, tokens)
    rank = jnp.broadcast_to(rank[:, None, :], shape)
    prob = jnp.broadcast_to(prob[:, None, :], shape)
    slot = lax.rem(lax.broadcasted_iota(jnp.int32, shape, 1), HELD).astype(F32)
    rows, half = experts * CAP, quarter // 2
    loads[2].wait()
    for core in range(CORES):
        hit = rank == slot + float(core * HELD)
        scale = jnp.sum(jnp.where(hit, prob, 0.0), axis=2, keepdims=True)
        mask = jnp.where(hit, 1.0, 0.0).reshape(rows, tokens).astype(BF16)
        left = dot(mask, grad_ref[:, :half], ((1,), (0,))).reshape(experts, CAP, half)
        right = dot(mask, grad_ref[:, half:], ((1,), (0,))).reshape(experts, CAP, half)
        picked = jnp.where(low_rows(left.shape), left, right)
        sent_ref[core] = (picked * scale).astype(BF16)


def mask_body(ids_ref, mask_ref, *, experts):
    tokens = ids_ref.shape[0]
    expert = lax.broadcasted_iota(jnp.int32, (tokens, experts), 1)
    named = jnp.zeros((tokens, experts), F32)
    for pick in range(TOP):
        named = jnp.where(ids_ref[:, pick : pick + 1] == expert, 1.0, named)
    square = (tokens, tokens)
    earlier = lax.broadcasted_iota(jnp.int32, square, 1) < lax.broadcasted_iota(jnp.int32, square, 0)
    rank = dot(jnp.where(earlier, 1.0, 0.0).astype(BF16), named.astype(BF16), ((1,), (0,)))
    rank = jnp.where(named > 0.0, rank, float(CAP)).astype(BF16)
    rows = experts * CAP
    spread = lax.broadcasted_iota(jnp.int32, (experts, rows), 0)
    spread = spread == lax.broadcasted_iota(jnp.int32, (experts, rows), 1) // CAP
    rank = dot(rank, jnp.where(spread, 1.0, 0.0).astype(BF16), ((1,), (0,)))
    slot = lax.rem(lax.broadcasted_iota(jnp.int32, (tokens, rows), 1), HELD).astype(F32)
    for core in range(CORES):
        hit = rank == slot + float(core * HELD)
        mask_ref[:, core * rows : (core + 1) * rows] = jnp.where(hit, 1.0, 0.0).astype(BF16)


def hidden_body(core_ref, rows_ref, mine_ref, other_ref, keep_ref, send_ref):
    total = None
    for lane, w_ref in ((core_ref[0], mine_ref), (1 - core_ref[0], other_ref)):
        rows = rows_ref[lane].astype(F32)
        half = rows.shape[-1]
        pairs = rows.reshape(rows.shape[0] // 2, 2, CAP, half)
        even, odd = pairs[:, 0], pairs[:, 1]
        low = low_rows(even.shape)
        left = jnp.where(low, even, pltpu.roll(odd, HELD, 1))
        right = jnp.where(low, pltpu.roll(even, HELD, 1), odd)
        for column, part in enumerate((left, right)):
            part = part.reshape(-1, half).astype(BF16)
            term = dot(part, w_ref[:, column * half : (column + 1) * half])
            total = term if total is None else total + term
    keep_ref[...] = total
    send_ref[...] = total.astype(BF16)


def slot_grad_body(core_ref, keep_ref, away_ref, gate_ref, mine_ref, other_ref, out_ref):
    hidden = keep_ref[...] + away_ref[...].astype(F32)
    up = (hidden * gate_ref[...].astype(F32)).astype(BF16)
    half = out_ref.shape[-1]
    for lane, w_ref in ((core_ref[0], mine_ref), (1 - core_ref[0], other_ref)):
        left = dot(up, w_ref[:half, :]).reshape(-1, CAP, half)
        right = dot(up, w_ref[half:, :]).reshape(-1, CAP, half)
        low = low_rows(left.shape)
        out_ref[lane, :, 0] = jnp.where(low, left, pltpu.roll(right, HELD, 1)).astype(BF16)
        out_ref[lane, :, 1] = jnp.where(low, pltpu.roll(left, HELD, 1), right).astype(BF16)


def combine_body(mask_in, back_ref, out_ref, mask_ref, sem):
    load = pltpu.make_async_copy(mask_in, mask_ref, sem)
    load.start()
    load.wait()
    half = back_ref.shape[1]
    mask = mask_ref[...]
    low = lax.rem(lax.broadcasted_iota(jnp.int32, mask.shape, 1), CAP) < HELD
    none = jnp.zeros_like(mask)
    left = jnp.where(low, mask, none)
    right = jnp.where(low, none, mask)
    out_ref[:, :half] = dot(left, back_ref[...], ((1,), (0,))).astype(BF16)
    out_ref[:, half:] = dot(right, back_ref[...], ((1,), (0,))).astype(BF16)


def dense_part_body(core_ref, rows_ref, w_ref, mine_ref, other_ref, full_ref):
    half = mine_ref.shape[0]
    full_ref[...] = dot(rows_ref[...], w_ref[...])
    mine_ref[...] = full_ref[pl.ds(pl.multiple_of(core_ref[0] * half, 16), half), :]
    other_ref[...] = full_ref[pl.ds(pl.multiple_of((1 - core_ref[0]) * half, 16), half), :]


def dense_gate_body(core_ref, mine_ref, pair_ref, away_ref, gate_ref, up_ref):
    half = up_ref.shape[0]
    gate = gate_ref[pl.ds(pl.multiple_of(core_ref[0] * half, 16), half), :].astype(F32)
    hidden = mine_ref[...] + pair_ref[...] + away_ref[...].astype(F32)
    up_ref[...] = (hidden * gate).astype(BF16)


def dense_out_body(core_ref, mine_ref, other_ref, w_ref, out_ref):
    half = mine_ref.shape[0]
    grad = dot(jnp.concatenate([mine_ref[...], other_ref[...]], axis=0), w_ref[...]).astype(BF16)
    out_ref[pl.ds(pl.multiple_of(core_ref[0] * half, 16), half), :] = grad[:half]
    out_ref[pl.ds(pl.multiple_of((1 - core_ref[0]) * half, 16), half), :] = grad[half:]


def dense_up_grad(core, grad_out, shared_down, shared_gate):
    tokens, depth = grad_out.shape
    width = shared_down.shape[0]
    half = jax.ShapeDtypeStruct((tokens // 2, width), F32)
    mine, other = call(
        dense_part_body,
        (half, half),
        [SCALAR, WHOLE, WHOLE],
        [pltpu.VMEM((tokens, width), F32)],
        flops=2 * tokens * width * depth,
        moved=2 * width * depth,
    )(core, grad_out, shared_down)
    pair = lax.ppermute(other, "tensor", CORE_SWAP)
    away = lax.ppermute((mine + pair).astype(BF16), "tensor", CHIP_SWAP)
    up = call(
        dense_gate_body,
        jax.ShapeDtypeStruct((tokens // 2, width), BF16),
        [SCALAR] + [WHOLE] * 4,
        flops=3 * tokens * width,
        moved=7 * tokens * width,
    )(core, mine, pair, away, shared_gate)
    return up, lax.ppermute(up, "tensor", CORE_SWAP)


def on_device(
    grad_out, expert_ids, route_probs, saved_gate, w_up, w_down, shared_gate, shared_up, shared_down
):
    experts = lax.axis_size("expert")
    tokens, quarter = grad_out.shape
    half, slots, held = quarter // 2, experts * CAP, experts * HELD
    core = (lax.axis_index("tensor") & 1).reshape(1)
    groups = [
        [place * 4 + chip * 2 + lane for lane in range(CORES) for place in range(experts)]
        for chip in range(2)
    ]

    def exchange(rows):
        rows = rows.reshape(CORES * experts, CAP, half)
        return lax.all_to_all(
            rows, ("expert", "tensor"), 0, 0, axis_index_groups=groups, tiled=True
        )

    ids, probs = expert_ids.T, route_probs.T
    sent = call(
        functools.partial(route_body, experts=experts),
        pltpu.VMEM((CORES, experts, CAP, half), BF16),
        [FAR] * 3,
        [pltpu.VMEM(array.shape, array.dtype) for array in (ids, probs, grad_out)]
        + [pltpu.SemaphoreType.DMA((3,))],
        flops=4 * slots * tokens * quarter,
        moved=4 * slots * quarter,
    )(*(pltpu.with_memory_space_constraint(array, pltpu.HBM) for array in (ids, probs, grad_out)))
    arrived = exchange(sent)

    down_other = lax.ppermute(w_down[0], "tensor", CORE_SWAP)
    up_other = lax.ppermute(w_up[0], "tensor", CORE_SWAP)
    gate = saved_gate.reshape(experts, CORES, HELD, -1)
    gate = lax.dynamic_index_in_dim(gate, core[0], 1, keepdims=False).reshape(held, -1)
    dense_up = dense_up_grad(core, grad_out, shared_down, shared_gate)
    shared_grad = call(
        dense_out_body,
        jax.ShapeDtypeStruct((tokens, quarter), BF16),
        [SCALAR] + [WHOLE] * 3,
        flops=2 * tokens * quarter * shared_up.shape[1],
        moved=2 * quarter * shared_up.shape[1],
    )(core, *dense_up, shared_up)
    mask = call(
        functools.partial(mask_body, experts=experts),
        jax.ShapeDtypeStruct((tokens, CORES * slots), BF16),
        [WHOLE],
        flops=2 * tokens * slots * experts,
        moved=4 * tokens * slots,
    )(expert_ids)
    arrived, down_other, up_other, gate, shared_grad, mask = lax.optimization_barrier(
        (arrived, down_other, up_other, gate, shared_grad, mask)
    )
    work = 4 * held * quarter * gate.shape[1]
    keep, send = call(
        hidden_body,
        (jax.ShapeDtypeStruct(gate.shape, F32), jax.ShapeDtypeStruct(gate.shape, BF16)),
        [SCALAR] + [WHOLE] * 3,
        flops=work,
        moved=4 * quarter * gate.shape[1],
    )(core, arrived.reshape(CORES, experts, CAP, half), w_down[0], down_other)
    away = lax.ppermute(send, "tensor", CHIP_SWAP)
    slot_grad = call(
        slot_grad_body,
        pltpu.VMEM((CORES, experts // 2, 2, CAP, half), BF16),
        [SCALAR] + [WHOLE] * 5,
        flops=work,
        moved=4 * quarter * gate.shape[1],
    )(core, keep, away, gate, w_up[0], up_other)
    back = exchange(slot_grad)
    moe_grad = call(
        combine_body,
        jax.ShapeDtypeStruct((tokens, quarter), BF16),
        [FAR, WHOLE],
        [pltpu.VMEM(mask.shape, BF16), pltpu.SemaphoreType.DMA(())],
        flops=4 * slots * tokens * quarter,
        moved=2 * slots * quarter,
    )(pltpu.with_memory_space_constraint(mask, pltpu.HBM), back.reshape(CORES * slots, half))
    return (moe_grad, shared_grad)


def solution(mesh):
    placed = (
        P(("dp", "expert"), "tensor"),
        P(("dp", "expert"), None),
        P(("dp", "expert"), None),
        P("dp", "expert", None, None),
        P("expert", "tensor", None),
        P("expert", None, "tensor"),
        P(("dp", "expert"), None),
        P("tensor", None),
        P(None, "tensor"),
    )
    return jax.shard_map(
        on_device,
        mesh=mesh,
        in_specs=placed,
        out_specs=(P(("dp", "expert"), "tensor"), P(("dp", "expert"), "tensor")),
        check_vma=False,
    )
```

time: 223 us -> 135 us (0.61)
  waiting for transfers between devices: 130 us -> 13.4 us
  blocking collectives: 0 us -> 48 us
  other arithmetic: 18.9 us -> 0.68 us
  Pallas kernels: 0 us -> 17.9 us
  matrix products: 17.4 us -> 0 us
  between operations: 14.2 us -> 0.79 us
  local copies, waits for them, and re-layouts: 1.76 us -> 12.2 us
  starting transfers between devices: 38 us -> 41.7 us
    psum x1 -> x0, waiting for transfers between devices: 70.8 us -> none  [on_device(): hidden = lax.psum(partial_hidden, 'tensor')]
    all_to_all x2 -> x1, waiting for transfers between devices: 59.7 us -> 3.49 us  [exchange(): lax.all_to_all(rows, ('expert', 'tensor'), 0, 0, axis_index_groups=groups...]
    all_to_all x0 -> x1, blocking collectives: none -> 48 us  [exchange(): lax.all_to_all(rows, ('expert', 'tensor'), 0, 0, axis_index_groups=groups...]
    another operation x3 -> x0, other arithmetic: 18.2 us -> none
    pallas_call x0 -> x8, Pallas kernels: none -> 17.9 us  [the longest x1 3.71 us: on_device(): call(hidden_body, (jax.ShapeDtypeStruct(gate.shape, F32), jax.ShapeDtypeS...]
    dot_general x6 -> x0, matrix products: 17.4 us -> none  [the longest x1 4.31 us: on_device(): lax.dot_general(arrived, w_down[0], (((1,), (1,)), ((), ())), preferred_e...]
    ppermute x0 -> x6, starting transfers between devices: none -> 16.1 us  [the longest x1 3.12 us: on_device(): away = lax.ppermute(send, 'tensor', CHIP_SWAP)]
    all_to_all x2 -> x1, starting transfers between devices: 38 us -> 25.6 us  [exchange(): lax.all_to_all(rows, ('expert', 'tensor'), 0, 0, axis_index_groups=groups...]
  transfers between devices with their start and end apart: 3 -> 7, of which waited for: 3 -> 4; matrix products, arithmetic and copies ran while one was open for 3% -> 6% of each run, Pallas kernels for 0% -> 4%
where the time goes in v3:
time: 135 us
  blocking collectives  48 us (36%)
  starting transfers between devices  41.7 us (31%)
  Pallas kernels  17.9 us (13%)
  waiting for transfers between devices  13.4 us (10%)
  local copies, waits for them, and re-layouts  12.2 us (9%)
    all_to_all x1, blocking collectives, exchange(): lax.all_to_all(rows, ('expert', 'tensor'), 0, 0, axis_index_groups=groups...  48 us
    all_to_all x1, starting transfers between devices, exchange(): lax.all_to_all(rows, ('expert', 'tensor'), 0, 0, axis_index_groups=groups...  25.6 us
    ppermute x1, waiting for transfers between devices, on_device(): away = lax.ppermute(send, 'tensor', CHIP_SWAP)  8.42 us
    unnamed x24, local copies, waits for them, and re-layouts  7.85 us
    pallas_call x1, Pallas kernels, on_device(): call(hidden_body, (jax.ShapeDtypeStruct(gate.shape, F32), jax.ShapeDtypeS...  3.71 us
    all_to_all x1, waiting for transfers between devices, exchange(): lax.all_to_all(rows, ('expert', 'tensor'), 0, 0, axis_index_groups=groups...  3.49 us
    pallas_call x1, Pallas kernels, on_device(): call(functools.partial(route_body, experts=experts), pltpu.VMEM((CORES, e...  3.3 us
    ppermute x1, starting transfers between devices, on_device(): away = lax.ppermute(send, 'tensor', CHIP_SWAP)  3.12 us
  transfers between devices with their start and end apart: 7, of which 4 were waited for; matrix products, arithmetic and copies ran while one was open for 6% of the time, Pallas kernels for 4%

profile of v3, /device:TPU:1, one launch (start us, length us, event | category | flops | bytes accessed | tf_op | source)
XLA Modules:
  0.0 134.7 jit_solution(11256758781036809278)
XLA Ops:
  0.6 3.3 %shard_map.104 = bf16[2,64,8,640]{3,2,1,0:T(8,128)(2,1)} custom-call(s32[6,160]{1,0:T(8,128)} %bitcast.20, f32[6,160]{1,0:T(8,128)} %bitcast.21, bf16[160,1280]{1,0:T(8,128)(2,1)} %rows_ref.1), custom_call_target="tpu_custom_call" | custom-call | flops 419430400 | bytes 2621440 | tf_op jit(solution)/shard_map/pallas_call | solution.py:209
  4.0 25.6 %all-to-all-start = ((bf16[128,8,640]{2,1,0:T(8,128)(2,1)}), bf16[128,8,640]{2,1,0:T(8,128)(2,1)S(1)}, u32[]{:S(2)}, u32[]{:S(2)}) async-start(bf16[128,8,640]{2,1,0:T(8,128)(2,1)} %bitcast.2), calls=%async_computation | async-start | bytes 2621440 | tf_op jit(solution)/shard_map/all_to_all | solution.py:204
  29.5 0.0 copy-start.10
  29.5 2.5 %collective-permute-start.1 = (bf16[1280,768]{1,0:T(8,128)(2,1)}, bf16[1280,768]{1,0:T(8,128)(2,1)}, u32[]{:S(2)}, u32[]{:S(2)}) collective-permute-start(bf16[1280,768]{1,0:T(8,128)(2,1)} %bitcast.18), channel_id=1, source_target_pairs={{0,1},{1,0},{2,3},{3,2},{4,5},{5,4},{6,7},{7,6},{8,9},{9,8},{10,11... | collective-permute-start | bytes 5898248 | tf_op jit(solution)/shard_map/ppermute | solution.py:221
  32.0 1.9 %collective-permute-start = (bf16[768,1280]{1,0:T(8,128)(2,1)}, bf16[768,1280]{1,0:T(8,128)(2,1)}, u32[]{:S(2)}, u32[]{:S(2)}) collective-permute-start(bf16[768,1280]{1,0:T(8,128)(2,1)} %bitcast.3.mine_ref), channel_id=1, source_target_pairs={{0,1},{1,0},{2,3},{3,2},{4,5},{5,4},{6,7},{7,6},{8,9},{9,8},{10,11... | collective-permute-start | bytes 5898248 | tf_op jit(solution)/shard_map/ppermute | solution.py:220
  34.0 1.0 copy-done.3
  35.0 0.8 shard_map.105
  35.8 2.4 %collective-permute-start.2 = (f32[80,768]{1,0:T(8,128)S(1)}, f32[80,768]{1,0:T(8,128)S(1)}, u32[]{:S(2)}, u32[]{:S(2)}) collective-permute-start(f32[80,768]{1,0:T(8,128)S(1)} %get-tuple-element.13), channel_id=1, source_target_pairs={{0,1},{1,0},{2,3},{3,2},{4,5},{5,4},{6,7},{7,6},{8,9},{9,8},{10,11... | collective-permute-start | bytes 737288 | tf_op jit(solution)/shard_map/ppermute | solution.py:178
  38.2 1.1 collective-permute-done.2.pair_ref
  39.4 0.7 add_convert_fusion
  40.0 0.7 copy-done.6
  40.7 3.1 %collective-permute-start.3 = (bf16[80,768]{1,0:T(8,128)(2,1)}, bf16[80,768]{1,0:T(8,128)(2,1)}, u32[]{:S(2)}, u32[]{:S(2)}) collective-permute-start(bf16[80,768]{1,0:T(8,128)(2,1)} %add_convert_fusion), channel_id=1, source_target_pairs={{0,2},{1,3},{2,0},{3,1},{4,6},{5,7},{6,4},{7,5},{8,10},{9,11},{10,... | collective-permute-start | bytes 368648 | tf_op jit(solution)/shard_map/ppermute | solution.py:179
  43.9 0.7 copy.12.ids_ref
  44.6 2.5 %reshape.27 = bf16[64,2,4,768]{3,2,1,0:T(4,128)(2,1)} reshape(bf16[1,1,512,768]{3,2,1,0:T(8,128)(2,1)} %param.12) | data formatting | bytes 1572864 | tf_op jit(solution)/shard_map/reshape | solution.py:222
  47.1 0.3 collective-permute-done.3.away_ref
  47.5 0.9 copy-done.7
  48.4 0.9 copy-done.9
  49.4 1.6 %shard_map.106.mine_ref = bf16[80,768]{1,0:T(8,128)(2,1)} custom-call(s32[1]{0:T(128)} %bitcast.5.core_ref, f32[80,768]{1,0:T(8,128)S(1)} %get-tuple-element.12.mine_ref, f32[80,768]{1,0:T(8,128)S(1)} %copy-done.7, bf16[80,768]{1,0:T(8,128)(2,1)} %collective-permute-done.3.away_ref, bf16[160,768]{1,0:T(8,128)(2,1)S(1)} %copy-done.9), custom_call_target="tpu_custom_call" | custom-call | flops 368640 | bytes 860160 | tf_op jit(solution)/shard_map/pallas_call | solution.py:180
  51.0 3.1 %collective-permute-start.4 = (bf16[80,768]{1,0:T(8,128)(2,1)}, bf16[80,768]{1,0:T(8,128)(2,1)S(1)}, u32[]{:S(2)}, u32[]{:S(2)}) collective-permute-start(bf16[80,768]{1,0:T(8,128)(2,1)} %shard_map.106.mine_ref), channel_id=1, source_target_pairs={{0,1},{1,0},{2,3},{3,2},{4,5},{5,4},{6,7},{7,6},{8,9},{9,8},{10,11... | collective-permute-start | bytes 368648 | tf_op jit(solution)/shard_map/ppermute | solution.py:187
  54.1 1.9 %dynamic-slice_bitcast_fusion = bf16[64,1,4,768]{3,2,0,1:T(4,128)(2,1)} fusion(bf16[64,2,4,768]{3,2,1,0:T(4,128)(2,1)} %reshape.27, s32[]{:T(128)S(6)} %select_n.4), kind=kLoop, calls=%fused_computation | loop fusion | bytes 786436
  55.9 1.8 %reshape.28.gate_ref = bf16[256,768]{1,0:T(8,128)(2,1)} reshape(bf16[64,1,4,768]{3,2,0,1:T(4,128)(2,1)} %dynamic-slice_bitcast_fusion) | data formatting | bytes 786432 | tf_op jit(solution)/shard_map/reshape | solution.py:223
  57.8 0.9 copy-done.8
  58.7 0.6 shard_map.108.mask_in
  59.3 0.7 copy-done.5
  60.0 2.5 %shard_map.107 = bf16[160,1280]{1,0:T(8,128)(2,1)} custom-call(s32[1]{0:T(128)} %bitcast.5.core_ref, bf16[80,768]{1,0:T(8,128)(2,1)} %shard_map.106.mine_ref, bf16[80,768]{1,0:T(8,128)(2,1)S(1)} %collective-permute-done.4.other_ref, bf16[1280,768]{1,0:T(8,128)(2,1)S(1)} %copy-done), custom_call_target="tpu_custom_call" | custom-call | flops 314572800 | bytes 1966080 | tf_op jit(solution)/shard_map/pallas_call | solution.py:225
  62.5 3.5 %all-to-all-done = bf16[128,8,640]{2,1,0:T(8,128)(2,1)S(1)} async-done(((bf16[128,8,640]{2,1,0:T(8,128)(2,1)}), bf16[128,8,640]{2,1,0:T(8,128)(2,1)S(1)}, u32[]{:S(2)}, u32[]{:S(2)}) %all-to-all-start) | async-done | bytes 1310752 | tf_op jit(solution)/shard_map/all_to_all | solution.py:204
  66.0 3.7 %shard_map.109 = (f32[256,768]{1,0:T(8,128)S(1)}, bf16[256,768]{1,0:T(8,128)(2,1)S(1)}) custom-call(s32[1]{0:T(128)} %bitcast.5.core_ref, bf16[2,64,8,640]{3,2,1,0:T(8,128)(2,1)S(1)} %bitcast.16, bf16[768,1280]{1,0:T(8,128)(2,1)} %bitcast.3.mine_ref, bf16[768,1280]{1,0:T(8,128)(2,1)} %collective-permute-done.other_ref), custom_call_target="tpu_custom_call" | custom-call | flops 1006632960 | bytes 3932160 | tf_op jit(solution)/shard_map/pallas_call | solution.py:243
  69.7 3.1 %collective-permute-start.5 = (bf16[256,768]{1,0:T(8,128)(2,1)S(1)}, bf16[256,768]{1,0:T(8,128)(2,1)S(1)}, u32[]{:S(2)}, u32[]{:S(2)}) collective-permute-start(bf16[256,768]{1,0:T(8,128)(2,1)S(1)} %get-tuple-element.18), channel_id=1, source_target_pairs={{0,2},{1,3},{2,0},{3,1},{4,6},{5,7},{6,4},{7,5},{8,10},{9,11},{10,... | collective-permute-start | bytes 1179656 | tf_op jit(solution)/shard_map/ppermute | solution.py:250
  72.8 8.4 %collective-permute-done.5.away_ref = bf16[256,768]{1,0:T(8,128)(2,1)S(1)} collective-permute-done((bf16[256,768]{1,0:T(8,128)(2,1)S(1)}, bf16[256,768]{1,0:T(8,128)(2,1)S(1)}, u32[]{:S(2)}, u32[]{:S(2)}) %collective-permute-start.5) | collective-permute-done | bytes 393248 | tf_op jit(solution)/shard_map/ppermute | solution.py:250
  81.3 3.0 %shard_map.110 = bf16[2,32,2,8,640]{4,3,2,1,0:T(8,128)(2,1)S(1)} custom-call(s32[1]{0:T(128)} %bitcast.5.core_ref, f32[256,768]{1,0:T(8,128)S(1)} %get-tuple-element.17.keep_ref, bf16[256,768]{1,0:T(8,128)(2,1)S(1)} %collective-permute-done.5.away_ref, bf16[256,768]{1,0:T(8,128)(2,1)S(1)} %copy-done.4, bf16[1280,768]{1,0:T(8,128)(2,1)S(1)} %bitcast.19, ...), custom_call_target="tpu_custom_call" | custom-call | flops 1006632960 | bytes 3932160 | tf_op jit(solution)/shard_map/pallas_call | solution.py:251
  84.2 48.0 %all_to_all.10 = bf16[128,8,640]{2,1,0:T(8,128)(2,1)S(1)} all-to-all(bf16[128,8,640]{2,1,0:T(8,128)(2,1)S(1)} %bitcast.17), channel_id=1, replica_groups={{0,4,8,12,16,20,24,28,32,36,40,44,48,52,56,60,64,68,72,76,80,84,88,92,9..., dimensions={0} | all-to-all | bytes 2621440 | tf_op jit(solution)/shard_map/all_to_all | solution.py:204
  132.2 2.4 %shard_map.111 = bf16[160,1280]{1,0:T(8,128)(2,1)} custom-call(bf16[160,1024]{1,0:T(8,128)(2,1)} %copy-done.5, bf16[1024,640]{1,0:T(8,128)(2,1)S(1)} %bitcast.15), custom_call_target="tpu_custom_call" | custom-call | flops 419430400 | bytes 1310720 | tf_op jit(solution)/shard_map/pallas_call | solution.py:259
  (18 shorter events, 0.0 us)
Async XLA Ops:
  0.6 33.3 %copy-start.1 = (bf16[768,1280]{1,0:T(8,128)(2,1)S(1)}, bf16[768,1280]{1,0:T(8,128)(2,1)}, u32[]{:S(2)}) copy-start(bf16[768,1280]{1,0:T(8,128)(2,1)} %w_ref.2) | copy-start | bytes 5898244
  4.0 62.0 %all-to-all-start = ((bf16[128,8,640]{2,1,0:T(8,128)(2,1)}), bf16[128,8,640]{2,1,0:T(8,128)(2,1)S(1)}, u32[]{:S(2)}, u32[]{:S(2)}) async-start(bf16[128,8,640]{2,1,0:T(8,128)(2,1)} %bitcast.2), calls=%async_computation | async-start | bytes 2621440 | tf_op jit(solution)/shard_map/all_to_all | solution.py:204
  29.5 14.3 %copy-start.10 = (s32[160,6]{0,1:T(8,128)S(1)}, s32[160,6]{0,1:T(8,128)}, u32[]{:S(2)}) copy-start(s32[160,6]{0,1:T(8,128)} %param.10) | copy-start | bytes 11524
  29.5 32.9 %collective-permute-start.1 = (bf16[1280,768]{1,0:T(8,128)(2,1)}, bf16[1280,768]{1,0:T(8,128)(2,1)}, u32[]{:S(2)}, u32[]{:S(2)}) collective-permute-start(bf16[1280,768]{1,0:T(8,128)(2,1)} %bitcast.18), channel_id=1, source_target_pairs={{0,1},{1,0},{2,3},{3,2},{4,5},{5,4},{6,7},{7,6},{8,9},{9,8},{10,11... | collective-permute-start | bytes 5898248 | tf_op jit(solution)/shard_map/ppermute | solution.py:221
  32.0 30.5 %collective-permute-start = (bf16[768,1280]{1,0:T(8,128)(2,1)}, bf16[768,1280]{1,0:T(8,128)(2,1)}, u32[]{:S(2)}, u32[]{:S(2)}) collective-permute-start(bf16[768,1280]{1,0:T(8,128)(2,1)} %bitcast.3.mine_ref), channel_id=1, source_target_pairs={{0,1},{1,0},{2,3},{3,2},{4,5},{5,4},{6,7},{7,6},{8,9},{9,8},{10,11... | collective-permute-start | bytes 5898248 | tf_op jit(solution)/shard_map/ppermute | solution.py:220
  34.0 1.0 copy-start.3
  35.8 3.5 %collective-permute-start.2 = (f32[80,768]{1,0:T(8,128)S(1)}, f32[80,768]{1,0:T(8,128)S(1)}, u32[]{:S(2)}, u32[]{:S(2)}) collective-permute-start(f32[80,768]{1,0:T(8,128)S(1)} %get-tuple-element.13), channel_id=1, source_target_pairs={{0,1},{1,0},{2,3},{3,2},{4,5},{5,4},{6,7},{7,6},{8,9},{9,8},{10,11... | collective-permute-start | bytes 737288 | tf_op jit(solution)/shard_map/ppermute | solution.py:178
  40.0 0.7 copy-start.6
  40.7 6.7 %collective-permute-start.3 = (bf16[80,768]{1,0:T(8,128)(2,1)}, bf16[80,768]{1,0:T(8,128)(2,1)}, u32[]{:S(2)}, u32[]{:S(2)}) collective-permute-start(bf16[80,768]{1,0:T(8,128)(2,1)} %add_convert_fusion), channel_id=1, source_target_pairs={{0,2},{1,3},{2,0},{3,1},{4,6},{5,7},{6,4},{7,5},{8,10},{9,11},{10,... | collective-permute-start | bytes 368648 | tf_op jit(solution)/shard_map/ppermute | solution.py:179
  44.6 15.4 %copy-start = (bf16[1280,768]{1,0:T(8,128)(2,1)S(1)}, bf16[1280,768]{1,0:T(8,128)(2,1)}, u32[]{:S(2)}) copy-start(bf16[1280,768]{1,0:T(8,128)(2,1)} %w_ref.3) | copy-start | bytes 5898244
  47.5 0.9 copy-start.7
  48.4 0.9 copy-start.9
  51.0 9.0 %collective-permute-start.4 = (bf16[80,768]{1,0:T(8,128)(2,1)}, bf16[80,768]{1,0:T(8,128)(2,1)S(1)}, u32[]{:S(2)}, u32[]{:S(2)}) collective-permute-start(bf16[80,768]{1,0:T(8,128)(2,1)} %shard_map.106.mine_ref), channel_id=1, source_target_pairs={{0,1},{1,0},{2,3},{3,2},{4,5},{5,4},{6,7},{7,6},{8,9},{9,8},{10,11... | collective-permute-start | bytes 368648 | tf_op jit(solution)/shard_map/ppermute | solution.py:187
  57.8 0.9 copy-start.8
  59.3 0.7 copy-start.5
  66.0 15.3 %copy-start.2 = (bf16[1,1280,768]{2,1,0:T(8,128)(2,1)S(1)}, bf16[1,1280,768]{2,1,0:T(8,128)(2,1)}, u32[]{:S(2)}) copy-start(bf16[1,1280,768]{2,1,0:T(8,128)(2,1)} %param.13) | copy-start | bytes 5898244
  66.0 15.3 %copy-start.4 = (bf16[256,768]{1,0:T(8,128)(2,1)S(1)}, bf16[256,768]{1,0:T(8,128)(2,1)}, u32[]{:S(2)}) copy-start(bf16[256,768]{1,0:T(8,128)(2,1)} %reshape.28.gate_ref) | copy-start | bytes 1179652
  69.7 11.5 %collective-permute-start.5 = (bf16[256,768]{1,0:T(8,128)(2,1)S(1)}, bf16[256,768]{1,0:T(8,128)(2,1)S(1)}, u32[]{:S(2)}, u32[]{:S(2)}) collective-permute-start(bf16[256,768]{1,0:T(8,128)(2,1)S(1)} %get-tuple-element.18), channel_id=1, source_target_pairs={{0,2},{1,3},{2,0},{3,1},{4,6},{5,7},{6,4},{7,5},{8,10},{9,11},{10,... | collective-permute-start | bytes 1179656 | tf_op jit(solution)/shard_map/ppermute | solution.py:250

commit v4 on v3

--- a/solution.py
+++ b/solution.py
@@ -16,6 +16,7 @@
 F32, BF16 = jnp.float32, jnp.bfloat16
 WHOLE = pl.BlockSpec(memory_space=pltpu.VMEM)
 FAR = pl.BlockSpec(memory_space=pltpu.HBM)
+ANY = pl.BlockSpec(memory_space=pl.ANY)
 SCALAR = pl.BlockSpec(memory_space=pltpu.SMEM)
 
 
@@ -35,8 +36,19 @@
     )
 
 
+def far(*arrays):
+    return tuple(pltpu.with_memory_space_constraint(array, pltpu.HBM) for array in arrays)
+
+
 def low_rows(shape):
     return lax.broadcasted_iota(jnp.int32, shape, len(shape) - 2) < HELD
+
+
+def pack(even, odd, side):
+    low = low_rows(even.shape)
+    if side == 0:
+        return jnp.where(low, even, pltpu.roll(odd, HELD, 1))
+    return jnp.where(low, pltpu.roll(even, HELD, 1), odd)
 
 
 def route_body(ids_in, prob_in, grad_in, sent_ref, ids_ref, prob_ref, grad_ref, sems, *, experts):
@@ -51,7 +63,9 @@
         load.start()
     loads[0].wait()
     loads[1].wait()
-    expert = lax.broadcasted_iota(jnp.int32, (experts, tokens), 0)
+    pairs, half = experts // 2, quarter // 2
+    row = lax.broadcasted_iota(jnp.int32, (experts, tokens), 0)
+    expert = jnp.where(row < pairs, 2 * row, 2 * (row - pairs) + 1)
     named = jnp.zeros((experts, tokens), F32)
     prob = jnp.zeros((experts, tokens), F32)
     for pick in range(TOP):
@@ -62,23 +76,33 @@
     earlier = lax.broadcasted_iota(jnp.int32, square, 0) < lax.broadcasted_iota(jnp.int32, square, 1)
     rank = dot(named.astype(BF16), jnp.where(earlier, 1.0, 0.0).astype(BF16), ((1,), (0,)))
     rank = jnp.where(named > 0.0, rank, float(CAP))
-    shape = (experts, CAP, tokens)
-    rank = jnp.broadcast_to(rank[:, None, :], shape)
-    prob = jnp.broadcast_to(prob[:, None, :], shape)
+    shape = (pairs, CAP, tokens)
+    low = low_rows(shape)
+
+    def spread(table):
+        even = jnp.broadcast_to(table[:pairs, None, :], shape)
+        return jnp.where(low, even, jnp.broadcast_to(table[pairs:, None, :], shape))
+
+    rank, prob = spread(rank), spread(prob)
     slot = lax.rem(lax.broadcasted_iota(jnp.int32, shape, 1), HELD).astype(F32)
-    rows, half = experts * CAP, quarter // 2
     loads[2].wait()
     for core in range(CORES):
         hit = rank == slot + float(core * HELD)
         scale = jnp.sum(jnp.where(hit, prob, 0.0), axis=2, keepdims=True)
-        mask = jnp.where(hit, 1.0, 0.0).reshape(rows, tokens).astype(BF16)
-        left = dot(mask, grad_ref[:, :half], ((1,), (0,))).reshape(experts, CAP, half)
-        right = dot(mask, grad_ref[:, half:], ((1,), (0,))).reshape(experts, CAP, half)
-        picked = jnp.where(low_rows(left.shape), left, right)
-        sent_ref[core] = (picked * scale).astype(BF16)
-
-
-def mask_body(ids_ref, mask_ref, *, experts):
+        mask = jnp.where(hit, 1.0, 0.0).reshape(pairs * CAP, tokens).astype(BF16)
+        left = dot(mask, grad_ref[:, :half], ((1,), (0,))).reshape(pairs, CAP, half) * scale
+        right = dot(mask, grad_ref[:, half:], ((1,), (0,))).reshape(pairs, CAP, half) * scale
+        sent_ref[core, :, 0] = pack(left, right, 0).astype(BF16)
+        sent_ref[core, :, 1] = pack(left, right, 1).astype(BF16)
+
+
+def prepare_body(ids_ref, after_ref, mine_in, other_in, mask_ref, w_ref, sems, *, experts):
+    loads = [
+        pltpu.make_async_copy(source, w_ref.at[index], sems.at[index])
+        for index, source in enumerate((mine_in, other_in))
+    ]
+    for load in loads:
+        load.start()
     tokens = ids_ref.shape[0]
     expert = lax.broadcasted_iota(jnp.int32, (tokens, experts), 1)
     named = jnp.zeros((tokens, experts), F32)
@@ -92,54 +116,63 @@
     spread = lax.broadcasted_iota(jnp.int32, (experts, rows), 0)
     spread = spread == lax.broadcasted_iota(jnp.int32, (experts, rows), 1) // CAP
     rank = dot(rank, jnp.where(spread, 1.0, 0.0).astype(BF16), ((1,), (0,)))
-    slot = lax.rem(lax.broadcasted_iota(jnp.int32, (tokens, rows), 1), HELD).astype(F32)
+    row = lax.broadcasted_iota(jnp.int32, (tokens, rows), 1)
+    slot = lax.rem(row, HELD).astype(F32)
+    low = lax.rem(row, CAP) < HELD
     for core in range(CORES):
         hit = rank == slot + float(core * HELD)
-        mask_ref[:, core * rows : (core + 1) * rows] = jnp.where(hit, 1.0, 0.0).astype(BF16)
-
-
-def hidden_body(core_ref, rows_ref, mine_ref, other_ref, keep_ref, send_ref):
+        columns = slice(core * rows, (core + 1) * rows)
+        mask_ref[:tokens, columns] = jnp.where(hit & low, 1.0, 0.0).astype(BF16)
+        mask_ref[tokens:, columns] = jnp.where(hit & ~low, 1.0, 0.0).astype(BF16)
+    for load in loads:
+        load.wait()
+
+
+def gate_pick_body(core_ref, gate_ref, out_ref):
+    rows = gate_ref[...].astype(F32).reshape(-1, 2, CAP, gate_ref.shape[1])
+    even, odd = rows[:, 0], rows[:, 1]
+    first, last = pack(even, odd, 0), pack(even, odd, 1)
+    chosen = jnp.where(core_ref[0] == 0, first, last)
+    out_ref[...] = chosen.reshape(out_ref.shape).astype(BF16)
+
+
+def hidden_body(core_ref, rows_ref, mine_in, other_in, keep_ref, send_ref, w_ref, sems):
+    loads = [
+        pltpu.make_async_copy(source, w_ref.at[index], sems.at[index])
+        for index, source in enumerate((mine_in, other_in))
+    ]
+    for load in loads:
+        load.start()
     total = None
-    for lane, w_ref in ((core_ref[0], mine_ref), (1 - core_ref[0], other_ref)):
+    for index, lane in enumerate((core_ref[0], 1 - core_ref[0])):
         rows = rows_ref[lane].astype(F32)
         half = rows.shape[-1]
-        pairs = rows.reshape(rows.shape[0] // 2, 2, CAP, half)
-        even, odd = pairs[:, 0], pairs[:, 1]
-        low = low_rows(even.shape)
-        left = jnp.where(low, even, pltpu.roll(odd, HELD, 1))
-        right = jnp.where(low, pltpu.roll(even, HELD, 1), odd)
-        for column, part in enumerate((left, right)):
-            part = part.reshape(-1, half).astype(BF16)
-            term = dot(part, w_ref[:, column * half : (column + 1) * half])
+        rows = rows.reshape(-1, 2, CAP, half)
+        parts = [pack(rows[:, 0], rows[:, 1], side).reshape(-1, half).astype(BF16) for side in range(2)]
+        loads[index].wait()
+        for side, part in enumerate(parts):
+            term = dot(part, w_ref[index, :, side * half : (side + 1) * half])
             total = term if total is None else total + term
     keep_ref[...] = total
     send_ref[...] = total.astype(BF16)
 
 
-def slot_grad_body(core_ref, keep_ref, away_ref, gate_ref, mine_ref, other_ref, out_ref):
+def slot_grad_body(core_ref, keep_ref, away_ref, gate_ref, w_ref, mask_in, out_ref):
     hidden = keep_ref[...] + away_ref[...].astype(F32)
     up = (hidden * gate_ref[...].astype(F32)).astype(BF16)
     half = out_ref.shape[-1]
-    for lane, w_ref in ((core_ref[0], mine_ref), (1 - core_ref[0], other_ref)):
-        left = dot(up, w_ref[:half, :]).reshape(-1, CAP, half)
-        right = dot(up, w_ref[half:, :]).reshape(-1, CAP, half)
-        low = low_rows(left.shape)
-        out_ref[lane, :, 0] = jnp.where(low, left, pltpu.roll(right, HELD, 1)).astype(BF16)
-        out_ref[lane, :, 1] = jnp.where(low, pltpu.roll(left, HELD, 1), right).astype(BF16)
-
-
-def combine_body(mask_in, back_ref, out_ref, mask_ref, sem):
-    load = pltpu.make_async_copy(mask_in, mask_ref, sem)
-    load.start()
-    load.wait()
-    half = back_ref.shape[1]
-    mask = mask_ref[...]
-    low = lax.rem(lax.broadcasted_iota(jnp.int32, mask.shape, 1), CAP) < HELD
-    none = jnp.zeros_like(mask)
-    left = jnp.where(low, mask, none)
-    right = jnp.where(low, none, mask)
-    out_ref[:, :half] = dot(left, back_ref[...], ((1,), (0,))).astype(BF16)
-    out_ref[:, half:] = dot(right, back_ref[...], ((1,), (0,))).astype(BF16)
+    for index, lane in enumerate((core_ref[0], 1 - core_ref[0])):
+        left = dot(up, w_ref[index, :half, :]).reshape(-1, CAP, half)
+        right = dot(up, w_ref[index, half:, :]).reshape(-1, CAP, half)
+        out_ref[lane, :, 0] = pack(left, right, 0).astype(BF16)
+        out_ref[lane, :, 1] = pack(left, right, 1).astype(BF16)
+
+
+def combine_body(mask_ref, back_ref, out_ref):
+    tokens, half = out_ref.shape[0], back_ref.shape[1]
+    both = dot(mask_ref[...], back_ref[...], ((1,), (0,))).astype(BF16)
+    out_ref[:, :half] = both[:tokens]
+    out_ref[:, half:] = both[tokens:]
 
 
 def dense_part_body(core_ref, rows_ref, w_ref, mine_ref, other_ref, full_ref):
@@ -208,19 +241,25 @@
     ids, probs = expert_ids.T, route_probs.T
     sent = call(
         functools.partial(route_body, experts=experts),
-        pltpu.VMEM((CORES, experts, CAP, half), BF16),
+        jax.ShapeDtypeStruct((CORES, experts // 2, 2, CAP, half), BF16),
         [FAR] * 3,
         [pltpu.VMEM(array.shape, array.dtype) for array in (ids, probs, grad_out)]
         + [pltpu.SemaphoreType.DMA((3,))],
-        flops=4 * slots * tokens * quarter,
+        flops=2 * slots * tokens * quarter,
         moved=4 * slots * quarter,
-    )(*(pltpu.with_memory_space_constraint(array, pltpu.HBM) for array in (ids, probs, grad_out)))
+    )(*far(ids, probs, grad_out))
     arrived = exchange(sent)
 
     down_other = lax.ppermute(w_down[0], "tensor", CORE_SWAP)
     up_other = lax.ppermute(w_up[0], "tensor", CORE_SWAP)
-    gate = saved_gate.reshape(experts, CORES, HELD, -1)
-    gate = lax.dynamic_index_in_dim(gate, core[0], 1, keepdims=False).reshape(held, -1)
+    width = w_down.shape[1]
+    gate = call(
+        gate_pick_body,
+        jax.ShapeDtypeStruct((held, width), BF16),
+        [SCALAR, WHOLE],
+        flops=slots * width,
+        moved=3 * slots * width,
+    )(core, saved_gate[0, 0])
     dense_up = dense_up_grad(core, grad_out, shared_down, shared_gate)
     shared_grad = call(
         dense_out_body,
@@ -229,41 +268,45 @@
         flops=2 * tokens * quarter * shared_up.shape[1],
         moved=2 * quarter * shared_up.shape[1],
     )(core, *dense_up, shared_up)
-    mask = call(
-        functools.partial(mask_body, experts=experts),
-        jax.ShapeDtypeStruct((tokens, CORES * slots), BF16),
-        [WHOLE],
-        flops=2 * tokens * slots * experts,
-        moved=4 * tokens * slots,
-    )(expert_ids)
-    arrived, down_other, up_other, gate, shared_grad, mask = lax.optimization_barrier(
-        (arrived, down_other, up_other, gate, shared_grad, mask)
+    ids, arrived, down_other, up_other, gate, shared_grad = lax.optimization_barrier(
+        (expert_ids, arrived, down_other, up_other, gate, shared_grad)
     )
-    work = 4 * held * quarter * gate.shape[1]
+    work = 4 * held * quarter * width
     keep, send = call(
         hidden_body,
         (jax.ShapeDtypeStruct(gate.shape, F32), jax.ShapeDtypeStruct(gate.shape, BF16)),
-        [SCALAR] + [WHOLE] * 3,
+        [SCALAR, WHOLE, FAR, FAR],
+        [pltpu.VMEM((CORES, width, quarter), BF16), pltpu.SemaphoreType.DMA((CORES,))],
         flops=work,
-        moved=4 * quarter * gate.shape[1],
-    )(core, arrived.reshape(CORES, experts, CAP, half), w_down[0], down_other)
+        moved=4 * quarter * width,
+    )(core, arrived.reshape(CORES, experts, CAP, half), *far(w_down[0], down_other))
     away = lax.ppermute(send, "tensor", CHIP_SWAP)
+    mask, w_both = call(
+        functools.partial(prepare_body, experts=experts),
+        (
+            jax.ShapeDtypeStruct((2 * tokens, CORES * slots), BF16),
+            jax.ShapeDtypeStruct((CORES, quarter, width), BF16),
+        ),
+        [WHOLE, ANY, FAR, FAR],
+        [pltpu.SemaphoreType.DMA((CORES,))],
+        flops=2 * tokens * slots * experts,
+        moved=4 * quarter * width,
+    )(ids, keep, *far(w_up[0], up_other))
     slot_grad = call(
         slot_grad_body,
-        pltpu.VMEM((CORES, experts // 2, 2, CAP, half), BF16),
-        [SCALAR] + [WHOLE] * 5,
+        jax.ShapeDtypeStruct((CORES, experts // 2, 2, CAP, half), BF16),
+        [SCALAR] + [WHOLE] * 4 + [ANY],
         flops=work,
-        moved=4 * quarter * gate.shape[1],
-    )(core, keep, away, gate, w_up[0], up_other)
+        moved=4 * quarter * width,
+    )(core, keep, away, gate, w_both, mask)
     back = exchange(slot_grad)
     moe_grad = call(
         combine_body,
         jax.ShapeDtypeStruct((tokens, quarter), BF16),
-        [FAR, WHOLE],
-        [pltpu.VMEM(mask.shape, BF16), pltpu.SemaphoreType.DMA(())],
+        [WHOLE] * 2,
         flops=4 * slots * tokens * quarter,
         moved=2 * slots * quarter,
-    )(pltpu.with_memory_space_constraint(mask, pltpu.HBM), back.reshape(CORES * slots, half))
+    )(mask, back.reshape(CORES * slots, half))
     return (moe_grad, shared_grad)
 
 

time: 135 us -> 129 us (0.956)
  waiting for transfers between devices: 13.4 us -> 25.6 us
  local copies, waits for them, and re-layouts: 12.2 us -> 1.13 us
  Pallas kernels: 17.9 us -> 14.2 us
  blocking collectives: 48 us -> 44.4 us
    all_to_all x1, waiting for transfers between devices: 3.49 us -> 14.3 us  [exchange(): lax.all_to_all(rows, ('expert', 'tensor'), 0, 0, axis_index_groups=groups...]
    unnamed x24 -> x12, local copies, waits for them, and re-layouts: 7.85 us -> 1.02 us
    reshape x2 -> x0, local copies, waits for them, and re-layouts: 4.35 us -> none  [the longest x1 2.52 us: on_device(): gate = saved_gate.reshape(experts, CORES, HELD, -1)]
    all_to_all x1, blocking collectives: 48 us -> 44.4 us  [exchange(): lax.all_to_all(rows, ('expert', 'tensor'), 0, 0, axis_index_groups=groups...]
    ppermute x1, waiting for transfers between devices: 0.33 us -> 3.31 us  [dense_up_grad(): away = lax.ppermute((mine + pair).astype(BF16), 'tensor', CHIP_SWAP)]
    ppermute x1, waiting for transfers between devices: 8.42 us -> 6.13 us  [on_device(): away = lax.ppermute(send, 'tensor', CHIP_SWAP)]
    pallas_call x1, Pallas kernels: 1.61 us -> 0.06 us  [dense_up_grad(): call(dense_gate_body, jax.ShapeDtypeStruct((tokens // 2, width), BF16), [...]
    pallas_call x4 -> x5, Pallas kernels: 9.28 us -> 8.16 us  [the longest x1 2.95 us: on_device(): call(functools.partial(route_body, experts=experts), jax.ShapeDtypeStruct...]
  transfers between devices with their start and end apart: 7 -> 7, of which waited for: 4 -> 5; matrix products, arithmetic and copies ran while one was open for 6% -> 0% of each run, Pallas kernels for 4% -> 4%
where the time goes in v4:
time: 129 us; the launch traced here: 128 us
  blocking collectives  44.4 us (34%)
  starting transfers between devices  42 us (33%)
  waiting for transfers between devices  25.6 us (20%)
  Pallas kernels  14.2 us (11%)
    all_to_all x1, blocking collectives, exchange(): lax.all_to_all(rows, ('expert', 'tensor'), 0, 0, axis_index_groups=groups...  44.4 us
    all_to_all x1, starting transfers between devices, exchange(): lax.all_to_all(rows, ('expert', 'tensor'), 0, 0, axis_index_groups=groups...  25.7 us
    all_to_all x1, waiting for transfers between devices, exchange(): lax.all_to_all(rows, ('expert', 'tensor'), 0, 0, axis_index_groups=groups...  14.3 us
    ppermute x1, waiting for transfers between devices, on_device(): away = lax.ppermute(send, 'tensor', CHIP_SWAP)  6.13 us
    pallas_call x1, Pallas kernels, on_device(): call(hidden_body, (jax.ShapeDtypeStruct(gate.shape, F32), jax.ShapeDtypeS...  3.56 us
    ppermute x1, waiting for transfers between devices, dense_up_grad(): away = lax.ppermute((mine + pair).astype(BF16), 'tensor', CHIP_SWAP)  3.31 us
    ppermute x1, starting transfers between devices, on_device(): away = lax.ppermute(send, 'tensor', CHIP_SWAP)  3.12 us
    ppermute x1, starting transfers between devices, dense_up_grad(): away = lax.ppermute((mine + pair).astype(BF16), 'tensor', CHIP_SWAP)  3.11 us
  transfers between devices with their start and end apart: 7, of which 5 were waited for; matrix products, arithmetic and copies ran while one was open for 0% of the time, Pallas kernels for 4%

profile of v4, /device:TPU:1, one launch (start us, length us, event | category | flops | bytes accessed | tf_op | source)
XLA Modules:
  0.0 128.1 jit_solution(3756755170027365371)
XLA Ops:
  0.6 0.0 copy-start.1
  0.6 2.9 %shard_map.104 = bf16[2,32,2,8,640]{4,3,2,1,0:T(8,128)(2,1)} custom-call(s32[6,160]{1,0:T(8,128)} %bitcast.18, f32[6,160]{1,0:T(8,128)} %bitcast.19, bf16[160,1280]{1,0:T(8,128)(2,1)} %rows_ref.1), custom_call_target="tpu_custom_call" | custom-call | flops 209715200 | bytes 2621440 | tf_op jit(solution)/shard_map/pallas_call | solution.py:242
  3.6 0.0 copy-start.4
  3.6 25.7 %all-to-all-start = ((bf16[128,8,640]{2,1,0:T(8,128)(2,1)}), bf16[128,8,640]{2,1,0:T(8,128)(2,1)S(1)}, u32[]{:S(2)}, u32[]{:S(2)}) async-start(bf16[128,8,640]{2,1,0:T(8,128)(2,1)} %bitcast.2), calls=%async_computation | async-start | bytes 2621440 | tf_op jit(solution)/shard_map/all_to_all | solution.py:237
  29.3 2.5 %collective-permute-start.1 = (bf16[1280,768]{1,0:T(8,128)(2,1)}, bf16[1280,768]{1,0:T(8,128)(2,1)}, u32[]{:S(2)}, u32[]{:S(2)}) collective-permute-start(bf16[1280,768]{1,0:T(8,128)(2,1)} %bitcast.14), channel_id=1, source_target_pairs={{0,1},{1,0},{2,3},{3,2},{4,5},{5,4},{6,7},{7,6},{8,9},{9,8},{10,11... | collective-permute-start | bytes 5898248 | tf_op jit(solution)/shard_map/ppermute | solution.py:254
  31.8 1.9 %collective-permute-start = (bf16[768,1280]{1,0:T(8,128)(2,1)}, bf16[768,1280]{1,0:T(8,128)(2,1)}, u32[]{:S(2)}, u32[]{:S(2)}) collective-permute-start(bf16[768,1280]{1,0:T(8,128)(2,1)} %bitcast.16), channel_id=1, source_target_pairs={{0,1},{1,0},{2,3},{3,2},{4,5},{5,4},{6,7},{7,6},{8,9},{9,8},{10,11... | collective-permute-start | bytes 5898248 | tf_op jit(solution)/shard_map/ppermute | solution.py:253
  33.7 0.0 copy-done.1
  33.8 0.0 copy-start.2
  33.8 1.0 copy-done.2
  34.8 0.8 shard_map.106
  35.6 0.0 copy-start
  35.6 2.5 %collective-permute-start.2 = (f32[80,768]{1,0:T(8,128)S(1)}, f32[80,768]{1,0:T(8,128)S(1)}, u32[]{:S(2)}, u32[]{:S(2)}) collective-permute-start(f32[80,768]{1,0:T(8,128)S(1)} %get-tuple-element.15), channel_id=1, source_target_pairs={{0,1},{1,0},{2,3},{3,2},{4,5},{5,4},{6,7},{7,6},{8,9},{9,8},{10,11... | collective-permute-start | bytes 737288 | tf_op jit(solution)/shard_map/ppermute | solution.py:211
  38.2 1.1 collective-permute-done.2.pair_ref
  39.3 3.1 %collective-permute-start.3 = (bf16[80,768]{1,0:T(8,128)(2,1)S(1)}, bf16[80,768]{1,0:T(8,128)(2,1)S(1)}, u32[]{:S(2)}, u32[]{:S(2)}) collective-permute-start(bf16[80,768]{1,0:T(8,128)(2,1)S(1)} %add_convert_fusion), channel_id=1, source_target_pairs={{0,2},{1,3},{2,0},{3,1},{4,6},{5,7},{6,4},{7,5},{8,10},{9,11},{10,... | collective-permute-start | bytes 368648 | tf_op jit(solution)/shard_map/ppermute | solution.py:212
  42.4 3.3 %collective-permute-done.3.away_ref = bf16[80,768]{1,0:T(8,128)(2,1)S(1)} collective-permute-done((bf16[80,768]{1,0:T(8,128)(2,1)S(1)}, bf16[80,768]{1,0:T(8,128)(2,1)S(1)}, u32[]{:S(2)}, u32[]{:S(2)}) %collective-permute-start.3) | collective-permute-done | bytes 122912 | tf_op jit(solution)/shard_map/ppermute | solution.py:212
  45.7 0.1 shard_map.107.mine_ref
  45.8 3.1 %collective-permute-start.4 = (bf16[80,768]{1,0:T(8,128)(2,1)S(1)}, bf16[80,768]{1,0:T(8,128)(2,1)S(1)}, u32[]{:S(2)}, u32[]{:S(2)}) collective-permute-start(bf16[80,768]{1,0:T(8,128)(2,1)S(1)} %shard_map.107.mine_ref), channel_id=1, source_target_pairs={{0,1},{1,0},{2,3},{3,2},{4,5},{5,4},{6,7},{7,6},{8,9},{9,8},{10,11... | collective-permute-start | bytes 368648 | tf_op jit(solution)/shard_map/ppermute | solution.py:220
  48.9 0.2 shard_map.105.gate_ref
  49.1 0.7 collective-permute-done.4.other_ref
  49.9 0.0 copy-done
  49.9 1.6 %shard_map.108 = bf16[160,1280]{1,0:T(8,128)(2,1)} custom-call(s32[1]{0:T(128)} %bitcast.5.core_ref, bf16[80,768]{1,0:T(8,128)(2,1)S(1)} %shard_map.107.mine_ref, bf16[80,768]{1,0:T(8,128)(2,1)S(1)} %collective-permute-done.4.other_ref, bf16[1280,768]{1,0:T(8,128)(2,1)S(1)} %copy-done), custom_call_target="tpu_custom_call" | custom-call | flops 314572800 | bytes 1966080 | tf_op jit(solution)/shard_map/pallas_call | solution.py:264
  51.4 0.0 collective-permute-done.1.other_in
  51.5 0.0 collective-permute-done.other_in
  51.5 14.3 %all-to-all-done = bf16[128,8,640]{2,1,0:T(8,128)(2,1)S(1)} async-done(((bf16[128,8,640]{2,1,0:T(8,128)(2,1)}), bf16[128,8,640]{2,1,0:T(8,128)(2,1)S(1)}, u32[]{:S(2)}, u32[]{:S(2)}) %all-to-all-start) | async-done | bytes 1310752 | tf_op jit(solution)/shard_map/all_to_all | solution.py:237
  65.8 3.6 %shard_map.109 = (f32[256,768]{1,0:T(8,128)S(1)}, bf16[256,768]{1,0:T(8,128)(2,1)S(1)}) custom-call(s32[1]{0:T(128)} %bitcast.5.core_ref, bf16[2,64,8,640]{3,2,1,0:T(8,128)(2,1)S(1)} %bitcast.11, bf16[768,1280]{1,0:T(8,128)(2,1)} %bitcast.17, bf16[768,1280]{1,0:T(8,128)(2,1)} %collective-permute-done.other_in), custom_call_target="tpu_custom_call" | custom-call | flops 1006632960 | bytes 3932160 | tf_op jit(solution)/shard_map/pallas_call | solution.py:275
  69.3 3.1 %collective-permute-start.5 = (bf16[256,768]{1,0:T(8,128)(2,1)S(1)}, bf16[256,768]{1,0:T(8,128)(2,1)S(1)}, u32[]{:S(2)}, u32[]{:S(2)}) collective-permute-start(bf16[256,768]{1,0:T(8,128)(2,1)S(1)} %get-tuple-element.22), channel_id=1, source_target_pairs={{0,2},{1,3},{2,0},{3,1},{4,6},{5,7},{6,4},{7,5},{8,10},{9,11},{10,... | collective-permute-start | bytes 1179656 | tf_op jit(solution)/shard_map/ppermute | solution.py:283
  72.5 0.1 copy.11.ids_ref
  72.6 2.2 %shard_map.110 = (bf16[320,1024]{1,0:T(8,128)(2,1)S(1)}, bf16[2,1280,768]{2,1,0:T(8,128)(2,1)S(1)}) custom-call(s32[160,6]{1,0:T(8,128)S(1)} %copy.11.ids_ref, f32[256,768]{1,0:T(8,128)S(1)} %get-tuple-element.19.after_ref.keep_ref, bf16[1280,768]{1,0:T(8,128)(2,1)} %bitcast.15, bf16[1280,768]{1,0:T(8,128)(2,1)} %collective-permute-done.1.other_in), custom_call_target="tpu_custom_call" | custom-call | flops 10485760 | bytes 3932160 | tf_op jit(solution)/shard_map/pallas_call | solution.py:284
  74.8 6.1 %collective-permute-done.5.away_ref = bf16[256,768]{1,0:T(8,128)(2,1)S(1)} collective-permute-done((bf16[256,768]{1,0:T(8,128)(2,1)S(1)}, bf16[256,768]{1,0:T(8,128)(2,1)S(1)}, u32[]{:S(2)}, u32[]{:S(2)}) %collective-permute-start.5) | collective-permute-done | bytes 393248 | tf_op jit(solution)/shard_map/ppermute | solution.py:283
  80.9 1.4 %shard_map.111 = bf16[2,32,2,8,640]{4,3,2,1,0:T(8,128)(2,1)S(1)} custom-call(s32[1]{0:T(128)} %bitcast.5.core_ref, f32[256,768]{1,0:T(8,128)S(1)} %get-tuple-element.19.after_ref.keep_ref, bf16[256,768]{1,0:T(8,128)(2,1)S(1)} %collective-permute-done.5.away_ref, bf16[256,768]{1,0:T(8,128)(2,1)S(1)} %shard_map.105.gate_ref, ...), custom_call_target="tpu_custom_call" | custom-call | flops 1006632960 | bytes 3932160 | tf_op jit(solution)/shard_map/pallas_call | solution.py:295
  82.3 44.4 %all_to_all.10 = bf16[128,8,640]{2,1,0:T(8,128)(2,1)S(1)} all-to-all(bf16[128,8,640]{2,1,0:T(8,128)(2,1)S(1)} %bitcast.12), channel_id=1, replica_groups={{0,4,8,12,16,20,24,28,32,36,40,44,48,52,56,60,64,68,72,76,80,84,88,92,9..., dimensions={0} | all-to-all | bytes 2621440 | tf_op jit(solution)/shard_map/all_to_all | solution.py:237
  126.7 1.4 %shard_map.112 = bf16[160,1280]{1,0:T(8,128)(2,1)} custom-call(bf16[320,1024]{1,0:T(8,128)(2,1)S(1)} %get-tuple-element.21.mask_in.mask_ref, bf16[1024,640]{1,0:T(8,128)(2,1)S(1)} %bitcast.10), custom_call_target="tpu_custom_call" | custom-call | flops 419430400 | bytes 1310720 | tf_op jit(solution)/shard_map/pallas_call | solution.py:303
  (6 shorter events, 0.0 us)
Async XLA Ops:
  0.6 33.1 %copy-start.1 = (bf16[768,1280]{1,0:T(8,128)(2,1)S(1)}, bf16[768,1280]{1,0:T(8,128)(2,1)}, u32[]{:S(2)}) copy-start(bf16[768,1280]{1,0:T(8,128)(2,1)} %w_ref.2) | copy-start | bytes 5898244
  3.6 42.1 %copy-start.4 = (bf16[160,768]{1,0:T(8,128)(2,1)S(1)}, bf16[160,768]{1,0:T(8,128)(2,1)}, u32[]{:S(2)}) copy-start(bf16[160,768]{1,0:T(8,128)(2,1)} %gate_ref.1) | copy-start | bytes 737284
  3.6 62.2 %all-to-all-start = ((bf16[128,8,640]{2,1,0:T(8,128)(2,1)}), bf16[128,8,640]{2,1,0:T(8,128)(2,1)S(1)}, u32[]{:S(2)}, u32[]{:S(2)}) async-start(bf16[128,8,640]{2,1,0:T(8,128)(2,1)} %bitcast.2), calls=%async_computation | async-start | bytes 2621440 | tf_op jit(solution)/shard_map/all_to_all | solution.py:237
  29.3 22.1 %collective-permute-start.1 = (bf16[1280,768]{1,0:T(8,128)(2,1)}, bf16[1280,768]{1,0:T(8,128)(2,1)}, u32[]{:S(2)}, u32[]{:S(2)}) collective-permute-start(bf16[1280,768]{1,0:T(8,128)(2,1)} %bitcast.14), channel_id=1, source_target_pairs={{0,1},{1,0},{2,3},{3,2},{4,5},{5,4},{6,7},{7,6},{8,9},{9,8},{10,11... | collective-permute-start | bytes 5898248 | tf_op jit(solution)/shard_map/ppermute | solution.py:254
  31.8 19.6 %collective-permute-start = (bf16[768,1280]{1,0:T(8,128)(2,1)}, bf16[768,1280]{1,0:T(8,128)(2,1)}, u32[]{:S(2)}, u32[]{:S(2)}) collective-permute-start(bf16[768,1280]{1,0:T(8,128)(2,1)} %bitcast.16), channel_id=1, source_target_pairs={{0,1},{1,0},{2,3},{3,2},{4,5},{5,4},{6,7},{7,6},{8,9},{9,8},{10,11... | collective-permute-start | bytes 5898248 | tf_op jit(solution)/shard_map/ppermute | solution.py:253
  33.8 1.0 copy-start.2
  34.8 14.2 %copy-start.3 = (bf16[1,1,512,768]{3,2,1,0:T(8,128)(2,1)S(1)}, bf16[1,1,512,768]{3,2,1,0:T(8,128)(2,1)}, u32[]{:S(2)}) copy-start(bf16[1,1,512,768]{3,2,1,0:T(8,128)(2,1)} %param.12) | copy-start | bytes 2359300
  35.6 14.3 %copy-start = (bf16[1280,768]{1,0:T(8,128)(2,1)S(1)}, bf16[1280,768]{1,0:T(8,128)(2,1)}, u32[]{:S(2)}) copy-start(bf16[1280,768]{1,0:T(8,128)(2,1)} %w_ref.3) | copy-start | bytes 5898244
  35.6 3.7 %collective-permute-start.2 = (f32[80,768]{1,0:T(8,128)S(1)}, f32[80,768]{1,0:T(8,128)S(1)}, u32[]{:S(2)}, u32[]{:S(2)}) collective-permute-start(f32[80,768]{1,0:T(8,128)S(1)} %get-tuple-element.15), channel_id=1, source_target_pairs={{0,1},{1,0},{2,3},{3,2},{4,5},{5,4},{6,7},{7,6},{8,9},{9,8},{10,11... | collective-permute-start | bytes 737288 | tf_op jit(solution)/shard_map/ppermute | solution.py:211
  39.3 6.4 %collective-permute-start.3 = (bf16[80,768]{1,0:T(8,128)(2,1)S(1)}, bf16[80,768]{1,0:T(8,128)(2,1)S(1)}, u32[]{:S(2)}, u32[]{:S(2)}) collective-permute-start(bf16[80,768]{1,0:T(8,128)(2,1)S(1)} %add_convert_fusion), channel_id=1, source_target_pairs={{0,2},{1,3},{2,0},{3,1},{4,6},{5,7},{6,4},{7,5},{8,10},{9,11},{10,... | collective-permute-start | bytes 368648 | tf_op jit(solution)/shard_map/ppermute | solution.py:212
  45.8 4.1 %collective-permute-start.4 = (bf16[80,768]{1,0:T(8,128)(2,1)S(1)}, bf16[80,768]{1,0:T(8,128)(2,1)S(1)}, u32[]{:S(2)}, u32[]{:S(2)}) collective-permute-start(bf16[80,768]{1,0:T(8,128)(2,1)S(1)} %shard_map.107.mine_ref), channel_id=1, source_target_pairs={{0,1},{1,0},{2,3},{3,2},{4,5},{5,4},{6,7},{7,6},{8,9},{9,8},{10,11... | collective-permute-start | bytes 368648 | tf_op jit(solution)/shard_map/ppermute | solution.py:220
  65.8 6.7 %copy-start.5 = (s32[160,6]{0,1:T(8,128)S(1)}, s32[160,6]{0,1:T(8,128)}, u32[]{:S(2)}) copy-start(s32[160,6]{0,1:T(8,128)} %param.10) | copy-start | bytes 11524
  69.3 11.5 %collective-permute-start.5 = (bf16[256,768]{1,0:T(8,128)(2,1)S(1)}, bf16[256,768]{1,0:T(8,128)(2,1)S(1)}, u32[]{:S(2)}, u32[]{:S(2)}) collective-permute-start(bf16[256,768]{1,0:T(8,128)(2,1)S(1)} %get-tuple-element.22), channel_id=1, source_target_pairs={{0,2},{1,3},{2,0},{3,1},{4,6},{5,7},{6,4},{7,5},{8,10},{9,11},{10,... | collective-permute-start | bytes 1179656 | tf_op jit(solution)/shard_map/ppermute | solution.py:283

commit v5 on v4

--- a/solution.py
+++ b/solution.py
@@ -16,7 +16,6 @@
 F32, BF16 = jnp.float32, jnp.bfloat16
 WHOLE = pl.BlockSpec(memory_space=pltpu.VMEM)
 FAR = pl.BlockSpec(memory_space=pltpu.HBM)
-ANY = pl.BlockSpec(memory_space=pl.ANY)
 SCALAR = pl.BlockSpec(memory_space=pltpu.SMEM)
 
 
@@ -24,12 +23,12 @@
     return lax.dot_general(a, b, (dims, ((), ())), preferred_element_type=F32)
 
 
-def call(body, outs, specs, scratch=(), flops=0, moved=0):
+def call(body, outs, specs, scratch=(), flops=0, moved=0, place=WHOLE):
     return pl.pallas_call(
         body,
         out_shape=outs,
         in_specs=specs,
-        out_specs=jax.tree.map(lambda _: WHOLE, outs),
+        out_specs=jax.tree.map(lambda _: place, outs),
         scratch_shapes=list(scratch),
         compiler_params=pltpu.CompilerParams(vmem_limit_bytes=12 << 20),
         cost_estimate=pl.CostEstimate(flops=flops, bytes_accessed=moved, transcendentals=0),
@@ -51,7 +50,9 @@
     return jnp.where(low, pltpu.roll(even, HELD, 1), odd)
 
 
-def route_body(ids_in, prob_in, grad_in, sent_ref, ids_ref, prob_ref, grad_ref, sems, *, experts):
+def route_body(
+    ids_in, prob_in, grad_in, sent_out, ids_ref, prob_ref, grad_ref, sent_ref, sems, *, experts
+):
     tokens, quarter = grad_ref.shape
     loads = [
         pltpu.make_async_copy(source, target, sems.at[index])
@@ -86,6 +87,10 @@
     rank, prob = spread(rank), spread(prob)
     slot = lax.rem(lax.broadcasted_iota(jnp.int32, shape, 1), HELD).astype(F32)
     loads[2].wait()
+    stores = [
+        pltpu.make_async_copy(sent_ref.at[core], sent_out.at[core], sems.at[3 + core])
+        for core in range(CORES)
+    ]
     for core in range(CORES):
         hit = rank == slot + float(core * HELD)
         scale = jnp.sum(jnp.where(hit, prob, 0.0), axis=2, keepdims=True)
@@ -94,15 +99,12 @@
         right = dot(mask, grad_ref[:, half:], ((1,), (0,))).reshape(pairs, CAP, half) * scale
         sent_ref[core, :, 0] = pack(left, right, 0).astype(BF16)
         sent_ref[core, :, 1] = pack(left, right, 1).astype(BF16)
-
-
-def prepare_body(ids_ref, after_ref, mine_in, other_in, mask_ref, w_ref, sems, *, experts):
-    loads = [
-        pltpu.make_async_copy(source, w_ref.at[index], sems.at[index])
-        for index, source in enumerate((mine_in, other_in))
-    ]
-    for load in loads:
-        load.start()
+        stores[core].start()
+    for store in stores:
+        store.wait()
+
+
+def mask_body(ids_ref, mask_ref, *, experts):
     tokens = ids_ref.shape[0]
     expert = lax.broadcasted_iota(jnp.int32, (tokens, experts), 1)
     named = jnp.zeros((tokens, experts), F32)
@@ -124,8 +126,6 @@
         columns = slice(core * rows, (core + 1) * rows)
         mask_ref[:tokens, columns] = jnp.where(hit & low, 1.0, 0.0).astype(BF16)
         mask_ref[tokens:, columns] = jnp.where(hit & ~low, 1.0, 0.0).astype(BF16)
-    for load in loads:
-        load.wait()
 
 
 def gate_pick_body(core_ref, gate_ref, out_ref):
@@ -136,29 +136,45 @@
     out_ref[...] = chosen.reshape(out_ref.shape).astype(BF16)
 
 
-def hidden_body(core_ref, rows_ref, mine_in, other_in, keep_ref, send_ref, w_ref, sems):
+def hidden_body(
+    core_ref, rows_ref, mine_in, other_in, up_mine_in, up_other_in, keep_ref, send_ref, up_ref, w_ref, sems
+):
+    half = rows_ref.shape[-1]
+    pieces = [(weight, side) for weight in (mine_in, other_in) for side in range(2)]
     loads = [
-        pltpu.make_async_copy(source, w_ref.at[index], sems.at[index])
-        for index, source in enumerate((mine_in, other_in))
-    ]
-    for load in loads:
-        load.start()
+        pltpu.make_async_copy(weight.at[:, pl.ds(side * half, half)], w_ref.at[index], sems.at[index])
+        for index, (weight, side) in enumerate(pieces)
+    ]
+    ups = [
+        pltpu.make_async_copy(source, up_ref.at[index], sems.at[len(loads) + index])
+        for index, source in enumerate((up_mine_in, up_other_in))
+    ]
+    loads[0].start()
+    loads[1].start()
+    parts = []
+    for lane in (core_ref[0], 1 - core_ref[0]):
+        rows = rows_ref[lane].astype(F32).reshape(-1, 2, CAP, half)
+        for side in range(2):
+            parts.append(pack(rows[:, 0], rows[:, 1], side).reshape(-1, half).astype(BF16))
     total = None
-    for index, lane in enumerate((core_ref[0], 1 - core_ref[0])):
-        rows = rows_ref[lane].astype(F32)
-        half = rows.shape[-1]
-        rows = rows.reshape(-1, 2, CAP, half)
-        parts = [pack(rows[:, 0], rows[:, 1], side).reshape(-1, half).astype(BF16) for side in range(2)]
+    for index, part in enumerate(parts):
         loads[index].wait()
-        for side, part in enumerate(parts):
-            term = dot(part, w_ref[index, :, side * half : (side + 1) * half])
-            total = term if total is None else total + term
+        if index + 2 < len(loads):
+            loads[index + 2].start()
+        else:
+            ups[index + 2 - len(loads)].start()
+        term = dot(part, w_ref[index])
+        total = term if total is None else total + term
     keep_ref[...] = total
     send_ref[...] = total.astype(BF16)
-
-
-def slot_grad_body(core_ref, keep_ref, away_ref, gate_ref, w_ref, mask_in, out_ref):
-    hidden = keep_ref[...] + away_ref[...].astype(F32)
+    for up in ups:
+        up.wait()
+
+
+def slot_grad_body(core_ref, keep_ref, away_ref, gate_ref, w_ref, mask_in, out_ref, mask_ref, sem):
+    load = pltpu.make_async_copy(mask_in, mask_ref, sem)
+    load.start()
+    hidden = keep_ref[...] + away_ref[1 - core_ref[1]].astype(F32)
     up = (hidden * gate_ref[...].astype(F32)).astype(BF16)
     half = out_ref.shape[-1]
     for index, lane in enumerate((core_ref[0], 1 - core_ref[0])):
@@ -166,6 +182,7 @@
         right = dot(up, w_ref[index, half:, :]).reshape(-1, CAP, half)
         out_ref[lane, :, 0] = pack(left, right, 0).astype(BF16)
         out_ref[lane, :, 1] = pack(left, right, 1).astype(BF16)
+    load.wait()
 
 
 def combine_body(mask_ref, back_ref, out_ref):
@@ -226,7 +243,8 @@
     experts = lax.axis_size("expert")
     tokens, quarter = grad_out.shape
     half, slots, held = quarter // 2, experts * CAP, experts * HELD
-    core = (lax.axis_index("tensor") & 1).reshape(1)
+    place = lax.axis_index("tensor")
+    core = jnp.stack([place & 1, place >> 1])
     groups = [
         [place * 4 + chip * 2 + lane for lane in range(CORES) for place in range(experts)]
         for chip in range(2)
@@ -244,9 +262,13 @@
         jax.ShapeDtypeStruct((CORES, experts // 2, 2, CAP, half), BF16),
         [FAR] * 3,
         [pltpu.VMEM(array.shape, array.dtype) for array in (ids, probs, grad_out)]
-        + [pltpu.SemaphoreType.DMA((3,))],
+        + [
+            pltpu.VMEM((CORES, experts // 2, 2, CAP, half), BF16),
+            pltpu.SemaphoreType.DMA((3 + CORES,)),
+        ],
         flops=2 * slots * tokens * quarter,
         moved=4 * slots * quarter,
+        place=FAR,
     )(*far(ids, probs, grad_out))
     arrived = exchange(sent)
 
@@ -268,37 +290,46 @@
         flops=2 * tokens * quarter * shared_up.shape[1],
         moved=2 * quarter * shared_up.shape[1],
     )(core, *dense_up, shared_up)
-    ids, arrived, down_other, up_other, gate, shared_grad = lax.optimization_barrier(
-        (expert_ids, arrived, down_other, up_other, gate, shared_grad)
+    mask = call(
+        functools.partial(mask_body, experts=experts),
+        jax.ShapeDtypeStruct((2 * tokens, CORES * slots), BF16),
+        [WHOLE],
+        flops=2 * tokens * slots * experts,
+        moved=4 * tokens * slots,
+    )(expert_ids)
+    arrived, down_other, up_other, gate, shared_grad, mask = lax.optimization_barrier(
+        (arrived, down_other, up_other, gate, shared_grad, mask)
     )
     work = 4 * held * quarter * width
-    keep, send = call(
+    keep, send, up_both = call(
         hidden_body,
-        (jax.ShapeDtypeStruct(gate.shape, F32), jax.ShapeDtypeStruct(gate.shape, BF16)),
-        [SCALAR, WHOLE, FAR, FAR],
-        [pltpu.VMEM((CORES, width, quarter), BF16), pltpu.SemaphoreType.DMA((CORES,))],
+        (
+            jax.ShapeDtypeStruct(gate.shape, F32),
+            jax.ShapeDtypeStruct(gate.shape, BF16),
+            jax.ShapeDtypeStruct((CORES, quarter, width), BF16),
+        ),
+        [SCALAR, WHOLE] + [FAR] * 4,
+        [pltpu.VMEM((2 * CORES, width, half), BF16), pltpu.SemaphoreType.DMA((3 * CORES,))],
+        flops=work,
+        moved=8 * quarter * width,
+    )(
+        core,
+        arrived.reshape(CORES, experts, CAP, half),
+        *far(w_down[0], down_other, w_up[0], up_other),
+    )
+    pair = [[lane, CORES + lane] for lane in range(CORES)]
+    away = lax.all_gather(send, "tensor", axis_index_groups=pair)
+    slot_grad, mask = call(
+        slot_grad_body,
+        (
+            jax.ShapeDtypeStruct((CORES, experts // 2, 2, CAP, half), BF16),
+            jax.ShapeDtypeStruct(mask.shape, BF16),
+        ),
+        [SCALAR] + [WHOLE] * 4 + [FAR],
+        [pltpu.SemaphoreType.DMA(())],
         flops=work,
         moved=4 * quarter * width,
-    )(core, arrived.reshape(CORES, experts, CAP, half), *far(w_down[0], down_other))
-    away = lax.ppermute(send, "tensor", CHIP_SWAP)
-    mask, w_both = call(
-        functools.partial(prepare_body, experts=experts),
-        (
-            jax.ShapeDtypeStruct((2 * tokens, CORES * slots), BF16),
-            jax.ShapeDtypeStruct((CORES, quarter, width), BF16),
-        ),
-        [WHOLE, ANY, FAR, FAR],
-        [pltpu.SemaphoreType.DMA((CORES,))],
-        flops=2 * tokens * slots * experts,
-        moved=4 * quarter * width,
-    )(ids, keep, *far(w_up[0], up_other))
-    slot_grad = call(
-        slot_grad_body,
-        jax.ShapeDtypeStruct((CORES, experts // 2, 2, CAP, half), BF16),
-        [SCALAR] + [WHOLE] * 4 + [ANY],
-        flops=work,
-        moved=4 * quarter * width,
-    )(core, keep, away, gate, w_both, mask)
+    )(core, keep, away, gate, up_both, *far(mask))
     back = exchange(slot_grad)
     moe_grad = call(
         combine_body,

time: 129 us -> 129 us (level)
  waiting for transfers between devices: 25.6 us -> 13.6 us
  blocking collectives: 44.4 us -> 54.7 us
  starting transfers between devices: 42 us -> 38.7 us
  Pallas kernels: 14.2 us -> 17.3 us
  local copies, waits for them, and re-layouts: 1.13 us -> 3.68 us
    all_gather x0 -> x1, blocking collectives: none -> 10.3 us  [on_device(): away = lax.all_gather(send, 'tensor', axis_index_groups=pair)]
    ppermute x1 -> x0, waiting for transfers between devices: 6.13 us -> none  [on_device(): away = lax.ppermute(send, 'tensor', CHIP_SWAP)]
    all_to_all x1, waiting for transfers between devices: 14.3 us -> 9.17 us  [exchange(): lax.all_to_all(rows, ('expert', 'tensor'), 0, 0, axis_index_groups=groups...]
    ppermute x1 -> x0, starting transfers between devices: 3.12 us -> none  [on_device(): away = lax.ppermute(send, 'tensor', CHIP_SWAP)]
    unnamed x12 -> x19, local copies, waits for them, and re-layouts: 1.02 us -> 3.68 us
    pallas_call x1, Pallas kernels: 3.56 us -> 5.31 us  [on_device(): call(hidden_body, (jax.ShapeDtypeStruct(gate.shape, F32), jax.ShapeDtypeS...]
  transfers between devices with their start and end apart: 7 -> 6, of which waited for: 5 -> 3; matrix products, arithmetic and copies ran while one was open for 0% -> 0% of each run, Pallas kernels for 4% -> 4%
where the time goes in v5:
time: 129 us
  blocking collectives  54.7 us (42%)
  starting transfers between devices  38.7 us (30%)
  Pallas kernels  17.3 us (13%)
  waiting for transfers between devices  13.6 us (11%)
  local copies, waits for them, and re-layouts  3.68 us (3%)
    all_to_all x1, blocking collectives, exchange(): lax.all_to_all(rows, ('expert', 'tensor'), 0, 0, axis_index_groups=groups...  44.4 us
    all_to_all x1, starting transfers between devices, exchange(): lax.all_to_all(rows, ('expert', 'tensor'), 0, 0, axis_index_groups=groups...  25.6 us
    all_gather x1, blocking collectives, on_device(): away = lax.all_gather(send, 'tensor', axis_index_groups=pair)  10.3 us
    all_to_all x1, waiting for transfers between devices, exchange(): lax.all_to_all(rows, ('expert', 'tensor'), 0, 0, axis_index_groups=groups...  9.17 us
    pallas_call x1, Pallas kernels, on_device(): call(hidden_body, (jax.ShapeDtypeStruct(gate.shape, F32), jax.ShapeDtypeS...  5.31 us
    unnamed x19, local copies, waits for them, and re-layouts  3.68 us
    ppermute x1, waiting for transfers between devices, dense_up_grad(): away = lax.ppermute((mine + pair).astype(BF16), 'tensor', CHIP_SWAP)  3.3 us
    ppermute x1, starting transfers between devices, dense_up_grad(): away = lax.ppermute((mine + pair).astype(BF16), 'tensor', CHIP_SWAP)  3.12 us
  transfers between devices with their start and end apart: 6, of which 3 were waited for; matrix products, arithmetic and copies ran while one was open for 0% of the time, Pallas kernels for 4%

profile of v5, /device:TPU:1, one launch (start us, length us, event | category | flops | bytes accessed | tf_op | source)
XLA Modules:
  0.0 128.8 jit_solution(4247613006012537501)
XLA Ops:
  0.6 0.0 copy-start.2
  0.6 2.7 %shard_map.104 = bf16[2,32,2,8,640]{4,3,2,1,0:T(8,128)(2,1)} custom-call(s32[6,160]{1,0:T(8,128)} %bitcast.21, f32[6,160]{1,0:T(8,128)} %bitcast.22, bf16[160,1280]{1,0:T(8,128)(2,1)} %rows_ref.1), custom_call_target="tpu_custom_call" | custom-call | flops 209715200 | bytes 2621440 | tf_op jit(solution)/shard_map/pallas_call | solution.py:260
  3.4 25.6 %all-to-all-start = ((bf16[128,8,640]{2,1,0:T(8,128)(2,1)}), bf16[128,8,640]{2,1,0:T(8,128)(2,1)S(1)}, u32[]{:S(2)}, u32[]{:S(2)}) async-start(bf16[128,8,640]{2,1,0:T(8,128)(2,1)} %bitcast.4), calls=%async_computation | async-start | bytes 2621440 | tf_op jit(solution)/shard_map/all_to_all | solution.py:255
  29.0 2.5 %collective-permute-start.1 = (bf16[1280,768]{1,0:T(8,128)(2,1)}, bf16[1280,768]{1,0:T(8,128)(2,1)}, u32[]{:S(2)}, u32[]{:S(2)}) collective-permute-start(bf16[1280,768]{1,0:T(8,128)(2,1)} %bitcast.19), channel_id=1, source_target_pairs={{0,1},{1,0},{2,3},{3,2},{4,5},{5,4},{6,7},{7,6},{8,9},{9,8},{10,11... | collective-permute-start | bytes 5898248 | tf_op jit(solution)/shard_map/ppermute | solution.py:276
  31.5 1.9 %collective-permute-start = (bf16[768,1280]{1,0:T(8,128)(2,1)}, bf16[768,1280]{1,0:T(8,128)(2,1)}, u32[]{:S(2)}, u32[]{:S(2)}) collective-permute-start(bf16[768,1280]{1,0:T(8,128)(2,1)} %bitcast.17), channel_id=1, source_target_pairs={{0,1},{1,0},{2,3},{3,2},{4,5},{5,4},{6,7},{7,6},{8,9},{9,8},{10,11... | collective-permute-start | bytes 5898248 | tf_op jit(solution)/shard_map/ppermute | solution.py:275
  33.4 0.1 pad_add_fusion.core_ref
  33.5 1.0 copy-done.3
  34.5 1.4 %shard_map.106 = (f32[80,768]{1,0:T(8,128)S(1)}, f32[80,768]{1,0:T(8,128)S(1)}) custom-call(s32[2]{0:T(128)S(1)} %pad_add_fusion.core_ref, bf16[160,1280]{1,0:T(8,128)(2,1)S(1)} %copy-done.3, bf16[768,1280]{1,0:T(8,128)(2,1)S(1)} %copy-done.2), custom_call_target="tpu_custom_call" | custom-call | flops 314572800 | bytes 1966080 | tf_op jit(solution)/shard_map/pallas_call | solution.py:220
  35.9 0.0 copy-start.1
  35.9 2.5 %collective-permute-start.2 = (f32[80,768]{1,0:T(8,128)S(1)}, f32[80,768]{1,0:T(8,128)S(1)}, u32[]{:S(2)}, u32[]{:S(2)}) collective-permute-start(f32[80,768]{1,0:T(8,128)S(1)} %get-tuple-element.16), channel_id=1, source_target_pairs={{0,1},{1,0},{2,3},{3,2},{4,5},{5,4},{6,7},{7,6},{8,9},{9,8},{10,11... | collective-permute-start | bytes 737288 | tf_op jit(solution)/shard_map/ppermute | solution.py:228
  38.4 1.1 collective-permute-done.2.pair_ref
  39.6 3.1 %collective-permute-start.3 = (bf16[80,768]{1,0:T(8,128)(2,1)S(1)}, bf16[80,768]{1,0:T(8,128)(2,1)S(1)}, u32[]{:S(2)}, u32[]{:S(2)}) collective-permute-start(bf16[80,768]{1,0:T(8,128)(2,1)S(1)} %add_convert_fusion), channel_id=1, source_target_pairs={{0,2},{1,3},{2,0},{3,1},{4,6},{5,7},{6,4},{7,5},{8,10},{9,11},{10,... | collective-permute-start | bytes 368648 | tf_op jit(solution)/shard_map/ppermute | solution.py:229
  42.7 3.3 %collective-permute-done.3.away_ref = bf16[80,768]{1,0:T(8,128)(2,1)S(1)} collective-permute-done((bf16[80,768]{1,0:T(8,128)(2,1)S(1)}, bf16[80,768]{1,0:T(8,128)(2,1)S(1)}, u32[]{:S(2)}, u32[]{:S(2)}) %collective-permute-start.3) | collective-permute-done | bytes 122912 | tf_op jit(solution)/shard_map/ppermute | solution.py:229
  46.0 0.9 copy-done.7
  46.9 0.6 shard_map.107.mine_ref
  47.5 3.1 %collective-permute-start.4 = (bf16[80,768]{1,0:T(8,128)(2,1)S(1)}, bf16[80,768]{1,0:T(8,128)(2,1)}, u32[]{:S(2)}, u32[]{:S(2)}) collective-permute-start(bf16[80,768]{1,0:T(8,128)(2,1)S(1)} %shard_map.107.mine_ref), channel_id=1, source_target_pairs={{0,1},{1,0},{2,3},{3,2},{4,5},{5,4},{6,7},{7,6},{8,9},{9,8},{10,11... | collective-permute-start | bytes 368648 | tf_op jit(solution)/shard_map/ppermute | solution.py:237
  50.7 0.7 shard_map.105.gate_ref
  51.4 0.0 copy-start.4
  51.4 0.7 copy-done.4
  52.2 0.1 copy.11.ids_ref
  52.3 0.6 shard_map.109.mask_in
  52.9 0.9 copy-done
  53.7 0.0 collective-permute-done.4.other_ref
  53.8 2.5 %shard_map.108 = bf16[160,1280]{1,0:T(8,128)(2,1)} custom-call(s32[2]{0:T(128)S(1)} %pad_add_fusion.core_ref, bf16[80,768]{1,0:T(8,128)(2,1)S(1)} %shard_map.107.mine_ref, bf16[80,768]{1,0:T(8,128)(2,1)} %collective-permute-done.4.other_ref, bf16[1280,768]{1,0:T(8,128)(2,1)S(1)} %copy-done.1), custom_call_target="tpu_custom_call" | custom-call | flops 314572800 | bytes 1966080 | tf_op jit(solution)/shard_map/pallas_call | solution.py:286
  56.2 0.0 collective-permute-done.1.up_other_in
  56.2 0.0 collective-permute-done.other_in
  56.2 9.2 %all-to-all-done = bf16[128,8,640]{2,1,0:T(8,128)(2,1)S(1)} async-done(((bf16[128,8,640]{2,1,0:T(8,128)(2,1)}), bf16[128,8,640]{2,1,0:T(8,128)(2,1)S(1)}, u32[]{:S(2)}, u32[]{:S(2)}) %all-to-all-start) | async-done | bytes 1310752 | tf_op jit(solution)/shard_map/all_to_all | solution.py:255
  65.4 5.3 %shard_map.110 = (f32[256,768]{1,0:T(8,128)S(1)}, bf16[256,768]{1,0:T(8,128)(2,1)S(1)}, bf16[2,1280,768]{2,1,0:T(8,128)(2,1)S(1)}) custom-call(s32[2]{0:T(128)S(1)} %pad_add_fusion.core_ref, bf16[2,64,8,640]{3,2,1,0:T(8,128)(2,1)S(1)} %bitcast.12, bf16[768,1280]{1,0:T(8,128)(2,1)} %bitcast.18, bf16[768,1280]{1,0:T(8,128)(2,1)} %collective-permute-done.other_in, ...), custom_call_target="tpu_custom_call" | custom-call | flops 1006632960 | bytes 7864320 | tf_op jit(solution)/shard_map/pallas_call | solution.py:304
  70.7 10.3 %all-gather = bf16[512,768]{1,0:T(8,128)(2,1)S(1)} all-gather(bf16[256,768]{1,0:T(8,128)(2,1)S(1)} %get-tuple-element.21), channel_id=2, replica_groups={{0,2},{1,3},{4,6},{5,7},{8,10},{9,11},{12,14},{13,15},{16,18},{17,19},{..., dimensions={0}, use_global_device_ids=true | all-gather | bytes 1179648 | tf_op jit(solution)/shard_map/all_gather | solution.py:321
  81.1 2.0 %shard_map.111 = (bf16[2,32,2,8,640]{4,3,2,1,0:T(8,128)(2,1)S(1)}, bf16[320,1024]{1,0:T(8,128)(2,1)S(1)}) custom-call(s32[2]{0:T(128)S(1)} %pad_add_fusion.core_ref, f32[256,768]{1,0:T(8,128)S(1)} %get-tuple-element.20.keep_ref, bf16[2,256,768]{2,1,0:T(8,128)(2,1)S(1)} %bitcast.14, bf16[256,768]{1,0:T(8,128)(2,1)S(1)} %copy-done.5, ...), custom_call_target="tpu_custom_call" | custom-call | flops 1006632960 | bytes 3932160 | tf_op jit(solution)/shard_map/pallas_call | solution.py:322
  83.1 44.4 %all_to_all.10 = bf16[128,8,640]{2,1,0:T(8,128)(2,1)S(1)} all-to-all(bf16[128,8,640]{2,1,0:T(8,128)(2,1)S(1)} %bitcast.15), channel_id=1, replica_groups={{0,4,8,12,16,20,24,28,32,36,40,44,48,52,56,60,64,68,72,76,80,84,88,92,9..., dimensions={0} | all-to-all | bytes 2621440 | tf_op jit(solution)/shard_map/all_to_all | solution.py:255
  127.4 1.4 %shard_map.112 = bf16[160,1280]{1,0:T(8,128)(2,1)} custom-call(bf16[320,1024]{1,0:T(8,128)(2,1)S(1)} %get-tuple-element.25.mask_ref, bf16[1024,640]{1,0:T(8,128)(2,1)S(1)} %bitcast.13), custom_call_target="tpu_custom_call" | custom-call | flops 419430400 | bytes 1310720 | tf_op jit(solution)/shard_map/pallas_call | solution.py:334
  (12 shorter events, 0.0 us)
Async XLA Ops:
  0.6 32.8 %copy-start.2 = (bf16[768,1280]{1,0:T(8,128)(2,1)S(1)}, bf16[768,1280]{1,0:T(8,128)(2,1)}, u32[]{:S(2)}) copy-start(bf16[768,1280]{1,0:T(8,128)(2,1)} %w_ref.2) | copy-start | bytes 5898244
  3.4 62.0 %all-to-all-start = ((bf16[128,8,640]{2,1,0:T(8,128)(2,1)}), bf16[128,8,640]{2,1,0:T(8,128)(2,1)S(1)}, u32[]{:S(2)}, u32[]{:S(2)}) async-start(bf16[128,8,640]{2,1,0:T(8,128)(2,1)} %bitcast.4), calls=%async_computation | async-start | bytes 2621440 | tf_op jit(solution)/shard_map/all_to_all | solution.py:255
  29.0 27.3 %collective-permute-start.1 = (bf16[1280,768]{1,0:T(8,128)(2,1)}, bf16[1280,768]{1,0:T(8,128)(2,1)}, u32[]{:S(2)}, u32[]{:S(2)}) collective-permute-start(bf16[1280,768]{1,0:T(8,128)(2,1)} %bitcast.19), channel_id=1, source_target_pairs={{0,1},{1,0},{2,3},{3,2},{4,5},{5,4},{6,7},{7,6},{8,9},{9,8},{10,11... | collective-permute-start | bytes 5898248 | tf_op jit(solution)/shard_map/ppermute | solution.py:276
  31.5 24.8 %collective-permute-start = (bf16[768,1280]{1,0:T(8,128)(2,1)}, bf16[768,1280]{1,0:T(8,128)(2,1)}, u32[]{:S(2)}, u32[]{:S(2)}) collective-permute-start(bf16[768,1280]{1,0:T(8,128)(2,1)} %bitcast.17), channel_id=1, source_target_pairs={{0,1},{1,0},{2,3},{3,2},{4,5},{5,4},{6,7},{7,6},{8,9},{9,8},{10,11... | collective-permute-start | bytes 5898248 | tf_op jit(solution)/shard_map/ppermute | solution.py:275
  33.5 1.0 copy-start.3
  34.5 16.2 %copy-start.6 = (bf16[1,1,512,768]{3,2,1,0:T(8,128)(2,1)S(1)}, bf16[1,1,512,768]{3,2,1,0:T(8,128)(2,1)}, u32[]{:S(2)}) copy-start(bf16[1,1,512,768]{3,2,1,0:T(8,128)(2,1)} %param.12) | copy-start | bytes 2359300
  34.5 17.7 %copy-start.8 = (s32[160,6]{0,1:T(8,128)S(1)}, s32[160,6]{0,1:T(8,128)}, u32[]{:S(2)}) copy-start(s32[160,6]{0,1:T(8,128)} %param.10) | copy-start | bytes 11524
  35.9 17.9 %copy-start.1 = (bf16[1280,768]{1,0:T(8,128)(2,1)S(1)}, bf16[1280,768]{1,0:T(8,128)(2,1)}, u32[]{:S(2)}) copy-start(bf16[1280,768]{1,0:T(8,128)(2,1)} %w_ref.3) | copy-start | bytes 5898244
  35.9 3.7 %collective-permute-start.2 = (f32[80,768]{1,0:T(8,128)S(1)}, f32[80,768]{1,0:T(8,128)S(1)}, u32[]{:S(2)}, u32[]{:S(2)}) collective-permute-start(f32[80,768]{1,0:T(8,128)S(1)} %get-tuple-element.16), channel_id=1, source_target_pairs={{0,1},{1,0},{2,3},{3,2},{4,5},{5,4},{6,7},{7,6},{8,9},{9,8},{10,11... | collective-permute-start | bytes 737288 | tf_op jit(solution)/shard_map/ppermute | solution.py:228
  39.6 6.4 %collective-permute-start.3 = (bf16[80,768]{1,0:T(8,128)(2,1)S(1)}, bf16[80,768]{1,0:T(8,128)(2,1)S(1)}, u32[]{:S(2)}, u32[]{:S(2)}) collective-permute-start(bf16[80,768]{1,0:T(8,128)(2,1)S(1)} %add_convert_fusion), channel_id=1, source_target_pairs={{0,2},{1,3},{2,0},{3,1},{4,6},{5,7},{6,4},{7,5},{8,10},{9,11},{10,... | collective-permute-start | bytes 368648 | tf_op jit(solution)/shard_map/ppermute | solution.py:229
  46.0 0.9 copy-start.7
  47.5 6.2 %collective-permute-start.4 = (bf16[80,768]{1,0:T(8,128)(2,1)S(1)}, bf16[80,768]{1,0:T(8,128)(2,1)}, u32[]{:S(2)}, u32[]{:S(2)}) collective-permute-start(bf16[80,768]{1,0:T(8,128)(2,1)S(1)} %shard_map.107.mine_ref), channel_id=1, source_target_pairs={{0,1},{1,0},{2,3},{3,2},{4,5},{5,4},{6,7},{7,6},{8,9},{9,8},{10,11... | collective-permute-start | bytes 368648 | tf_op jit(solution)/shard_map/ppermute | solution.py:237
  51.4 0.7 copy-start.4
  52.9 0.9 copy-start
  65.4 15.7 %copy-start.5 = (bf16[256,768]{1,0:T(8,128)(2,1)S(1)}, bf16[256,768]{1,0:T(8,128)(2,1)}, u32[]{:S(2)}) copy-start(bf16[256,768]{1,0:T(8,128)(2,1)} %copy-done.4) | copy-start | bytes 1179652

commit v6 on v4

--- a/solution.py
+++ b/solution.py
@@ -10,13 +10,13 @@
 TOP = 6
 CAP = 8
 CORES = 2
+CUTS = 2
 HELD = CAP // CORES
 CORE_SWAP = [(0, 1), (1, 0), (2, 3), (3, 2)]
 CHIP_SWAP = [(0, 2), (1, 3), (2, 0), (3, 1)]
 F32, BF16 = jnp.float32, jnp.bfloat16
 WHOLE = pl.BlockSpec(memory_space=pltpu.VMEM)
 FAR = pl.BlockSpec(memory_space=pltpu.HBM)
-ANY = pl.BlockSpec(memory_space=pl.ANY)
 SCALAR = pl.BlockSpec(memory_space=pltpu.SMEM)
 
 
@@ -24,12 +24,12 @@
     return lax.dot_general(a, b, (dims, ((), ())), preferred_element_type=F32)
 
 
-def call(body, outs, specs, scratch=(), flops=0, moved=0):
+def call(body, outs, specs, scratch=(), flops=0, moved=0, place=WHOLE):
     return pl.pallas_call(
         body,
         out_shape=outs,
         in_specs=specs,
-        out_specs=jax.tree.map(lambda _: WHOLE, outs),
+        out_specs=jax.tree.map(lambda _: place, outs),
         scratch_shapes=list(scratch),
         compiler_params=pltpu.CompilerParams(vmem_limit_bytes=12 << 20),
         cost_estimate=pl.CostEstimate(flops=flops, bytes_accessed=moved, transcendentals=0),
@@ -51,7 +51,9 @@
     return jnp.where(low, pltpu.roll(even, HELD, 1), odd)
 
 
-def route_body(ids_in, prob_in, grad_in, sent_ref, ids_ref, prob_ref, grad_ref, sems, *, experts):
+def route_body(
+    ids_in, prob_in, grad_in, sent_out, ids_ref, prob_ref, grad_ref, sent_ref, sems, *, experts
+):
     tokens, quarter = grad_ref.shape
     loads = [
         pltpu.make_async_copy(source, target, sems.at[index])
@@ -86,6 +88,10 @@
     rank, prob = spread(rank), spread(prob)
     slot = lax.rem(lax.broadcasted_iota(jnp.int32, shape, 1), HELD).astype(F32)
     loads[2].wait()
+    stores = [
+        pltpu.make_async_copy(sent_ref.at[core], sent_out.at[core], sems.at[3 + core])
+        for core in range(CORES)
+    ]
     for core in range(CORES):
         hit = rank == slot + float(core * HELD)
         scale = jnp.sum(jnp.where(hit, prob, 0.0), axis=2, keepdims=True)
@@ -94,15 +100,22 @@
         right = dot(mask, grad_ref[:, half:], ((1,), (0,))).reshape(pairs, CAP, half) * scale
         sent_ref[core, :, 0] = pack(left, right, 0).astype(BF16)
         sent_ref[core, :, 1] = pack(left, right, 1).astype(BF16)
-
-
-def prepare_body(ids_ref, after_ref, mine_in, other_in, mask_ref, w_ref, sems, *, experts):
+        stores[core].start()
+    for store in stores:
+        store.wait()
+
+
+def prepare_body(
+    ids_ref, keep_ref, away_ref, gate_ref, mine_in, other_in, up_ref, mask_ref, w_ref, sems, *, experts
+):
     loads = [
         pltpu.make_async_copy(source, w_ref.at[index], sems.at[index])
         for index, source in enumerate((mine_in, other_in))
     ]
     for load in loads:
         load.start()
+    hidden = keep_ref[...] + away_ref[...].astype(F32)
+    up_ref[...] = (hidden * gate_ref[:, : up_ref.shape[1]].astype(F32)).astype(BF16)
     tokens = ids_ref.shape[0]
     expert = lax.broadcasted_iota(jnp.int32, (tokens, experts), 1)
     named = jnp.zeros((tokens, experts), F32)
@@ -136,31 +149,34 @@
     out_ref[...] = chosen.reshape(out_ref.shape).astype(BF16)
 
 
-def hidden_body(core_ref, rows_ref, mine_in, other_in, keep_ref, send_ref, w_ref, sems):
+def hidden_body(core_ref, rows_ref, mine_in, other_in, keep_ref, send_ref, w_ref, sems, *, first):
+    count, half = keep_ref.shape[1], rows_ref.shape[-1]
     loads = [
-        pltpu.make_async_copy(source, w_ref.at[index], sems.at[index])
+        pltpu.make_async_copy(source.at[pl.ds(first, count), :], w_ref.at[index], sems.at[index])
         for index, source in enumerate((mine_in, other_in))
     ]
     for load in loads:
         load.start()
+    parts = []
+    for lane in (core_ref[0], 1 - core_ref[0]):
+        rows = rows_ref[lane].astype(F32).reshape(-1, 2, CAP, half)
+        for side in range(2):
+            parts.append(pack(rows[:, 0], rows[:, 1], side).reshape(-1, half).astype(BF16))
     total = None
-    for index, lane in enumerate((core_ref[0], 1 - core_ref[0])):
-        rows = rows_ref[lane].astype(F32)
-        half = rows.shape[-1]
-        rows = rows.reshape(-1, 2, CAP, half)
-        parts = [pack(rows[:, 0], rows[:, 1], side).reshape(-1, half).astype(BF16) for side in range(2)]
-        loads[index].wait()
-        for side, part in enumerate(parts):
-            term = dot(part, w_ref[index, :, side * half : (side + 1) * half])
+    for index, load in enumerate(loads):
+        load.wait()
+        for side in range(2):
+            term = dot(parts[2 * index + side], w_ref[index, :, side * half : (side + 1) * half])
             total = term if total is None else total + term
     keep_ref[...] = total
     send_ref[...] = total.astype(BF16)
 
 
-def slot_grad_body(core_ref, keep_ref, away_ref, gate_ref, w_ref, mask_in, out_ref):
+def slot_grad_body(core_ref, first_ref, keep_ref, away_ref, gate_ref, w_ref, out_ref):
+    units, half = first_ref.shape[1], out_ref.shape[-1]
     hidden = keep_ref[...] + away_ref[...].astype(F32)
-    up = (hidden * gate_ref[...].astype(F32)).astype(BF16)
-    half = out_ref.shape[-1]
+    last = (hidden * gate_ref[:, units:].astype(F32)).astype(BF16)
+    up = jnp.concatenate([first_ref[...], last], axis=1)
     for index, lane in enumerate((core_ref[0], 1 - core_ref[0])):
         left = dot(up, w_ref[index, :half, :]).reshape(-1, CAP, half)
         right = dot(up, w_ref[index, half:, :]).reshape(-1, CAP, half)
@@ -244,9 +260,13 @@
         jax.ShapeDtypeStruct((CORES, experts // 2, 2, CAP, half), BF16),
         [FAR] * 3,
         [pltpu.VMEM(array.shape, array.dtype) for array in (ids, probs, grad_out)]
-        + [pltpu.SemaphoreType.DMA((3,))],
+        + [
+            pltpu.VMEM((CORES, experts // 2, 2, CAP, half), BF16),
+            pltpu.SemaphoreType.DMA((3 + CORES,)),
+        ],
         flops=2 * slots * tokens * quarter,
         moved=4 * slots * quarter,
+        place=FAR,
     )(*far(ids, probs, grad_out))
     arrived = exchange(sent)
 
@@ -272,33 +292,39 @@
         (expert_ids, arrived, down_other, up_other, gate, shared_grad)
     )
     work = 4 * held * quarter * width
-    keep, send = call(
-        hidden_body,
-        (jax.ShapeDtypeStruct(gate.shape, F32), jax.ShapeDtypeStruct(gate.shape, BF16)),
-        [SCALAR, WHOLE, FAR, FAR],
-        [pltpu.VMEM((CORES, width, quarter), BF16), pltpu.SemaphoreType.DMA((CORES,))],
-        flops=work,
-        moved=4 * quarter * width,
-    )(core, arrived.reshape(CORES, experts, CAP, half), *far(w_down[0], down_other))
-    away = lax.ppermute(send, "tensor", CHIP_SWAP)
-    mask, w_both = call(
+    units = width // CUTS
+    rows = arrived.reshape(CORES, experts, CAP, half)
+    keeps, aways = [], []
+    for cut in range(CUTS):
+        keep, send = call(
+            functools.partial(hidden_body, first=cut * units),
+            (jax.ShapeDtypeStruct((held, units), F32), jax.ShapeDtypeStruct((held, units), BF16)),
+            [SCALAR, WHOLE, FAR, FAR],
+            [pltpu.VMEM((CORES, units, quarter), BF16), pltpu.SemaphoreType.DMA((CORES,))],
+            flops=work // CUTS,
+            moved=4 * quarter * units,
+        )(core, rows, *far(w_down[0], down_other))
+        keeps.append(keep)
+        aways.append(lax.ppermute(send, "tensor", CHIP_SWAP))
+    first, mask, w_both = call(
         functools.partial(prepare_body, experts=experts),
         (
+            jax.ShapeDtypeStruct((held, units), BF16),
             jax.ShapeDtypeStruct((2 * tokens, CORES * slots), BF16),
             jax.ShapeDtypeStruct((CORES, quarter, width), BF16),
         ),
-        [WHOLE, ANY, FAR, FAR],
+        [WHOLE] * 4 + [FAR] * 2,
         [pltpu.SemaphoreType.DMA((CORES,))],
         flops=2 * tokens * slots * experts,
         moved=4 * quarter * width,
-    )(ids, keep, *far(w_up[0], up_other))
+    )(ids, keeps[0], aways[0], gate, *far(w_up[0], up_other))
     slot_grad = call(
         slot_grad_body,
         jax.ShapeDtypeStruct((CORES, experts // 2, 2, CAP, half), BF16),
-        [SCALAR] + [WHOLE] * 4 + [ANY],
+        [SCALAR] + [WHOLE] * 5,
         flops=work,
         moved=4 * quarter * width,
-    )(core, keep, away, gate, w_both, mask)
+    )(core, first, keeps[1], aways[1], gate, w_both)
     back = exchange(slot_grad)
     moe_grad = call(
         combine_body,

time: 129 us -> 129 us (level)
  waiting for transfers between devices: 25.6 us -> 22 us
  starting transfers between devices: 42 us -> 44.2 us
    ppermute x1 -> x2, waiting for transfers between devices: 6.13 us -> 2.56 us  [on_device(): aways.append(lax.ppermute(send, 'tensor', CHIP_SWAP))]
    ppermute x1 -> x2, starting transfers between devices: 3.12 us -> 5.28 us  [on_device(): aways.append(lax.ppermute(send, 'tensor', CHIP_SWAP))]
    pallas_call x1 -> x2, Pallas kernels: 3.56 us -> 4.82 us  [on_device(): call(functools.partial(hidden_body, first=cut * units), (jax.ShapeDtypeSt...]
  transfers between devices with their start and end apart: 7 -> 8, of which waited for: 5 -> 5; matrix products, arithmetic and copies ran while one was open for 0% -> 0% of each run, Pallas kernels for 4% -> 6%
where the time goes in v6:
time: 129 us; the launch traced here: 128 us
  blocking collectives  44.7 us (35%)
  starting transfers between devices  44.2 us (34%)
  waiting for transfers between devices  22 us (17%)
  Pallas kernels  15.3 us (12%)
    all_to_all x1, blocking collectives, exchange(): lax.all_to_all(rows, ('expert', 'tensor'), 0, 0, axis_index_groups=groups...  44.7 us
    all_to_all x1, starting transfers between devices, exchange(): lax.all_to_all(rows, ('expert', 'tensor'), 0, 0, axis_index_groups=groups...  25.7 us
    all_to_all x1, waiting for transfers between devices, exchange(): lax.all_to_all(rows, ('expert', 'tensor'), 0, 0, axis_index_groups=groups...  14.3 us
    ppermute x2, starting transfers between devices, on_device(): aways.append(lax.ppermute(send, 'tensor', CHIP_SWAP))  5.28 us
    pallas_call x2, Pallas kernels, on_device(): call(functools.partial(hidden_body, first=cut * units), (jax.ShapeDtypeSt...  4.82 us
    ppermute x1, waiting for transfers between devices, dense_up_grad(): away = lax.ppermute((mine + pair).astype(BF16), 'tensor', CHIP_SWAP)  3.3 us
    ppermute x1, starting transfers between devices, dense_up_grad(): away = lax.ppermute((mine + pair).astype(BF16), 'tensor', CHIP_SWAP)  3.12 us
    ppermute x1, starting transfers between devices, dense_up_grad(): return (up, lax.ppermute(up, 'tensor', CORE_SWAP))  3.1 us
  transfers between devices with their start and end apart: 8, of which 5 were waited for; matrix products, arithmetic and copies ran while one was open for 0% of the time, Pallas kernels for 6%

profile of v6, /device:TPU:1, one launch (start us, length us, event | category | flops | bytes accessed | tf_op | source)
XLA Modules:
  0.0 128.1 jit_solution(14441980834211080547)
XLA Ops:
  0.6 2.7 %shard_map.104 = bf16[2,32,2,8,640]{4,3,2,1,0:T(8,128)(2,1)} custom-call(s32[6,160]{1,0:T(8,128)} %bitcast.20, f32[6,160]{1,0:T(8,128)} %bitcast.21, bf16[160,1280]{1,0:T(8,128)(2,1)} %rows_ref.1), custom_call_target="tpu_custom_call" | custom-call | flops 209715200 | bytes 2621440 | tf_op jit(solution)/shard_map/pallas_call | solution.py:258
  3.4 0.0 copy-start.4
  3.4 25.7 %all-to-all-start = ((bf16[128,8,640]{2,1,0:T(8,128)(2,1)}), bf16[128,8,640]{2,1,0:T(8,128)(2,1)S(1)}, u32[]{:S(2)}, u32[]{:S(2)}) async-start(bf16[128,8,640]{2,1,0:T(8,128)(2,1)} %bitcast.2), calls=%async_computation | async-start | bytes 2621440 | tf_op jit(solution)/shard_map/all_to_all | solution.py:253
  29.1 2.5 %collective-permute-start.1 = (bf16[1280,768]{1,0:T(8,128)(2,1)}, bf16[1280,768]{1,0:T(8,128)(2,1)}, u32[]{:S(2)}, u32[]{:S(2)}) collective-permute-start(bf16[1280,768]{1,0:T(8,128)(2,1)} %bitcast.18), channel_id=1, source_target_pairs={{0,1},{1,0},{2,3},{3,2},{4,5},{5,4},{6,7},{7,6},{8,9},{9,8},{10,11... | collective-permute-start | bytes 5898248 | tf_op jit(solution)/shard_map/ppermute | solution.py:274
  31.6 1.9 %collective-permute-start = (bf16[768,1280]{1,0:T(8,128)(2,1)}, bf16[768,1280]{1,0:T(8,128)(2,1)}, u32[]{:S(2)}, u32[]{:S(2)}) collective-permute-start(bf16[768,1280]{1,0:T(8,128)(2,1)} %bitcast.15), channel_id=1, source_target_pairs={{0,1},{1,0},{2,3},{3,2},{4,5},{5,4},{6,7},{7,6},{8,9},{9,8},{10,11... | collective-permute-start | bytes 5898248 | tf_op jit(solution)/shard_map/ppermute | solution.py:273
  33.6 0.0 copy-start.2
  33.6 1.0 copy-done.2
  34.6 0.8 shard_map.106
  35.4 0.0 copy-start
  35.4 2.5 %collective-permute-start.2 = (f32[80,768]{1,0:T(8,128)S(1)}, f32[80,768]{1,0:T(8,128)S(1)}, u32[]{:S(2)}, u32[]{:S(2)}) collective-permute-start(f32[80,768]{1,0:T(8,128)S(1)} %get-tuple-element.18), channel_id=1, source_target_pairs={{0,1},{1,0},{2,3},{3,2},{4,5},{5,4},{6,7},{7,6},{8,9},{9,8},{10,11... | collective-permute-start | bytes 737288 | tf_op jit(solution)/shard_map/ppermute | solution.py:227
  38.0 1.1 collective-permute-done.2.pair_ref
  39.1 3.1 %collective-permute-start.3 = (bf16[80,768]{1,0:T(8,128)(2,1)S(1)}, bf16[80,768]{1,0:T(8,128)(2,1)S(1)}, u32[]{:S(2)}, u32[]{:S(2)}) collective-permute-start(bf16[80,768]{1,0:T(8,128)(2,1)S(1)} %add_convert_fusion), channel_id=1, source_target_pairs={{0,2},{1,3},{2,0},{3,1},{4,6},{5,7},{6,4},{7,5},{8,10},{9,11},{10,... | collective-permute-start | bytes 368648 | tf_op jit(solution)/shard_map/ppermute | solution.py:228
  42.2 3.3 %collective-permute-done.3.away_ref = bf16[80,768]{1,0:T(8,128)(2,1)S(1)} collective-permute-done((bf16[80,768]{1,0:T(8,128)(2,1)S(1)}, bf16[80,768]{1,0:T(8,128)(2,1)S(1)}, u32[]{:S(2)}, u32[]{:S(2)}) %collective-permute-start.3) | collective-permute-done | bytes 122912 | tf_op jit(solution)/shard_map/ppermute | solution.py:228
  45.5 0.1 shard_map.107.mine_ref
  45.6 3.1 %collective-permute-start.4 = (bf16[80,768]{1,0:T(8,128)(2,1)S(1)}, bf16[80,768]{1,0:T(8,128)(2,1)S(1)}, u32[]{:S(2)}, u32[]{:S(2)}) collective-permute-start(bf16[80,768]{1,0:T(8,128)(2,1)S(1)} %shard_map.107.mine_ref), channel_id=1, source_target_pairs={{0,1},{1,0},{2,3},{3,2},{4,5},{5,4},{6,7},{7,6},{8,9},{9,8},{10,11... | collective-permute-start | bytes 368648 | tf_op jit(solution)/shard_map/ppermute | solution.py:236
  48.7 0.2 shard_map.105.gate_ref
  48.9 0.7 collective-permute-done.4.other_ref
  49.7 1.6 %shard_map.108 = bf16[160,1280]{1,0:T(8,128)(2,1)} custom-call(s32[1]{0:T(128)} %bitcast.5.core_ref, bf16[80,768]{1,0:T(8,128)(2,1)S(1)} %shard_map.107.mine_ref, bf16[80,768]{1,0:T(8,128)(2,1)S(1)} %collective-permute-done.4.other_ref, bf16[1280,768]{1,0:T(8,128)(2,1)S(1)} %copy-done), custom_call_target="tpu_custom_call" | custom-call | flops 314572800 | bytes 1966080 | tf_op jit(solution)/shard_map/pallas_call | solution.py:284
  51.3 0.0 collective-permute-done.1.other_in
  51.3 0.0 collective-permute-done.other_in
  51.3 14.3 %all-to-all-done = bf16[128,8,640]{2,1,0:T(8,128)(2,1)S(1)} async-done(((bf16[128,8,640]{2,1,0:T(8,128)(2,1)}), bf16[128,8,640]{2,1,0:T(8,128)(2,1)S(1)}, u32[]{:S(2)}, u32[]{:S(2)}) %all-to-all-start) | async-done | bytes 1310752 | tf_op jit(solution)/shard_map/all_to_all | solution.py:253
  65.6 2.4 %shard_map.109 = (f32[256,384]{1,0:T(8,128)S(1)}, bf16[256,384]{1,0:T(8,128)(2,1)S(1)}) custom-call(s32[1]{0:T(128)} %bitcast.5.core_ref, bf16[2,64,8,640]{3,2,1,0:T(8,128)(2,1)S(1)} %bitcast.10, bf16[768,1280]{1,0:T(8,128)(2,1)} %bitcast.16, bf16[768,1280]{1,0:T(8,128)(2,1)} %collective-permute-done.other_in), custom_call_target="tpu_custom_call" | custom-call | flops 503316480 | bytes 1966080 | tf_op jit(solution)/shard_map/pallas_call | solution.py:299
  68.0 0.0 copy-start.5
  68.0 3.1 %collective-permute-start.5 = (bf16[256,384]{1,0:T(8,128)(2,1)S(1)}, bf16[256,384]{1,0:T(8,128)(2,1)S(1)}, u32[]{:S(2)}, u32[]{:S(2)}) collective-permute-start(bf16[256,384]{1,0:T(8,128)(2,1)S(1)} %get-tuple-element.23), channel_id=1, source_target_pairs={{0,2},{1,3},{2,0},{3,1},{4,6},{5,7},{6,4},{7,5},{8,10},{9,11},{10,... | collective-permute-start | bytes 589832 | tf_op jit(solution)/shard_map/ppermute | solution.py:308
  71.1 2.4 %shard_map.111 = (f32[256,384]{1,0:T(8,128)S(1)}, bf16[256,384]{1,0:T(8,128)(2,1)S(1)}) custom-call(s32[1]{0:T(128)} %bitcast.5.core_ref, bf16[2,64,8,640]{3,2,1,0:T(8,128)(2,1)S(1)} %bitcast.11, bf16[768,1280]{1,0:T(8,128)(2,1)} %bitcast.17, bf16[768,1280]{1,0:T(8,128)(2,1)} %collective-permute-done.other_in), custom_call_target="tpu_custom_call" | custom-call | flops 503316480 | bytes 1966080 | tf_op jit(solution)/shard_map/pallas_call | solution.py:299
  73.5 2.2 %collective-permute-start.6 = (bf16[256,384]{1,0:T(8,128)(2,1)S(1)}, bf16[256,384]{1,0:T(8,128)(2,1)S(1)}, u32[]{:S(2)}, u32[]{:S(2)}) collective-permute-start(bf16[256,384]{1,0:T(8,128)(2,1)S(1)} %get-tuple-element.29), channel_id=1, source_target_pairs={{0,2},{1,3},{2,0},{3,1},{4,6},{5,7},{6,4},{7,5},{8,10},{9,11},{10,... | collective-permute-start | bytes 589832 | tf_op jit(solution)/shard_map/ppermute | solution.py:308
  75.7 0.1 copy.11.ids_ref
  75.8 2.2 %shard_map.110 = (bf16[256,384]{1,0:T(8,128)(2,1)S(1)}, bf16[320,1024]{1,0:T(8,128)(2,1)S(1)}, bf16[2,1280,768]{2,1,0:T(8,128)(2,1)S(1)}) custom-call(s32[160,6]{1,0:T(8,128)S(1)} %copy.11.ids_ref, f32[256,384]{1,0:T(8,128)S(1)} %get-tuple-element.22.keep_ref, bf16[256,384]{1,0:T(8,128)(2,1)S(1)} %collective-permute-done.5.away_ref, ...), custom_call_target="tpu_custom_call" | custom-call | flops 10485760 | bytes 3932160 | tf_op jit(solution)/shard_map/pallas_call | solution.py:309
  78.0 2.6 %collective-permute-done.6.away_ref = bf16[256,384]{1,0:T(8,128)(2,1)S(1)} collective-permute-done((bf16[256,384]{1,0:T(8,128)(2,1)S(1)}, bf16[256,384]{1,0:T(8,128)(2,1)S(1)}, u32[]{:S(2)}, u32[]{:S(2)}) %collective-permute-start.6) | collective-permute-done | bytes 196640 | tf_op jit(solution)/shard_map/ppermute | solution.py:308
  80.6 1.4 %shard_map.112 = bf16[2,32,2,8,640]{4,3,2,1,0:T(8,128)(2,1)S(1)} custom-call(s32[1]{0:T(128)} %bitcast.5.core_ref, bf16[256,384]{1,0:T(8,128)(2,1)S(1)} %get-tuple-element.27.first_ref, f32[256,384]{1,0:T(8,128)S(1)} %get-tuple-element.28.keep_ref, bf16[256,384]{1,0:T(8,128)(2,1)S(1)} %collective-permute-done.6.away_ref, ...), custom_call_target="tpu_custom_call" | custom-call | flops 1006632960 | bytes 3932160 | tf_op jit(solution)/shard_map/pallas_call | solution.py:321
  82.0 44.7 %all_to_all.10 = bf16[128,8,640]{2,1,0:T(8,128)(2,1)S(1)} all-to-all(bf16[128,8,640]{2,1,0:T(8,128)(2,1)S(1)} %bitcast.12), channel_id=1, replica_groups={{0,4,8,12,16,20,24,28,32,36,40,44,48,52,56,60,64,68,72,76,80,84,88,92,9..., dimensions={0} | all-to-all | bytes 2621440 | tf_op jit(solution)/shard_map/all_to_all | solution.py:253
  126.7 1.4 %shard_map.113 = bf16[160,1280]{1,0:T(8,128)(2,1)} custom-call(bf16[320,1024]{1,0:T(8,128)(2,1)S(1)} %get-tuple-element.26.mask_ref, bf16[1024,640]{1,0:T(8,128)(2,1)S(1)} %bitcast.13), custom_call_target="tpu_custom_call" | custom-call | flops 419430400 | bytes 1310720 | tf_op jit(solution)/shard_map/pallas_call | solution.py:329
  (9 shorter events, 0.0 us)
Async XLA Ops:
  0.6 32.9 %copy-start.1 = (bf16[768,1280]{1,0:T(8,128)(2,1)S(1)}, bf16[768,1280]{1,0:T(8,128)(2,1)}, u32[]{:S(2)}) copy-start(bf16[768,1280]{1,0:T(8,128)(2,1)} %w_ref.2) | copy-start | bytes 5898244
  3.4 42.1 %copy-start.4 = (bf16[160,768]{1,0:T(8,128)(2,1)S(1)}, bf16[160,768]{1,0:T(8,128)(2,1)}, u32[]{:S(2)}) copy-start(bf16[160,768]{1,0:T(8,128)(2,1)} %gate_ref.1) | copy-start | bytes 737284
  3.4 62.2 %all-to-all-start = ((bf16[128,8,640]{2,1,0:T(8,128)(2,1)}), bf16[128,8,640]{2,1,0:T(8,128)(2,1)S(1)}, u32[]{:S(2)}, u32[]{:S(2)}) async-start(bf16[128,8,640]{2,1,0:T(8,128)(2,1)} %bitcast.2), calls=%async_computation | async-start | bytes 2621440 | tf_op jit(solution)/shard_map/all_to_all | solution.py:253
  29.1 22.1 %collective-permute-start.1 = (bf16[1280,768]{1,0:T(8,128)(2,1)}, bf16[1280,768]{1,0:T(8,128)(2,1)}, u32[]{:S(2)}, u32[]{:S(2)}) collective-permute-start(bf16[1280,768]{1,0:T(8,128)(2,1)} %bitcast.18), channel_id=1, source_target_pairs={{0,1},{1,0},{2,3},{3,2},{4,5},{5,4},{6,7},{7,6},{8,9},{9,8},{10,11... | collective-permute-start | bytes 5898248 | tf_op jit(solution)/shard_map/ppermute | solution.py:274
  31.6 19.7 %collective-permute-start = (bf16[768,1280]{1,0:T(8,128)(2,1)}, bf16[768,1280]{1,0:T(8,128)(2,1)}, u32[]{:S(2)}, u32[]{:S(2)}) collective-permute-start(bf16[768,1280]{1,0:T(8,128)(2,1)} %bitcast.15), channel_id=1, source_target_pairs={{0,1},{1,0},{2,3},{3,2},{4,5},{5,4},{6,7},{7,6},{8,9},{9,8},{10,11... | collective-permute-start | bytes 5898248 | tf_op jit(solution)/shard_map/ppermute | solution.py:273
  33.6 1.0 copy-start.2
  34.6 14.2 %copy-start.3 = (bf16[1,1,512,768]{3,2,1,0:T(8,128)(2,1)S(1)}, bf16[1,1,512,768]{3,2,1,0:T(8,128)(2,1)}, u32[]{:S(2)}) copy-start(bf16[1,1,512,768]{3,2,1,0:T(8,128)(2,1)} %param.12) | copy-start | bytes 2359300
  35.4 14.3 %copy-start = (bf16[1280,768]{1,0:T(8,128)(2,1)S(1)}, bf16[1280,768]{1,0:T(8,128)(2,1)}, u32[]{:S(2)}) copy-start(bf16[1280,768]{1,0:T(8,128)(2,1)} %w_ref.3) | copy-start | bytes 5898244
  35.4 3.7 %collective-permute-start.2 = (f32[80,768]{1,0:T(8,128)S(1)}, f32[80,768]{1,0:T(8,128)S(1)}, u32[]{:S(2)}, u32[]{:S(2)}) collective-permute-start(f32[80,768]{1,0:T(8,128)S(1)} %get-tuple-element.18), channel_id=1, source_target_pairs={{0,1},{1,0},{2,3},{3,2},{4,5},{5,4},{6,7},{7,6},{8,9},{9,8},{10,11... | collective-permute-start | bytes 737288 | tf_op jit(solution)/shard_map/ppermute | solution.py:227
  39.1 6.4 %collective-permute-start.3 = (bf16[80,768]{1,0:T(8,128)(2,1)S(1)}, bf16[80,768]{1,0:T(8,128)(2,1)S(1)}, u32[]{:S(2)}, u32[]{:S(2)}) collective-permute-start(bf16[80,768]{1,0:T(8,128)(2,1)S(1)} %add_convert_fusion), channel_id=1, source_target_pairs={{0,2},{1,3},{2,0},{3,1},{4,6},{5,7},{6,4},{7,5},{8,10},{9,11},{10,... | collective-permute-start | bytes 368648 | tf_op jit(solution)/shard_map/ppermute | solution.py:228
  45.6 4.1 %collective-permute-start.4 = (bf16[80,768]{1,0:T(8,128)(2,1)S(1)}, bf16[80,768]{1,0:T(8,128)(2,1)S(1)}, u32[]{:S(2)}, u32[]{:S(2)}) collective-permute-start(bf16[80,768]{1,0:T(8,128)(2,1)S(1)} %shard_map.107.mine_ref), channel_id=1, source_target_pairs={{0,1},{1,0},{2,3},{3,2},{4,5},{5,4},{6,7},{7,6},{8,9},{9,8},{10,11... | collective-permute-start | bytes 368648 | tf_op jit(solution)/shard_map/ppermute | solution.py:236
  68.0 7.7 %copy-start.5 = (s32[160,6]{0,1:T(8,128)S(1)}, s32[160,6]{0,1:T(8,128)}, u32[]{:S(2)}) copy-start(s32[160,6]{0,1:T(8,128)} %param.10) | copy-start | bytes 11524
  68.0 7.8 %collective-permute-start.5 = (bf16[256,384]{1,0:T(8,128)(2,1)S(1)}, bf16[256,384]{1,0:T(8,128)(2,1)S(1)}, u32[]{:S(2)}, u32[]{:S(2)}) collective-permute-start(bf16[256,384]{1,0:T(8,128)(2,1)S(1)} %get-tuple-element.23), channel_id=1, source_target_pairs={{0,2},{1,3},{2,0},{3,1},{4,6},{5,7},{6,4},{7,5},{8,10},{9,11},{10,... | collective-permute-start | bytes 589832 | tf_op jit(solution)/shard_map/ppermute | solution.py:308
  73.5 7.0 %collective-permute-start.6 = (bf16[256,384]{1,0:T(8,128)(2,1)S(1)}, bf16[256,384]{1,0:T(8,128)(2,1)S(1)}, u32[]{:S(2)}, u32[]{:S(2)}) collective-permute-start(bf16[256,384]{1,0:T(8,128)(2,1)S(1)} %get-tuple-element.29), channel_id=1, source_target_pairs={{0,2},{1,3},{2,0},{3,1},{4,6},{5,7},{6,4},{7,5},{8,10},{9,11},{10,... | collective-permute-start | bytes 589832 | tf_op jit(solution)/shard_map/ppermute | solution.py:308

commit v7 on v6

--- a/solution.py
+++ b/solution.py
@@ -10,13 +10,13 @@
 TOP = 6
 CAP = 8
 CORES = 2
-CUTS = 2
 HELD = CAP // CORES
 CORE_SWAP = [(0, 1), (1, 0), (2, 3), (3, 2)]
 CHIP_SWAP = [(0, 2), (1, 3), (2, 0), (3, 1)]
 F32, BF16 = jnp.float32, jnp.bfloat16
 WHOLE = pl.BlockSpec(memory_space=pltpu.VMEM)
 FAR = pl.BlockSpec(memory_space=pltpu.HBM)
+ANY = pl.BlockSpec(memory_space=pl.ANY)
 SCALAR = pl.BlockSpec(memory_space=pltpu.SMEM)
 
 
@@ -106,16 +106,15 @@
 
 
 def prepare_body(
-    ids_ref, keep_ref, away_ref, gate_ref, mine_in, other_in, up_ref, mask_ref, w_ref, sems, *, experts
+    ids_ref, own_in, mine_in, other_in, mask_ref, w_ref, own_ref, sems, *, experts
 ):
     loads = [
         pltpu.make_async_copy(source, w_ref.at[index], sems.at[index])
         for index, source in enumerate((mine_in, other_in))
     ]
+    loads.append(pltpu.make_async_copy(own_in, own_ref, sems.at[CORES]))
     for load in loads:
         load.start()
-    hidden = keep_ref[...] + away_ref[...].astype(F32)
-    up_ref[...] = (hidden * gate_ref[:, : up_ref.shape[1]].astype(F32)).astype(BF16)
     tokens = ids_ref.shape[0]
     expert = lax.broadcasted_iota(jnp.int32, (tokens, experts), 1)
     named = jnp.zeros((tokens, experts), F32)
@@ -149,34 +148,36 @@
     out_ref[...] = chosen.reshape(out_ref.shape).astype(BF16)
 
 
-def hidden_body(core_ref, rows_ref, mine_in, other_in, keep_ref, send_ref, w_ref, sems, *, first):
-    count, half = keep_ref.shape[1], rows_ref.shape[-1]
+def bring_body(source_in, after_in, near_ref, sem):
+    load = pltpu.make_async_copy(source_in, near_ref, sem)
+    load.start()
+    load.wait()
+
+
+def hidden_body(core_ref, rows_ref, mine_in, other_ref, send_ref, w_ref, sems):
+    half = rows_ref.shape[-1]
     loads = [
-        pltpu.make_async_copy(source.at[pl.ds(first, count), :], w_ref.at[index], sems.at[index])
-        for index, source in enumerate((mine_in, other_in))
+        pltpu.make_async_copy(mine_in.at[:, pl.ds(side * half, half)], w_ref.at[side], sems.at[side])
+        for side in range(2)
     ]
     for load in loads:
         load.start()
     parts = []
-    for lane in (core_ref[0], 1 - core_ref[0]):
+    for lane in (1 - core_ref[0], core_ref[0]):
         rows = rows_ref[lane].astype(F32).reshape(-1, 2, CAP, half)
         for side in range(2):
             parts.append(pack(rows[:, 0], rows[:, 1], side).reshape(-1, half).astype(BF16))
-    total = None
-    for index, load in enumerate(loads):
+    total = dot(parts[0], other_ref[:, :half]) + dot(parts[1], other_ref[:, half:])
+    for side, load in enumerate(loads):
         load.wait()
-        for side in range(2):
-            term = dot(parts[2 * index + side], w_ref[index, :, side * half : (side + 1) * half])
-            total = term if total is None else total + term
-    keep_ref[...] = total
+        total = total + dot(parts[2 + side], w_ref[side])
     send_ref[...] = total.astype(BF16)
 
 
-def slot_grad_body(core_ref, first_ref, keep_ref, away_ref, gate_ref, w_ref, out_ref):
-    units, half = first_ref.shape[1], out_ref.shape[-1]
-    hidden = keep_ref[...] + away_ref[...].astype(F32)
-    last = (hidden * gate_ref[:, units:].astype(F32)).astype(BF16)
-    up = jnp.concatenate([first_ref[...], last], axis=1)
+def slot_grad_body(core_ref, own_ref, away_ref, gate_ref, w_ref, mask_in, out_ref):
+    hidden = own_ref[...].astype(F32) + away_ref[...].astype(F32)
+    up = (hidden * gate_ref[...].astype(F32)).astype(BF16)
+    half = out_ref.shape[-1]
     for index, lane in enumerate((core_ref[0], 1 - core_ref[0])):
         left = dot(up, w_ref[index, :half, :]).reshape(-1, CAP, half)
         right = dot(up, w_ref[index, half:, :]).reshape(-1, CAP, half)
@@ -288,43 +289,45 @@
         flops=2 * tokens * quarter * shared_up.shape[1],
         moved=2 * quarter * shared_up.shape[1],
     )(core, *dense_up, shared_up)
+    down_other = call(
+        bring_body,
+        jax.ShapeDtypeStruct(down_other.shape, BF16),
+        [FAR, ANY],
+        [pltpu.SemaphoreType.DMA(())],
+        moved=4 * quarter * width,
+    )(*far(down_other), shared_grad)
     ids, arrived, down_other, up_other, gate, shared_grad = lax.optimization_barrier(
         (expert_ids, arrived, down_other, up_other, gate, shared_grad)
     )
     work = 4 * held * quarter * width
-    units = width // CUTS
-    rows = arrived.reshape(CORES, experts, CAP, half)
-    keeps, aways = [], []
-    for cut in range(CUTS):
-        keep, send = call(
-            functools.partial(hidden_body, first=cut * units),
-            (jax.ShapeDtypeStruct((held, units), F32), jax.ShapeDtypeStruct((held, units), BF16)),
-            [SCALAR, WHOLE, FAR, FAR],
-            [pltpu.VMEM((CORES, units, quarter), BF16), pltpu.SemaphoreType.DMA((CORES,))],
-            flops=work // CUTS,
-            moved=4 * quarter * units,
-        )(core, rows, *far(w_down[0], down_other))
-        keeps.append(keep)
-        aways.append(lax.ppermute(send, "tensor", CHIP_SWAP))
-    first, mask, w_both = call(
+    send = call(
+        hidden_body,
+        jax.ShapeDtypeStruct(gate.shape, BF16),
+        [SCALAR, WHOLE, FAR, WHOLE],
+        [pltpu.VMEM((2, width, half), BF16), pltpu.SemaphoreType.DMA((2,))],
+        flops=work,
+        moved=4 * quarter * width,
+    )(core, arrived.reshape(CORES, experts, CAP, half), *far(w_down[0]), down_other)
+    away = lax.ppermute(send, "tensor", CHIP_SWAP)
+    mask, w_both, own = call(
         functools.partial(prepare_body, experts=experts),
         (
-            jax.ShapeDtypeStruct((held, units), BF16),
             jax.ShapeDtypeStruct((2 * tokens, CORES * slots), BF16),
             jax.ShapeDtypeStruct((CORES, quarter, width), BF16),
+            jax.ShapeDtypeStruct(gate.shape, BF16),
         ),
-        [WHOLE] * 4 + [FAR] * 2,
-        [pltpu.SemaphoreType.DMA((CORES,))],
+        [WHOLE] + [FAR] * 3,
+        [pltpu.SemaphoreType.DMA((CORES + 1,))],
         flops=2 * tokens * slots * experts,
         moved=4 * quarter * width,
-    )(ids, keeps[0], aways[0], gate, *far(w_up[0], up_other))
+    )(ids, *far(send, w_up[0], up_other))
     slot_grad = call(
         slot_grad_body,
         jax.ShapeDtypeStruct((CORES, experts // 2, 2, CAP, half), BF16),
-        [SCALAR] + [WHOLE] * 5,
+        [SCALAR] + [WHOLE] * 4 + [ANY],
         flops=work,
         moved=4 * quarter * width,
-    )(core, first, keeps[1], aways[1], gate, w_both)
+    )(core, own, away, gate, w_both, mask)
     back = exchange(slot_grad)
     moe_grad = call(
         combine_body,

time: 129 us -> 129 us (level)
  starting transfers between devices: 44.2 us -> 42 us
    ppermute x2 -> x1, waiting for transfers between devices: 2.56 us -> 6.23 us  [on_device(): away = lax.ppermute(send, 'tensor', CHIP_SWAP)]
    all_to_all x1, waiting for transfers between devices: 14.3 us -> 11.7 us  [exchange(): lax.all_to_all(rows, ('expert', 'tensor'), 0, 0, axis_index_groups=groups...]
    ppermute x2 -> x1, starting transfers between devices: 5.28 us -> 3.12 us  [on_device(): away = lax.ppermute(send, 'tensor', CHIP_SWAP)]
  transfers between devices with their start and end apart: 8 -> 7, of which waited for: 5 -> 5; matrix products, arithmetic and copies ran while one was open for 0% -> 0% of each run, Pallas kernels for 6% -> 5%
where the time goes in v7:
time: 129 us
  blocking collectives  44.3 us (34%)
  starting transfers between devices  42 us (33%)
  waiting for transfers between devices  23.1 us (18%)
  Pallas kernels  16.1 us (12%)
  local copies, waits for them, and re-layouts  2.14 us (2%)
    all_to_all x1, blocking collectives, exchange(): lax.all_to_all(rows, ('expert', 'tensor'), 0, 0, axis_index_groups=groups...  44.3 us
    all_to_all x1, starting transfers between devices, exchange(): lax.all_to_all(rows, ('expert', 'tensor'), 0, 0, axis_index_groups=groups...  25.7 us
    all_to_all x1, waiting for transfers between devices, exchange(): lax.all_to_all(rows, ('expert', 'tensor'), 0, 0, axis_index_groups=groups...  11.7 us
    ppermute x1, waiting for transfers between devices, on_device(): away = lax.ppermute(send, 'tensor', CHIP_SWAP)  6.23 us
    pallas_call x1, Pallas kernels, on_device(): call(hidden_body, jax.ShapeDtypeStruct(gate.shape, BF16), [SCALAR, WHOLE,...  3.98 us
    ppermute x1, waiting for transfers between devices, dense_up_grad(): away = lax.ppermute((mine + pair).astype(BF16), 'tensor', CHIP_SWAP)  3.31 us
    ppermute x1, starting transfers between devices, on_device(): away = lax.ppermute(send, 'tensor', CHIP_SWAP)  3.12 us
    ppermute x1, starting transfers between devices, dense_up_grad(): away = lax.ppermute((mine + pair).astype(BF16), 'tensor', CHIP_SWAP)  3.12 us
  transfers between devices with their start and end apart: 7, of which 5 were waited for; matrix products, arithmetic and copies ran while one was open for 0% of the time, Pallas kernels for 5%

profile of v7, /device:TPU:1, one launch (start us, length us, event | category | flops | bytes accessed | tf_op | source)
XLA Modules:
  0.0 128.5 jit_solution(409847480914094501)
XLA Ops:
  0.6 2.7 %shard_map.104 = bf16[2,32,2,8,640]{4,3,2,1,0:T(8,128)(2,1)} custom-call(s32[6,160]{1,0:T(8,128)} %bitcast.18, f32[6,160]{1,0:T(8,128)} %bitcast.19, bf16[160,1280]{1,0:T(8,128)(2,1)} %rows_ref.1), custom_call_target="tpu_custom_call" | custom-call | flops 209715200 | bytes 2621440 | tf_op jit(solution)/shard_map/pallas_call | solution.py:259
  3.4 0.0 copy-start.7
  3.4 25.7 %all-to-all-start = ((bf16[128,8,640]{2,1,0:T(8,128)(2,1)}), bf16[128,8,640]{2,1,0:T(8,128)(2,1)S(1)}, u32[]{:S(2)}, u32[]{:S(2)}) async-start(bf16[128,8,640]{2,1,0:T(8,128)(2,1)} %bitcast.2), calls=%async_computation | async-start | bytes 2621440 | tf_op jit(solution)/shard_map/all_to_all | solution.py:254
  29.1 2.5 %collective-permute-start = (bf16[768,1280]{1,0:T(8,128)(2,1)}, bf16[768,1280]{1,0:T(8,128)(2,1)}, u32[]{:S(2)}, u32[]{:S(2)}) collective-permute-start(bf16[768,1280]{1,0:T(8,128)(2,1)} %bitcast.14), channel_id=1, source_target_pairs={{0,1},{1,0},{2,3},{3,2},{4,5},{5,4},{6,7},{7,6},{8,9},{9,8},{10,11... | collective-permute-start | bytes 5898248 | tf_op jit(solution)/shard_map/ppermute | solution.py:274
  31.6 1.9 %collective-permute-start.4 = (bf16[1280,768]{1,0:T(8,128)(2,1)}, bf16[1280,768]{1,0:T(8,128)(2,1)}, u32[]{:S(2)}, u32[]{:S(2)}) collective-permute-start(bf16[1280,768]{1,0:T(8,128)(2,1)} %bitcast.16), channel_id=1, source_target_pairs={{0,1},{1,0},{2,3},{3,2},{4,5},{5,4},{6,7},{7,6},{8,9},{9,8},{10,11... | collective-permute-start | bytes 5898248 | tf_op jit(solution)/shard_map/ppermute | solution.py:275
  33.5 0.0 copy-done.1
  33.6 0.0 copy-start.3
  33.6 1.0 copy-done.3
  34.6 0.8 shard_map.105
  35.4 0.0 copy-start
  35.4 2.5 %collective-permute-start.1 = (f32[80,768]{1,0:T(8,128)S(1)}, f32[80,768]{1,0:T(8,128)S(1)}, u32[]{:S(2)}, u32[]{:S(2)}) collective-permute-start(f32[80,768]{1,0:T(8,128)S(1)} %get-tuple-element.14), channel_id=1, source_target_pairs={{0,1},{1,0},{2,3},{3,2},{4,5},{5,4},{6,7},{7,6},{8,9},{9,8},{10,11... | collective-permute-start | bytes 737288 | tf_op jit(solution)/shard_map/ppermute | solution.py:228
  38.0 1.1 collective-permute-done.1.pair_ref
  39.1 3.1 %collective-permute-start.2 = (bf16[80,768]{1,0:T(8,128)(2,1)S(1)}, bf16[80,768]{1,0:T(8,128)(2,1)S(1)}, u32[]{:S(2)}, u32[]{:S(2)}) collective-permute-start(bf16[80,768]{1,0:T(8,128)(2,1)S(1)} %add_convert_fusion), channel_id=1, source_target_pairs={{0,2},{1,3},{2,0},{3,1},{4,6},{5,7},{6,4},{7,5},{8,10},{9,11},{10,... | collective-permute-start | bytes 368648 | tf_op jit(solution)/shard_map/ppermute | solution.py:229
  42.2 3.3 %collective-permute-done.2.away_ref = bf16[80,768]{1,0:T(8,128)(2,1)S(1)} collective-permute-done((bf16[80,768]{1,0:T(8,128)(2,1)S(1)}, bf16[80,768]{1,0:T(8,128)(2,1)S(1)}, u32[]{:S(2)}, u32[]{:S(2)}) %collective-permute-start.2) | collective-permute-done | bytes 122912 | tf_op jit(solution)/shard_map/ppermute | solution.py:229
  45.5 0.1 shard_map.106.mine_ref
  45.6 3.1 %collective-permute-start.3 = (bf16[80,768]{1,0:T(8,128)(2,1)S(1)}, bf16[80,768]{1,0:T(8,128)(2,1)S(1)}, u32[]{:S(2)}, u32[]{:S(2)}) collective-permute-start(bf16[80,768]{1,0:T(8,128)(2,1)S(1)} %shard_map.106.mine_ref), channel_id=1, source_target_pairs={{0,1},{1,0},{2,3},{3,2},{4,5},{5,4},{6,7},{7,6},{8,9},{9,8},{10,11... | collective-permute-start | bytes 368648 | tf_op jit(solution)/shard_map/ppermute | solution.py:237
  48.7 0.2 shard_map.109.gate_ref
  48.9 0.7 collective-permute-done.3.other_ref
  49.7 1.6 %shard_map.107.after_in = bf16[160,1280]{1,0:T(8,128)(2,1)} custom-call(s32[1]{0:T(128)} %bitcast.4.core_ref, bf16[80,768]{1,0:T(8,128)(2,1)S(1)} %shard_map.106.mine_ref, bf16[80,768]{1,0:T(8,128)(2,1)S(1)} %collective-permute-done.3.other_ref, bf16[1280,768]{1,0:T(8,128)(2,1)S(1)} %copy-done), custom_call_target="tpu_custom_call" | custom-call | flops 314572800 | bytes 1966080 | tf_op jit(solution)/shard_map/pallas_call | solution.py:285
  51.3 0.0 collective-permute-done.source_in
  51.3 1.0 copy-done.2
  52.3 1.6 %shard_map.108.other_ref = bf16[768,1280]{1,0:T(8,128)(2,1)S(1)} custom-call(bf16[768,1280]{1,0:T(8,128)(2,1)} %collective-permute-done.source_in, bf16[160,1280]{1,0:T(8,128)(2,1)S(1)} %copy-done.2), custom_call_target="tpu_custom_call" | custom-call | bytes 3932160 | tf_op jit(solution)/shard_map/pallas_call | solution.py:292
  53.8 0.0 collective-permute-done.4.other_in
  53.8 11.7 %all-to-all-done = bf16[128,8,640]{2,1,0:T(8,128)(2,1)S(1)} async-done(((bf16[128,8,640]{2,1,0:T(8,128)(2,1)}), bf16[128,8,640]{2,1,0:T(8,128)(2,1)S(1)}, u32[]{:S(2)}, u32[]{:S(2)}) %all-to-all-start) | async-done | bytes 1310752 | tf_op jit(solution)/shard_map/all_to_all | solution.py:254
  65.6 4.0 %shard_map.110.own_in = bf16[256,768]{1,0:T(8,128)(2,1)} custom-call(s32[1]{0:T(128)} %bitcast.4.core_ref, bf16[2,64,8,640]{3,2,1,0:T(8,128)(2,1)S(1)} %bitcast.12, bf16[768,1280]{1,0:T(8,128)(2,1)} %bitcast.15, bf16[768,1280]{1,0:T(8,128)(2,1)S(1)} %shard_map.108.other_ref), custom_call_target="tpu_custom_call" | custom-call | flops 1006632960 | bytes 3932160 | tf_op jit(solution)/shard_map/pallas_call | solution.py:303
  69.5 3.1 %collective-permute-start.5 = (bf16[256,768]{1,0:T(8,128)(2,1)}, bf16[256,768]{1,0:T(8,128)(2,1)S(1)}, u32[]{:S(2)}, u32[]{:S(2)}) collective-permute-start(bf16[256,768]{1,0:T(8,128)(2,1)} %shard_map.110.own_in), channel_id=1, source_target_pairs={{0,2},{1,3},{2,0},{3,1},{4,6},{5,7},{6,4},{7,5},{8,10},{9,11},{10,... | collective-permute-start | bytes 1179656 | tf_op jit(solution)/shard_map/ppermute | solution.py:311
  72.7 0.1 copy.11.ids_ref
  72.8 2.3 %shard_map.111 = (bf16[320,1024]{1,0:T(8,128)(2,1)S(1)}, bf16[2,1280,768]{2,1,0:T(8,128)(2,1)S(1)}, bf16[256,768]{1,0:T(8,128)(2,1)S(1)}) custom-call(s32[160,6]{1,0:T(8,128)S(1)} %copy.11.ids_ref, bf16[256,768]{1,0:T(8,128)(2,1)} %shard_map.110.own_in, bf16[1280,768]{1,0:T(8,128)(2,1)} %bitcast.17, bf16[1280,768]{1,0:T(8,128)(2,1)} %collective-permute-done.4.other_in), custom_call_target="tpu_custom_call" | custom-call | flops 10485760 | bytes 3932160 | tf_op jit(solution)/shard_map/pallas_call | solution.py:312
  75.1 6.2 %collective-permute-done.5.away_ref = bf16[256,768]{1,0:T(8,128)(2,1)S(1)} collective-permute-done((bf16[256,768]{1,0:T(8,128)(2,1)}, bf16[256,768]{1,0:T(8,128)(2,1)S(1)}, u32[]{:S(2)}, u32[]{:S(2)}) %collective-permute-start.5) | collective-permute-done | bytes 393248 | tf_op jit(solution)/shard_map/ppermute | solution.py:311
  81.3 1.4 %shard_map.112 = bf16[2,32,2,8,640]{4,3,2,1,0:T(8,128)(2,1)S(1)} custom-call(s32[1]{0:T(128)} %bitcast.4.core_ref, bf16[256,768]{1,0:T(8,128)(2,1)S(1)} %get-tuple-element.20.own_ref, bf16[256,768]{1,0:T(8,128)(2,1)S(1)} %collective-permute-done.5.away_ref, bf16[256,768]{1,0:T(8,128)(2,1)S(1)} %copy-done.5, ...), custom_call_target="tpu_custom_call" | custom-call | flops 1006632960 | bytes 3932160 | tf_op jit(solution)/shard_map/pallas_call | solution.py:324
  82.8 44.3 %all_to_all.10 = bf16[128,8,640]{2,1,0:T(8,128)(2,1)S(1)} all-to-all(bf16[128,8,640]{2,1,0:T(8,128)(2,1)S(1)} %bitcast.10), channel_id=1, replica_groups={{0,4,8,12,16,20,24,28,32,36,40,44,48,52,56,60,64,68,72,76,80,84,88,92,9..., dimensions={0} | all-to-all | bytes 2621440 | tf_op jit(solution)/shard_map/all_to_all | solution.py:254
  127.1 1.4 %shard_map.113 = bf16[160,1280]{1,0:T(8,128)(2,1)} custom-call(bf16[320,1024]{1,0:T(8,128)(2,1)S(1)} %get-tuple-element.19.mask_in.mask_ref, bf16[1024,640]{1,0:T(8,128)(2,1)S(1)} %bitcast.11), custom_call_target="tpu_custom_call" | custom-call | flops 419430400 | bytes 1310720 | tf_op jit(solution)/shard_map/pallas_call | solution.py:332
  (13 shorter events, 0.0 us)
Async XLA Ops:
  0.6 32.9 %copy-start.1 = (bf16[768,1280]{1,0:T(8,128)(2,1)S(1)}, bf16[768,1280]{1,0:T(8,128)(2,1)}, u32[]{:S(2)}) copy-start(bf16[768,1280]{1,0:T(8,128)(2,1)} %w_ref.2) | copy-start | bytes 5898244
  3.4 42.1 %copy-start.7 = (bf16[160,768]{1,0:T(8,128)(2,1)S(1)}, bf16[160,768]{1,0:T(8,128)(2,1)}, u32[]{:S(2)}) copy-start(bf16[160,768]{1,0:T(8,128)(2,1)} %gate_ref.1) | copy-start | bytes 737284
  3.4 62.2 %all-to-all-start = ((bf16[128,8,640]{2,1,0:T(8,128)(2,1)}), bf16[128,8,640]{2,1,0:T(8,128)(2,1)S(1)}, u32[]{:S(2)}, u32[]{:S(2)}) async-start(bf16[128,8,640]{2,1,0:T(8,128)(2,1)} %bitcast.2), calls=%async_computation | async-start | bytes 2621440 | tf_op jit(solution)/shard_map/all_to_all | solution.py:254
  29.1 22.1 %collective-permute-start = (bf16[768,1280]{1,0:T(8,128)(2,1)}, bf16[768,1280]{1,0:T(8,128)(2,1)}, u32[]{:S(2)}, u32[]{:S(2)}) collective-permute-start(bf16[768,1280]{1,0:T(8,128)(2,1)} %bitcast.14), channel_id=1, source_target_pairs={{0,1},{1,0},{2,3},{3,2},{4,5},{5,4},{6,7},{7,6},{8,9},{9,8},{10,11... | collective-permute-start | bytes 5898248 | tf_op jit(solution)/shard_map/ppermute | solution.py:274
  31.6 22.2 %collective-permute-start.4 = (bf16[1280,768]{1,0:T(8,128)(2,1)}, bf16[1280,768]{1,0:T(8,128)(2,1)}, u32[]{:S(2)}, u32[]{:S(2)}) collective-permute-start(bf16[1280,768]{1,0:T(8,128)(2,1)} %bitcast.16), channel_id=1, source_target_pairs={{0,1},{1,0},{2,3},{3,2},{4,5},{5,4},{6,7},{7,6},{8,9},{9,8},{10,11... | collective-permute-start | bytes 5898248 | tf_op jit(solution)/shard_map/ppermute | solution.py:275
  33.6 1.0 copy-start.3
  34.6 14.2 %copy-start.6 = (bf16[1,1,512,768]{3,2,1,0:T(8,128)(2,1)S(1)}, bf16[1,1,512,768]{3,2,1,0:T(8,128)(2,1)}, u32[]{:S(2)}) copy-start(bf16[1,1,512,768]{3,2,1,0:T(8,128)(2,1)} %param.12) | copy-start | bytes 2359300
  35.4 14.3 %copy-start = (bf16[1280,768]{1,0:T(8,128)(2,1)S(1)}, bf16[1280,768]{1,0:T(8,128)(2,1)}, u32[]{:S(2)}) copy-start(bf16[1280,768]{1,0:T(8,128)(2,1)} %w_ref.3) | copy-start | bytes 5898244
  35.4 3.7 %collective-permute-start.1 = (f32[80,768]{1,0:T(8,128)S(1)}, f32[80,768]{1,0:T(8,128)S(1)}, u32[]{:S(2)}, u32[]{:S(2)}) collective-permute-start(f32[80,768]{1,0:T(8,128)S(1)} %get-tuple-element.14), channel_id=1, source_target_pairs={{0,1},{1,0},{2,3},{3,2},{4,5},{5,4},{6,7},{7,6},{8,9},{9,8},{10,11... | collective-permute-start | bytes 737288 | tf_op jit(solution)/shard_map/ppermute | solution.py:228
  39.1 6.4 %collective-permute-start.2 = (bf16[80,768]{1,0:T(8,128)(2,1)S(1)}, bf16[80,768]{1,0:T(8,128)(2,1)S(1)}, u32[]{:S(2)}, u32[]{:S(2)}) collective-permute-start(bf16[80,768]{1,0:T(8,128)(2,1)S(1)} %add_convert_fusion), channel_id=1, source_target_pairs={{0,2},{1,3},{2,0},{3,1},{4,6},{5,7},{6,4},{7,5},{8,10},{9,11},{10,... | collective-permute-start | bytes 368648 | tf_op jit(solution)/shard_map/ppermute | solution.py:229
  45.6 4.1 %collective-permute-start.3 = (bf16[80,768]{1,0:T(8,128)(2,1)S(1)}, bf16[80,768]{1,0:T(8,128)(2,1)S(1)}, u32[]{:S(2)}, u32[]{:S(2)}) collective-permute-start(bf16[80,768]{1,0:T(8,128)(2,1)S(1)} %shard_map.106.mine_ref), channel_id=1, source_target_pairs={{0,1},{1,0},{2,3},{3,2},{4,5},{5,4},{6,7},{7,6},{8,9},{9,8},{10,11... | collective-permute-start | bytes 368648 | tf_op jit(solution)/shard_map/ppermute | solution.py:237
  48.9 4.9 %copy-start.4 = (bf16[256,768]{1,0:T(8,128)(2,1)}, bf16[256,768]{1,0:T(8,128)(2,1)S(1)}, u32[]{:S(2)}) copy-start(bf16[256,768]{1,0:T(8,128)(2,1)S(1)} %shard_map.109.gate_ref) | copy-start | bytes 1179652
  51.3 1.0 copy-start.2
  65.6 7.1 %copy-start.8 = (s32[160,6]{0,1:T(8,128)S(1)}, s32[160,6]{0,1:T(8,128)}, u32[]{:S(2)}) copy-start(s32[160,6]{0,1:T(8,128)} %param.10) | copy-start | bytes 11524
  69.5 11.8 %collective-permute-start.5 = (bf16[256,768]{1,0:T(8,128)(2,1)}, bf16[256,768]{1,0:T(8,128)(2,1)S(1)}, u32[]{:S(2)}, u32[]{:S(2)}) collective-permute-start(bf16[256,768]{1,0:T(8,128)(2,1)} %shard_map.110.own_in), channel_id=1, source_target_pairs={{0,2},{1,3},{2,0},{3,1},{4,6},{5,7},{6,4},{7,5},{8,10},{9,11},{10,... | collective-permute-start | bytes 1179656 | tf_op jit(solution)/shard_map/ppermute | solution.py:311
  72.8 8.5 %copy-start.5 = (bf16[256,768]{1,0:T(8,128)(2,1)S(1)}, bf16[256,768]{1,0:T(8,128)(2,1)}, u32[]{:S(2)}) copy-start(bf16[256,768]{1,0:T(8,128)(2,1)} %copy-done.4) | copy-start | bytes 1179652

commit v8 on v4

--- a/solution.py
+++ b/solution.py
@@ -24,12 +24,12 @@
     return lax.dot_general(a, b, (dims, ((), ())), preferred_element_type=F32)
 
 
-def call(body, outs, specs, scratch=(), flops=0, moved=0):
+def call(body, outs, specs, scratch=(), flops=0, moved=0, place=WHOLE):
     return pl.pallas_call(
         body,
         out_shape=outs,
         in_specs=specs,
-        out_specs=jax.tree.map(lambda _: WHOLE, outs),
+        out_specs=jax.tree.map(lambda _: place, outs),
         scratch_shapes=list(scratch),
         compiler_params=pltpu.CompilerParams(vmem_limit_bytes=12 << 20),
         cost_estimate=pl.CostEstimate(flops=flops, bytes_accessed=moved, transcendentals=0),
@@ -51,7 +51,9 @@
     return jnp.where(low, pltpu.roll(even, HELD, 1), odd)
 
 
-def route_body(ids_in, prob_in, grad_in, sent_ref, ids_ref, prob_ref, grad_ref, sems, *, experts):
+def route_body(
+    ids_in, prob_in, grad_in, sent_out, ids_ref, prob_ref, grad_ref, sent_ref, sems, *, experts
+):
     tokens, quarter = grad_ref.shape
     loads = [
         pltpu.make_async_copy(source, target, sems.at[index])
@@ -86,6 +88,10 @@
     rank, prob = spread(rank), spread(prob)
     slot = lax.rem(lax.broadcasted_iota(jnp.int32, shape, 1), HELD).astype(F32)
     loads[2].wait()
+    stores = [
+        pltpu.make_async_copy(sent_ref.at[core], sent_out.at[core], sems.at[3 + core])
+        for core in range(CORES)
+    ]
     for core in range(CORES):
         hit = rank == slot + float(core * HELD)
         scale = jnp.sum(jnp.where(hit, prob, 0.0), axis=2, keepdims=True)
@@ -94,6 +100,9 @@
         right = dot(mask, grad_ref[:, half:], ((1,), (0,))).reshape(pairs, CAP, half) * scale
         sent_ref[core, :, 0] = pack(left, right, 0).astype(BF16)
         sent_ref[core, :, 1] = pack(left, right, 1).astype(BF16)
+        stores[core].start()
+    for store in stores:
+        store.wait()
 
 
 def prepare_body(ids_ref, after_ref, mine_in, other_in, mask_ref, w_ref, sems, *, experts):
@@ -244,9 +253,13 @@
         jax.ShapeDtypeStruct((CORES, experts // 2, 2, CAP, half), BF16),
         [FAR] * 3,
         [pltpu.VMEM(array.shape, array.dtype) for array in (ids, probs, grad_out)]
-        + [pltpu.SemaphoreType.DMA((3,))],
+        + [
+            pltpu.VMEM((CORES, experts // 2, 2, CAP, half), BF16),
+            pltpu.SemaphoreType.DMA((3 + CORES,)),
+        ],
         flops=2 * slots * tokens * quarter,
         moved=4 * slots * quarter,
+        place=FAR,
     )(*far(ids, probs, grad_out))
     arrived = exchange(sent)
 

time: 129 us -> 128 us (level)
  no operation moved by 1% of the time
where the time goes in v8:
time: 128 us
  blocking collectives  44.4 us (35%)
  starting transfers between devices  42 us (33%)
  waiting for transfers between devices  25.6 us (20%)
  Pallas kernels  14 us (11%)
    all_to_all x1, blocking collectives, exchange(): lax.all_to_all(rows, ('expert', 'tensor'), 0, 0, axis_index_groups=groups...  44.4 us
    all_to_all x1, starting transfers between devices, exchange(): lax.all_to_all(rows, ('expert', 'tensor'), 0, 0, axis_index_groups=groups...  25.7 us
    all_to_all x1, waiting for transfers between devices, exchange(): lax.all_to_all(rows, ('expert', 'tensor'), 0, 0, axis_index_groups=groups...  14.3 us
    ppermute x1, waiting for transfers between devices, on_device(): away = lax.ppermute(send, 'tensor', CHIP_SWAP)  6.09 us
    pallas_call x1, Pallas kernels, on_device(): call(hidden_body, (jax.ShapeDtypeStruct(gate.shape, F32), jax.ShapeDtypeS...  3.55 us
    ppermute x1, waiting for transfers between devices, dense_up_grad(): away = lax.ppermute((mine + pair).astype(BF16), 'tensor', CHIP_SWAP)  3.3 us
    ppermute x1, starting transfers between devices, on_device(): away = lax.ppermute(send, 'tensor', CHIP_SWAP)  3.14 us
    ppermute x1, starting transfers between devices, dense_up_grad(): away = lax.ppermute((mine + pair).astype(BF16), 'tensor', CHIP_SWAP)  3.12 us
  transfers between devices with their start and end apart: 7, of which 5 were waited for; matrix products, arithmetic and copies ran while one was open for 0% of the time, Pallas kernels for 4%

profile of v8, /device:TPU:1, one launch (start us, length us, event | category | flops | bytes accessed | tf_op | source)
XLA Modules:
  0.0 127.9 jit_solution(6966432792927460539)
XLA Ops:
  0.6 0.0 copy-start.1
  0.6 2.8 %shard_map.104 = bf16[2,32,2,8,640]{4,3,2,1,0:T(8,128)(2,1)} custom-call(s32[6,160]{1,0:T(8,128)} %bitcast.18, f32[6,160]{1,0:T(8,128)} %bitcast.19, bf16[160,1280]{1,0:T(8,128)(2,1)} %rows_ref.1), custom_call_target="tpu_custom_call" | custom-call | flops 209715200 | bytes 2621440 | tf_op jit(solution)/shard_map/pallas_call | solution.py:251
  3.4 0.0 copy-start.4
  3.4 25.7 %all-to-all-start = ((bf16[128,8,640]{2,1,0:T(8,128)(2,1)}), bf16[128,8,640]{2,1,0:T(8,128)(2,1)S(1)}, u32[]{:S(2)}, u32[]{:S(2)}) async-start(bf16[128,8,640]{2,1,0:T(8,128)(2,1)} %bitcast.2), calls=%async_computation | async-start | bytes 2621440 | tf_op jit(solution)/shard_map/all_to_all | solution.py:246
  29.1 2.5 %collective-permute-start.1 = (bf16[1280,768]{1,0:T(8,128)(2,1)}, bf16[1280,768]{1,0:T(8,128)(2,1)}, u32[]{:S(2)}, u32[]{:S(2)}) collective-permute-start(bf16[1280,768]{1,0:T(8,128)(2,1)} %bitcast.14), channel_id=1, source_target_pairs={{0,1},{1,0},{2,3},{3,2},{4,5},{5,4},{6,7},{7,6},{8,9},{9,8},{10,11... | collective-permute-start | bytes 5898248 | tf_op jit(solution)/shard_map/ppermute | solution.py:267
  31.6 1.9 %collective-permute-start = (bf16[768,1280]{1,0:T(8,128)(2,1)}, bf16[768,1280]{1,0:T(8,128)(2,1)}, u32[]{:S(2)}, u32[]{:S(2)}) collective-permute-start(bf16[768,1280]{1,0:T(8,128)(2,1)} %bitcast.16), channel_id=1, source_target_pairs={{0,1},{1,0},{2,3},{3,2},{4,5},{5,4},{6,7},{7,6},{8,9},{9,8},{10,11... | collective-permute-start | bytes 5898248 | tf_op jit(solution)/shard_map/ppermute | solution.py:266
  33.5 0.0 copy-done.1
  33.6 0.0 copy-start.2
  33.6 1.0 copy-done.2
  34.6 0.8 shard_map.106
  35.4 0.0 copy-start
  35.4 2.5 %collective-permute-start.2 = (f32[80,768]{1,0:T(8,128)S(1)}, f32[80,768]{1,0:T(8,128)S(1)}, u32[]{:S(2)}, u32[]{:S(2)}) collective-permute-start(f32[80,768]{1,0:T(8,128)S(1)} %get-tuple-element.15), channel_id=1, source_target_pairs={{0,1},{1,0},{2,3},{3,2},{4,5},{5,4},{6,7},{7,6},{8,9},{9,8},{10,11... | collective-permute-start | bytes 737288 | tf_op jit(solution)/shard_map/ppermute | solution.py:220
  38.0 1.1 collective-permute-done.2.pair_ref
  39.1 3.1 %collective-permute-start.3 = (bf16[80,768]{1,0:T(8,128)(2,1)S(1)}, bf16[80,768]{1,0:T(8,128)(2,1)S(1)}, u32[]{:S(2)}, u32[]{:S(2)}) collective-permute-start(bf16[80,768]{1,0:T(8,128)(2,1)S(1)} %add_convert_fusion), channel_id=1, source_target_pairs={{0,2},{1,3},{2,0},{3,1},{4,6},{5,7},{6,4},{7,5},{8,10},{9,11},{10,... | collective-permute-start | bytes 368648 | tf_op jit(solution)/shard_map/ppermute | solution.py:221
  42.2 3.3 %collective-permute-done.3.away_ref = bf16[80,768]{1,0:T(8,128)(2,1)S(1)} collective-permute-done((bf16[80,768]{1,0:T(8,128)(2,1)S(1)}, bf16[80,768]{1,0:T(8,128)(2,1)S(1)}, u32[]{:S(2)}, u32[]{:S(2)}) %collective-permute-start.3) | collective-permute-done | bytes 122912 | tf_op jit(solution)/shard_map/ppermute | solution.py:221
  45.5 0.1 shard_map.107.mine_ref
  45.6 3.1 %collective-permute-start.4 = (bf16[80,768]{1,0:T(8,128)(2,1)S(1)}, bf16[80,768]{1,0:T(8,128)(2,1)S(1)}, u32[]{:S(2)}, u32[]{:S(2)}) collective-permute-start(bf16[80,768]{1,0:T(8,128)(2,1)S(1)} %shard_map.107.mine_ref), channel_id=1, source_target_pairs={{0,1},{1,0},{2,3},{3,2},{4,5},{5,4},{6,7},{7,6},{8,9},{9,8},{10,11... | collective-permute-start | bytes 368648 | tf_op jit(solution)/shard_map/ppermute | solution.py:229
  48.7 0.0 copy-done.3
  48.7 0.2 shard_map.105.gate_ref
  48.9 0.7 collective-permute-done.4.other_ref
  49.7 1.6 %shard_map.108 = bf16[160,1280]{1,0:T(8,128)(2,1)} custom-call(s32[1]{0:T(128)} %bitcast.5.core_ref, bf16[80,768]{1,0:T(8,128)(2,1)S(1)} %shard_map.107.mine_ref, bf16[80,768]{1,0:T(8,128)(2,1)S(1)} %collective-permute-done.4.other_ref, bf16[1280,768]{1,0:T(8,128)(2,1)S(1)} %copy-done), custom_call_target="tpu_custom_call" | custom-call | flops 314572800 | bytes 1966080 | tf_op jit(solution)/shard_map/pallas_call | solution.py:277
  51.3 0.0 collective-permute-done.1.other_in
  51.3 0.0 collective-permute-done.other_in
  51.3 14.3 %all-to-all-done = bf16[128,8,640]{2,1,0:T(8,128)(2,1)S(1)} async-done(((bf16[128,8,640]{2,1,0:T(8,128)(2,1)}), bf16[128,8,640]{2,1,0:T(8,128)(2,1)S(1)}, u32[]{:S(2)}, u32[]{:S(2)}) %all-to-all-start) | async-done | bytes 1310752 | tf_op jit(solution)/shard_map/all_to_all | solution.py:246
  65.6 3.6 %shard_map.109 = (f32[256,768]{1,0:T(8,128)S(1)}, bf16[256,768]{1,0:T(8,128)(2,1)S(1)}) custom-call(s32[1]{0:T(128)} %bitcast.5.core_ref, bf16[2,64,8,640]{3,2,1,0:T(8,128)(2,1)S(1)} %bitcast.11, bf16[768,1280]{1,0:T(8,128)(2,1)} %bitcast.17, bf16[768,1280]{1,0:T(8,128)(2,1)} %collective-permute-done.other_in), custom_call_target="tpu_custom_call" | custom-call | flops 1006632960 | bytes 3932160 | tf_op jit(solution)/shard_map/pallas_call | solution.py:288
  69.1 3.1 %collective-permute-start.5 = (bf16[256,768]{1,0:T(8,128)(2,1)S(1)}, bf16[256,768]{1,0:T(8,128)(2,1)S(1)}, u32[]{:S(2)}, u32[]{:S(2)}) collective-permute-start(bf16[256,768]{1,0:T(8,128)(2,1)S(1)} %get-tuple-element.22), channel_id=1, source_target_pairs={{0,2},{1,3},{2,0},{3,1},{4,6},{5,7},{6,4},{7,5},{8,10},{9,11},{10,... | collective-permute-start | bytes 1179656 | tf_op jit(solution)/shard_map/ppermute | solution.py:296
  72.3 0.1 copy.11.ids_ref
  72.4 2.2 %shard_map.110 = (bf16[320,1024]{1,0:T(8,128)(2,1)S(1)}, bf16[2,1280,768]{2,1,0:T(8,128)(2,1)S(1)}) custom-call(s32[160,6]{1,0:T(8,128)S(1)} %copy.11.ids_ref, f32[256,768]{1,0:T(8,128)S(1)} %get-tuple-element.19.after_ref.keep_ref, bf16[1280,768]{1,0:T(8,128)(2,1)} %bitcast.15, bf16[1280,768]{1,0:T(8,128)(2,1)} %collective-permute-done.1.other_in), custom_call_target="tpu_custom_call" | custom-call | flops 10485760 | bytes 3932160 | tf_op jit(solution)/shard_map/pallas_call | solution.py:297
  74.6 6.1 %collective-permute-done.5.away_ref = bf16[256,768]{1,0:T(8,128)(2,1)S(1)} collective-permute-done((bf16[256,768]{1,0:T(8,128)(2,1)S(1)}, bf16[256,768]{1,0:T(8,128)(2,1)S(1)}, u32[]{:S(2)}, u32[]{:S(2)}) %collective-permute-start.5) | collective-permute-done | bytes 393248 | tf_op jit(solution)/shard_map/ppermute | solution.py:296
  80.7 1.4 %shard_map.111 = bf16[2,32,2,8,640]{4,3,2,1,0:T(8,128)(2,1)S(1)} custom-call(s32[1]{0:T(128)} %bitcast.5.core_ref, f32[256,768]{1,0:T(8,128)S(1)} %get-tuple-element.19.after_ref.keep_ref, bf16[256,768]{1,0:T(8,128)(2,1)S(1)} %collective-permute-done.5.away_ref, bf16[256,768]{1,0:T(8,128)(2,1)S(1)} %shard_map.105.gate_ref, ...), custom_call_target="tpu_custom_call" | custom-call | flops 1006632960 | bytes 3932160 | tf_op jit(solution)/shard_map/pallas_call | solution.py:308
  82.1 44.4 %all_to_all.10 = bf16[128,8,640]{2,1,0:T(8,128)(2,1)S(1)} all-to-all(bf16[128,8,640]{2,1,0:T(8,128)(2,1)S(1)} %bitcast.12), channel_id=1, replica_groups={{0,4,8,12,16,20,24,28,32,36,40,44,48,52,56,60,64,68,72,76,80,84,88,92,9..., dimensions={0} | all-to-all | bytes 2621440 | tf_op jit(solution)/shard_map/all_to_all | solution.py:246
  126.5 1.4 %shard_map.112 = bf16[160,1280]{1,0:T(8,128)(2,1)} custom-call(bf16[320,1024]{1,0:T(8,128)(2,1)S(1)} %get-tuple-element.21.mask_in.mask_ref, bf16[1024,640]{1,0:T(8,128)(2,1)S(1)} %bitcast.10), custom_call_target="tpu_custom_call" | custom-call | flops 419430400 | bytes 1310720 | tf_op jit(solution)/shard_map/pallas_call | solution.py:316
  (6 shorter events, 0.0 us)
Async XLA Ops:
  0.6 32.9 %copy-start.1 = (bf16[768,1280]{1,0:T(8,128)(2,1)S(1)}, bf16[768,1280]{1,0:T(8,128)(2,1)}, u32[]{:S(2)}) copy-start(bf16[768,1280]{1,0:T(8,128)(2,1)} %w_ref.2) | copy-start | bytes 5898244
  3.4 42.1 %copy-start.4 = (bf16[160,768]{1,0:T(8,128)(2,1)S(1)}, bf16[160,768]{1,0:T(8,128)(2,1)}, u32[]{:S(2)}) copy-start(bf16[160,768]{1,0:T(8,128)(2,1)} %gate_ref.1) | copy-start | bytes 737284
  3.4 62.2 %all-to-all-start = ((bf16[128,8,640]{2,1,0:T(8,128)(2,1)}), bf16[128,8,640]{2,1,0:T(8,128)(2,1)S(1)}, u32[]{:S(2)}, u32[]{:S(2)}) async-start(bf16[128,8,640]{2,1,0:T(8,128)(2,1)} %bitcast.2), calls=%async_computation | async-start | bytes 2621440 | tf_op jit(solution)/shard_map/all_to_all | solution.py:246
  29.1 22.1 %collective-permute-start.1 = (bf16[1280,768]{1,0:T(8,128)(2,1)}, bf16[1280,768]{1,0:T(8,128)(2,1)}, u32[]{:S(2)}, u32[]{:S(2)}) collective-permute-start(bf16[1280,768]{1,0:T(8,128)(2,1)} %bitcast.14), channel_id=1, source_target_pairs={{0,1},{1,0},{2,3},{3,2},{4,5},{5,4},{6,7},{7,6},{8,9},{9,8},{10,11... | collective-permute-start | bytes 5898248 | tf_op jit(solution)/shard_map/ppermute | solution.py:267
  31.6 19.6 %collective-permute-start = (bf16[768,1280]{1,0:T(8,128)(2,1)}, bf16[768,1280]{1,0:T(8,128)(2,1)}, u32[]{:S(2)}, u32[]{:S(2)}) collective-permute-start(bf16[768,1280]{1,0:T(8,128)(2,1)} %bitcast.16), channel_id=1, source_target_pairs={{0,1},{1,0},{2,3},{3,2},{4,5},{5,4},{6,7},{7,6},{8,9},{9,8},{10,11... | collective-permute-start | bytes 5898248 | tf_op jit(solution)/shard_map/ppermute | solution.py:266
  33.6 1.0 copy-start.2
  34.6 14.2 %copy-start.3 = (bf16[1,1,512,768]{3,2,1,0:T(8,128)(2,1)S(1)}, bf16[1,1,512,768]{3,2,1,0:T(8,128)(2,1)}, u32[]{:S(2)}) copy-start(bf16[1,1,512,768]{3,2,1,0:T(8,128)(2,1)} %param.12) | copy-start | bytes 2359300
  35.4 14.3 %copy-start = (bf16[1280,768]{1,0:T(8,128)(2,1)S(1)}, bf16[1280,768]{1,0:T(8,128)(2,1)}, u32[]{:S(2)}) copy-start(bf16[1280,768]{1,0:T(8,128)(2,1)} %w_ref.3) | copy-start | bytes 5898244
  35.4 3.7 %collective-permute-start.2 = (f32[80,768]{1,0:T(8,128)S(1)}, f32[80,768]{1,0:T(8,128)S(1)}, u32[]{:S(2)}, u32[]{:S(2)}) collective-permute-start(f32[80,768]{1,0:T(8,128)S(1)} %get-tuple-element.15), channel_id=1, source_target_pairs={{0,1},{1,0},{2,3},{3,2},{4,5},{5,4},{6,7},{7,6},{8,9},{9,8},{10,11... | collective-permute-start | bytes 737288 | tf_op jit(solution)/shard_map/ppermute | solution.py:220
  39.1 6.4 %collective-permute-start.3 = (bf16[80,768]{1,0:T(8,128)(2,1)S(1)}, bf16[80,768]{1,0:T(8,128)(2,1)S(1)}, u32[]{:S(2)}, u32[]{:S(2)}) collective-permute-start(bf16[80,768]{1,0:T(8,128)(2,1)S(1)} %add_convert_fusion), channel_id=1, source_target_pairs={{0,2},{1,3},{2,0},{3,1},{4,6},{5,7},{6,4},{7,5},{8,10},{9,11},{10,... | collective-permute-start | bytes 368648 | tf_op jit(solution)/shard_map/ppermute | solution.py:221
  45.6 4.1 %collective-permute-start.4 = (bf16[80,768]{1,0:T(8,128)(2,1)S(1)}, bf16[80,768]{1,0:T(8,128)(2,1)S(1)}, u32[]{:S(2)}, u32[]{:S(2)}) collective-permute-start(bf16[80,768]{1,0:T(8,128)(2,1)S(1)} %shard_map.107.mine_ref), channel_id=1, source_target_pairs={{0,1},{1,0},{2,3},{3,2},{4,5},{5,4},{6,7},{7,6},{8,9},{9,8},{10,11... | collective-permute-start | bytes 368648 | tf_op jit(solution)/shard_map/ppermute | solution.py:229
  65.6 6.7 %copy-start.5 = (s32[160,6]{0,1:T(8,128)S(1)}, s32[160,6]{0,1:T(8,128)}, u32[]{:S(2)}) copy-start(s32[160,6]{0,1:T(8,128)} %param.10) | copy-start | bytes 11524
  69.1 11.5 %collective-permute-start.5 = (bf16[256,768]{1,0:T(8,128)(2,1)S(1)}, bf16[256,768]{1,0:T(8,128)(2,1)S(1)}, u32[]{:S(2)}, u32[]{:S(2)}) collective-permute-start(bf16[256,768]{1,0:T(8,128)(2,1)S(1)} %get-tuple-element.22), channel_id=1, source_target_pairs={{0,2},{1,3},{2,0},{3,1},{4,6},{5,7},{6,4},{7,5},{8,10},{9,11},{10,... | collective-permute-start | bytes 1179656 | tf_op jit(solution)/shard_map/ppermute | solution.py:296
